TPU v7x, 256 devices: a whole 4x4x8 slice. The times are simulated.
256 devices in a mesh: sec: 4 (over y), gx: 64 (over x, z, core).
Axes of the slice: x: 4, y: 4, z: 8, core: 2. Of those that a mesh axis runs over, the one named last changes fastest.
Arguments:
- pressure_start: float32 [16, 1024, 1024], P('sec', 'gx'), may hold values from -8 to 8
- soil_type: int32 [16, 1024, 1024], P('sec', 'gx'), may hold values from 0 to 11
- saturated_conductivity: float32 [12], replicated, may hold values from 0.2 to 5
- storage_coefficient: float32 [12], replicated, may hold values from 0.1 to 1
- rainfall: float32 [3, 1024, 1024], P(None, 'gx'), may hold values from 0 to 2
Outputs:
- pressure: float32 [16, 1024, 1024], P('sec', 'gx')
- inflow: float32 [4, 3, 1024, 1024], P('sec', None, 'gx')
All inputs are finite; a program needn't handle non-finite values.
Results may differ from a plain program's by a relative error of at most 0.0001.
Values sent between devices are 32-bit elements; how exact they have to be, the bound alone decides.
No kernel may reach another device: no remote copies, remote signals or barrier semaphores. Data moves between devices by JAX's collectives and lax.ppermute only.
A program may use at most 64 MiB of HBM per device.

v0:
```python
import jax
import jax.numpy as jnp
from jax import lax
from jax.sharding import PartitionSpec as P

ITERS = 4


def prefix(shard, axis, combine, identity, reverse):
    count, here = (lax.axis_size(axis), lax.axis_index(axis))
    everything = jax.tree.map(lambda part: lax.all_gather(part, axis), shard)
    start = jax.tree.map(
        lambda part, zero: jnp.broadcast_to(jnp.asarray(zero, part.dtype), part.shape),
        shard,
        identity,
    )

    def lap(k, before):
        at = count - 1 - k if reverse else k
        reached = at > here if reverse else at < here
        new = combine(before, jax.tree.map(lambda part: part[at], everything))
        return jax.tree.map(lambda a, b: jnp.where(reached, a, b), new, before)

    return lax.fori_loop(0, count, lap, start)


def padded_2(block, sides, width):
    for axis, dim in sides:
        count = lax.axis_size(axis)
        forward = [(i, i + 1) for i in range(count - 1)]
        backward = [(target, source) for source, target in forward]
        low = lax.ppermute(
            lax.slice_in_dim(block, block.shape[dim] - width, None, axis=dim), axis, forward
        )
        high = lax.ppermute(lax.slice_in_dim(block, 0, width, axis=dim), axis, backward)
        block = jnp.concatenate([low, block, high], axis=dim)
    return block


def lookup(kinds, table):
    total = jnp.zeros(kinds.shape, jnp.float32)
    for kind in range(table.shape[0]):
        total = jnp.where(kinds == kind, table[kind], total)
    return total


def harmonic(cond, other):
    return 2.0 * cond * other / (cond + other)


def neighbours(padded):
    return [
        padded[:-2, 1:-1, 1:-1],
        padded[2:, 1:-1, 1:-1],
        padded[1:-1, :-2, 1:-1],
        padded[1:-1, 2:, 1:-1],
        padded[1:-1, 1:-1, :-2],
        padded[1:-1, 1:-1, 2:],
    ]


def pad_side(rimmed):
    return jnp.pad(rimmed, ((0, 0), (0, 0), (1, 1)))


def face_terms(conductivity, padded):
    return [harmonic(conductivity, other) for other in neighbours(padded)]


def stencil(field, padded, faces, capacity):
    result = capacity * field
    for face, other in zip(faces, neighbours(padded)):
        result = result + face * (field - other)
    return result


def affine(earlier, later):
    return (earlier[0] * later[0], later[0] * earlier[1] + later[1])


def adding(earlier, later):
    return earlier + later


def body(pressure_start, soil_type, saturated_conductivity, storage_coefficient, rainfall):
    cond_table = lookup(soil_type, saturated_conductivity)
    store_table = lookup(soil_type, storage_coefficient)
    head = pressure_start
    layers = head.shape[0]
    depth = jnp.float32(layers)
    flows = []
    for step in range(rainfall.shape[0]):
        saturation = jax.nn.sigmoid(head)
        conductivity = cond_table * (0.05 + saturation * saturation)
        capacity = store_table * (0.1 + saturation * (1.0 - saturation))
        water = jnp.sum(saturation, axis=0)
        bottom = conductivity[layers - 1]
        ones_field = jnp.ones_like(water)
        zero_field = jnp.zeros_like(water)
        below = prefix(water, "sec", adding, zero_field, True)
        slope = water / depth * (0.5 + 0.5 * below / (below + depth))
        offset = 0.5 * bottom
        prefix_a, prefix_b = prefix((slope, offset), "sec", affine, (ones_field, zero_field), False)
        entering = prefix_a * rainfall[step] + prefix_b
        leaving = slope * entering + offset
        flows.append(entering)
        source = jnp.zeros(head.shape, jnp.float32).at[0].add(entering).at[layers - 1].add(-leaving)

        def apply(field):
            paired = jnp.stack([field, conductivity])
            rimmed = padded_2(paired, (("sec", 1), ("gx", 2)), 1)
            faces_now = face_terms(conductivity, pad_side(rimmed[1]))
            return (stencil(field, pad_side(rimmed[0]), faces_now, capacity), faces_now)

        start_image, faces = apply(head)
        gravity = faces[0] - faces[1]
        rhs = capacity * head + gravity + source
        diagonal = capacity
        for face in faces:
            diagonal = diagonal + face
        iterate = head
        residual = rhs - start_image
        precond = residual / diagonal
        direction = precond
        product = lax.psum(jnp.sum(residual * precond), ("sec", "gx"))
        for turn in range(ITERS):
            image, unused = apply(direction)
            alpha = product / lax.psum(jnp.sum(direction * image), ("sec", "gx"))
            iterate = iterate + alpha * direction
            residual = residual - alpha * image
            if turn + 1 < ITERS:
                precond = residual / diagonal
                renewed = lax.psum(jnp.sum(residual * precond), ("sec", "gx"))
                direction = precond + renewed / product * direction
                product = renewed
        head = iterate
    return (head, jnp.stack(flows)[None])


def solution(mesh):
    placed = (P("sec", "gx", None), P("sec", "gx", None), P(), P(), P(None, "gx", None))
    return jax.shard_map(
        body,
        mesh=mesh,
        in_specs=placed,
        out_specs=(P("sec", "gx", None), P("sec", None, "gx", None)),
        check_vma=False,
    )
```

profile of v0, /device:TPU:1, one launch (start us, length us, event | category | flops | bytes accessed | tf_op | source)
XLA Modules:
  0.0 2007.3 jit_solution(6144754909317096840)
XLA Ops:
  48.4 12.7 collective-permute-start.3
  92.4 80.7 %all-reduce.35 = (f32[]{:T(128)}, f32[]{:T(128)}) all-reduce(f32[]{:T(128)} %get-tuple-element.856, f32[]{:T(128)} %get-tuple-element.855), channel_id=1, replica_groups=mesh['sec'=4,'gx'=64] {'sec','gx'}, use_global_device_ids=true, to_apply=%region_6.7 | all-reduce | flops 2 | bytes 16 | tf_op jit(solution)/shard_map/psum | solution.py:125
  175.1 73.8 %psum.170 = f32[]{:T(128)} all-reduce(f32[]{:T(128)} %get-tuple-element.968), channel_id=1, replica_groups=mesh['sec'=4,'gx'=64] {'sec','gx'}, use_global_device_ids=true, to_apply=%region_10.11 | all-reduce | flops 1 | bytes 8 | tf_op jit(solution)/shard_map/psum | solution.py:133
  266.9 76.2 %psum.171 = f32[]{:T(128)} all-reduce(f32[]{:T(128)} %get-tuple-element.966), channel_id=1, replica_groups=mesh['sec'=4,'gx'=64] {'sec','gx'}, use_global_device_ids=true, to_apply=%region_12.13 | all-reduce | flops 1 | bytes 8 | tf_op jit(solution)/shard_map/psum | solution.py:128
  345.2 74.2 %psum.172 = f32[]{:T(128)} all-reduce(f32[]{:T(128)} %get-tuple-element.963), channel_id=1, replica_groups=mesh['sec'=4,'gx'=64] {'sec','gx'}, use_global_device_ids=true, to_apply=%region_14.15 | all-reduce | flops 1 | bytes 8 | tf_op jit(solution)/shard_map/psum | solution.py:133
  437.5 76.4 %psum.173 = f32[]{:T(128)} all-reduce(f32[]{:T(128)} %get-tuple-element.961), channel_id=1, replica_groups=mesh['sec'=4,'gx'=64] {'sec','gx'}, use_global_device_ids=true, to_apply=%region_16.17 | all-reduce | flops 1 | bytes 8 | tf_op jit(solution)/shard_map/psum | solution.py:128
  515.9 74.2 %psum.174 = f32[]{:T(128)} all-reduce(f32[]{:T(128)} %multiply_reduce_fusion.14), channel_id=1, replica_groups=mesh['sec'=4,'gx'=64] {'sec','gx'}, use_global_device_ids=true, to_apply=%region_18.19 | all-reduce | flops 1 | bytes 8 | tf_op jit(solution)/shard_map/psum | solution.py:133
  608.3 76.0 %psum.175 = f32[]{:T(128)} all-reduce(f32[]{:T(128)} %fusion.365), channel_id=1, replica_groups=mesh['sec'=4,'gx'=64] {'sec','gx'}, use_global_device_ids=true, to_apply=%region_20.21 | all-reduce | flops 1 | bytes 8 | tf_op jit(solution)/shard_map/psum | solution.py:128
  720.7 11.8 collective-permute-start.23
  756.0 76.8 %all-reduce.34 = (f32[]{:T(128)}, f32[]{:T(128)}) all-reduce(f32[]{:T(128)} %get-tuple-element.854, f32[]{:T(128)} %get-tuple-element.853), channel_id=1, replica_groups=mesh['sec'=4,'gx'=64] {'sec','gx'}, use_global_device_ids=true, to_apply=%region_27.28 | all-reduce | flops 2 | bytes 16 | tf_op jit(solution)/shard_map/psum | solution.py:125
  834.8 74.2 %psum.178 = f32[]{:T(128)} all-reduce(f32[]{:T(128)} %get-tuple-element.949), channel_id=1, replica_groups=mesh['sec'=4,'gx'=64] {'sec','gx'}, use_global_device_ids=true, to_apply=%region_31.32 | all-reduce | flops 1 | bytes 8 | tf_op jit(solution)/shard_map/psum | solution.py:133
  927.0 76.6 %psum.179 = f32[]{:T(128)} all-reduce(f32[]{:T(128)} %get-tuple-element.947), channel_id=1, replica_groups=mesh['sec'=4,'gx'=64] {'sec','gx'}, use_global_device_ids=true, to_apply=%region_33.34 | all-reduce | flops 1 | bytes 8 | tf_op jit(solution)/shard_map/psum | solution.py:128
  1005.6 74.2 %psum.180 = f32[]{:T(128)} all-reduce(f32[]{:T(128)} %get-tuple-element.944), channel_id=1, replica_groups=mesh['sec'=4,'gx'=64] {'sec','gx'}, use_global_device_ids=true, to_apply=%region_35.36 | all-reduce | flops 1 | bytes 8 | tf_op jit(solution)/shard_map/psum | solution.py:133
  1097.9 76.0 %psum.181 = f32[]{:T(128)} all-reduce(f32[]{:T(128)} %get-tuple-element.942), channel_id=1, replica_groups=mesh['sec'=4,'gx'=64] {'sec','gx'}, use_global_device_ids=true, to_apply=%region_37.38 | all-reduce | flops 1 | bytes 8 | tf_op jit(solution)/shard_map/psum | solution.py:128
  1175.9 74.2 %psum.182 = f32[]{:T(128)} all-reduce(f32[]{:T(128)} %multiply_reduce_fusion.7), channel_id=1, replica_groups=mesh['sec'=4,'gx'=64] {'sec','gx'}, use_global_device_ids=true, to_apply=%region_39.40 | all-reduce | flops 1 | bytes 8 | tf_op jit(solution)/shard_map/psum | solution.py:133
  1268.3 76.0 %psum.183 = f32[]{:T(128)} all-reduce(f32[]{:T(128)} %fusion.364), channel_id=1, replica_groups=mesh['sec'=4,'gx'=64] {'sec','gx'}, use_global_device_ids=true, to_apply=%region_41.42 | all-reduce | flops 1 | bytes 8 | tf_op jit(solution)/shard_map/psum | solution.py:128
  1380.7 11.8 collective-permute-start.43
  1416.0 77.0 %all-reduce.33 = (f32[]{:T(128)}, f32[]{:T(128)}) all-reduce(f32[]{:T(128)} %get-tuple-element.852, f32[]{:T(128)} %get-tuple-element.851), channel_id=1, replica_groups=mesh['sec'=4,'gx'=64] {'sec','gx'}, use_global_device_ids=true, to_apply=%region_48.49 | all-reduce | flops 2 | bytes 16 | tf_op jit(solution)/shard_map/psum | solution.py:125
  1495.0 74.2 %psum.186 = f32[]{:T(128)} all-reduce(f32[]{:T(128)} %get-tuple-element.930), channel_id=1, replica_groups=mesh['sec'=4,'gx'=64] {'sec','gx'}, use_global_device_ids=true, to_apply=%region_52.53 | all-reduce | flops 1 | bytes 8 | tf_op jit(solution)/shard_map/psum | solution.py:133
  1587.3 76.4 %psum.187 = f32[]{:T(128)} all-reduce(f32[]{:T(128)} %get-tuple-element.928), channel_id=1, replica_groups=mesh['sec'=4,'gx'=64] {'sec','gx'}, use_global_device_ids=true, to_apply=%region_54.55 | all-reduce | flops 1 | bytes 8 | tf_op jit(solution)/shard_map/psum | solution.py:128
  1665.7 74.2 %psum.188 = f32[]{:T(128)} all-reduce(f32[]{:T(128)} %get-tuple-element.925), channel_id=1, replica_groups=mesh['sec'=4,'gx'=64] {'sec','gx'}, use_global_device_ids=true, to_apply=%region_56.57 | all-reduce | flops 1 | bytes 8 | tf_op jit(solution)/shard_map/psum | solution.py:133
  1758.0 76.0 %psum.189 = f32[]{:T(128)} all-reduce(f32[]{:T(128)} %get-tuple-element.923), channel_id=1, replica_groups=mesh['sec'=4,'gx'=64] {'sec','gx'}, use_global_device_ids=true, to_apply=%region_58.59 | all-reduce | flops 1 | bytes 8 | tf_op jit(solution)/shard_map/psum | solution.py:128
  1836.0 74.2 %psum.190 = f32[]{:T(128)} all-reduce(f32[]{:T(128)} %multiply_reduce_fusion), channel_id=1, replica_groups=mesh['sec'=4,'gx'=64] {'sec','gx'}, use_global_device_ids=true, to_apply=%region_60.61 | all-reduce | flops 1 | bytes 8 | tf_op jit(solution)/shard_map/psum | solution.py:133
  1929.0 75.9 %psum.191 = f32[]{:T(128)} all-reduce(f32[]{:T(128)} %fusion.363), channel_id=1, replica_groups=mesh['sec'=4,'gx'=64] {'sec','gx'}, use_global_device_ids=true, to_apply=%region_62.63 | all-reduce | flops 1 | bytes 8 | tf_op jit(solution)/shard_map/psum | solution.py:128
  (333 shorter events, 354.0 us)
Async XLA Ops:
  12.3 35.9 %collective-permute-start.1 = (f32[2,1,16,1024]{3,2,1,0:T(8,128)S(1)}, f32[2,1,16,1024]{3,2,1,0:T(8,128)S(1)}, u32[]{:S(2)}, u32[]{:S(2)}) collective-permute-start(f32[2,1,16,1024]{3,2,1,0:T(8,128)S(1)} %get-tuple-element.977), channel_id=1, source_target_pairs={{64,0},{128,64},{192,128},{65,1},{129,65},{193,129},{66,2},{130,66... | collective-permute-start | bytes 393224 | tf_op jit(solution)/shard_map/ppermute | solution.py:35
  13.6 34.6 %collective-permute-start = (f32[2,1,16,1024]{3,2,1,0:T(8,128)S(1)}, f32[2,1,16,1024]{3,2,1,0:T(8,128)S(1)}, u32[]{:S(2)}, u32[]{:S(2)}) collective-permute-start(f32[2,1,16,1024]{3,2,1,0:T(8,128)S(1)} %get-tuple-element.1086), channel_id=1, source_target_pairs={{0,64},{64,128},{128,192},{1,65},{65,129},{129,193},{2,66},{66,130... | collective-permute-start | bytes 393224 | tf_op jit(solution)/shard_map/ppermute | solution.py:32
  48.4 16.0 collective-permute-start.3
  74.9 7.4 collective-permute-start.5
  76.2 7.0 collective-permute-start.4
  257.6 6.5 collective-permute-start.11
  428.1 6.6 collective-permute-start.15
  598.9 6.6 collective-permute-start.19
  685.9 34.6 %collective-permute-start.21 = (f32[2,1,16,1024]{3,2,1,0:T(8,128)S(1)}, f32[2,1,16,1024]{3,2,1,0:T(8,128)S(1)}, u32[]{:S(2)}, u32[]{:S(2)}) collective-permute-start(f32[2,1,16,1024]{3,2,1,0:T(8,128)S(1)} %get-tuple-element.959), channel_id=1, source_target_pairs={{64,0},{128,64},{192,128},{65,1},{129,65},{193,129},{66,2},{130,66... | collective-permute-start | bytes 393224 | tf_op jit(solution)/shard_map/ppermute | solution.py:35
  687.2 33.4 %collective-permute-start.20 = (f32[2,1,16,1024]{3,2,1,0:T(8,128)S(1)}, f32[2,1,16,1024]{3,2,1,0:T(8,128)S(1)}, u32[]{:S(2)}, u32[]{:S(2)}) collective-permute-start(f32[2,1,16,1024]{3,2,1,0:T(8,128)S(1)} %get-tuple-element.1076), channel_id=1, source_target_pairs={{0,64},{64,128},{128,192},{1,65},{65,129},{129,193},{2,66},{66,130... | collective-permute-start | bytes 393224 | tf_op jit(solution)/shard_map/ppermute | solution.py:32
  720.7 15.4 collective-permute-start.23
  739.8 6.6 collective-permute-start.24
  746.5 6.7 collective-permute-start.27
  917.8 6.4 collective-permute-start.31
  1088.6 6.6 collective-permute-start.35
  1258.9 6.6 collective-permute-start.39
  1345.9 34.7 %collective-permute-start.41 = (f32[2,1,16,1024]{3,2,1,0:T(8,128)S(1)}, f32[2,1,16,1024]{3,2,1,0:T(8,128)S(1)}, u32[]{:S(2)}, u32[]{:S(2)}) collective-permute-start(f32[2,1,16,1024]{3,2,1,0:T(8,128)S(1)} %get-tuple-element.940), channel_id=1, source_target_pairs={{64,0},{128,64},{192,128},{65,1},{129,65},{193,129},{66,2},{130,66... | collective-permute-start | bytes 393224 | tf_op jit(solution)/shard_map/ppermute | solution.py:35
  1347.2 33.4 %collective-permute-start.40 = (f32[2,1,16,1024]{3,2,1,0:T(8,128)S(1)}, f32[2,1,16,1024]{3,2,1,0:T(8,128)S(1)}, u32[]{:S(2)}, u32[]{:S(2)}) collective-permute-start(f32[2,1,16,1024]{3,2,1,0:T(8,128)S(1)} %get-tuple-element.1067), channel_id=1, source_target_pairs={{0,64},{64,128},{128,192},{1,65},{65,129},{129,193},{2,66},{66,130... | collective-permute-start | bytes 393224 | tf_op jit(solution)/shard_map/ppermute | solution.py:32
  1380.7 15.4 collective-permute-start.43
  1399.8 6.6 collective-permute-start.44
  1406.5 6.7 collective-permute-start.47
  1578.0 6.4 collective-permute-start.51
  1748.6 6.6 collective-permute-start.55
  1918.9 6.6 collective-permute-start.59
  (54 other events, 277.8 us)
where the time goes:
time: 2020 us; the launch traced here: 2010 us
  blocking collectives  1670 us (83%)
  starting transfers between devices  204 us (10%)
  other arithmetic  50.2 us (2%)
  waiting for transfers between devices  41.8 us (2%)
  between operations  30.5 us (2%)
    psum x9, blocking collectives, body(): alpha = product / lax.psum(jnp.sum(direction * image), ('sec', 'gx'))  685 us
    psum x9, blocking collectives, body(): renewed = lax.psum(jnp.sum(residual * precond), ('sec', 'gx'))  667 us
    psum x3, blocking collectives, body(): product = lax.psum(jnp.sum(residual * precond), ('sec', 'gx'))  235 us
    ppermute x30, starting transfers between devices, padded_2(): lax.ppermute(lax.slice_in_dim(block, block.shape[dim] - width, None, axis...  109 us
    ppermute x30, starting transfers between devices, padded_2(): lax.ppermute(lax.slice_in_dim(block, 0, width, axis=dim), axis, backward)  95.3 us
    all_gather x9, blocking collectives, prefix(): everything = jax.tree.map(lambda part: lax.all_gather(part, axis), shard)  86.9 us
  transfers between devices with their start and end apart: 60, of which 39 were waited for; matrix products, arithmetic and copies ran while one was open for 0% of the time, Pallas kernels for 0%

commit v1 on v0

v1 whole, which is shorter than its diff:
```python
import functools

import jax
import jax.numpy as jnp
from jax import lax
from jax.experimental import pallas as pl
from jax.experimental.pallas import tpu as pltpu
from jax.sharding import PartitionSpec as P

ITERS = 4
SECTIONS = 4
LZ = 4
NZ = SECTIONS * LZ
OWN_ROWS = 16
OWN_COLS = 256
WIDE = 384
HALF = 64
FRAME = 48
SPANS = ((0, 48), (0, 40), (8, 40))
F32 = jnp.float32
VMEM = pl.BlockSpec(memory_space=pltpu.VMEM)


def params():
    return pltpu.CompilerParams(vmem_limit_bytes=56 * 1024 * 1024)


def pack_kernel(head_ref, soil_ref, rain_ref, out_ref):
    section = lax.axis_index("sec")
    low_half = lax.broadcasted_iota(jnp.int32, (OWN_ROWS, 128), 1) < HALF
    rain_step = jnp.minimum(section, 2)
    for target in range(SECTIONS):
        start = target * OWN_COLS
        after = (start + OWN_COLS) % (SECTIONS * OWN_COLS)
        before = (start - 128) % (SECTIONS * OWN_COLS)

        def put(slot, read):
            out_ref[target, slot, :, 0:OWN_COLS] = read(start, OWN_COLS)
            out_ref[target, slot, :, OWN_COLS:WIDE] = jnp.where(low_half, read(after, 128), read(before, 128))

        for q in range(LZ):
            put(q, lambda at, n: head_ref[q, :, at : at + n])
            put(LZ + q, lambda at, n: soil_ref[q, :, at : at + n].astype(F32))
        put(2 * LZ, lambda at, n: rain_ref[rain_step, :, at : at + n])


def weights(sums_ref):
    total = jnp.sum(sums_ref[...], axis=0, keepdims=True)
    lane = lax.broadcasted_iota(jnp.int32, total.shape, 1)
    m = [jnp.sum(jnp.where(lane == k, total, 0.0), axis=1, keepdims=True) for k in range(8)]
    step_m = [m[k] - m[k + 1] for k in range(7)]
    zero = jnp.zeros_like(m[0])

    def form(poly, other, table):
        result = zero
        for i, a in enumerate(poly):
            for j, b in enumerate(other):
                result = result + a * b * table[i + j]
        return result

    z = [jnp.ones_like(zero)]
    direction = z
    rz = m[0]
    change = [zero] * ITERS
    for turn in range(ITERS):
        below = form(direction, direction, step_m)
        alpha = jnp.where(below > 0.0, rz / jnp.where(below > 0.0, below, 1.0), 0.0)
        for i, a in enumerate(direction):
            change[i] = change[i] + alpha * a
        if turn + 1 < ITERS:
            long = direction + [zero]
            image = [long[i] - (long[i - 1] if i else zero) for i in range(len(long))]
            z = [a - alpha * b for a, b in zip(z + [zero], image)]
            renewed = form(z, z, m)
            beta = jnp.where(rz > 0.0, renewed / jnp.where(rz > 0.0, rz, 1.0), 0.0)
            direction = [a + beta * b for a, b in zip(z, long)]
            rz = renewed
    return change


def recip(x):
    return pl.reciprocal(x, approx=False)


def setup_terms(h, cond_table, store_table):
    saturation = recip(1.0 + jnp.exp(-h))
    cond = cond_table * (0.05 + saturation * saturation)
    capacity = store_table * (0.1 + saturation * (1.0 - saturation))
    return saturation, cond, capacity


def gather(table, kinds):
    rows, cols = kinds.shape
    parts = []
    for j in range(cols // 128):
        parts.append(
            jnp.concatenate(
                [
                    jnp.take_along_axis(table, kinds[8 * i : 8 * i + 8, 128 * j : 128 * j + 128], axis=1, mode="promise_in_bounds")
                    for i in range(rows // 8)
                ],
                axis=0,
            )
        )
    return jnp.concatenate(parts, axis=1)


def step_kernel(step, n_rows_all, *refs):
    first = step == 0
    r0, r1 = SPANS[step]
    rows = r1 - r0
    own = OWN_ROWS - r0
    if first:
        (low_ref, mid_ref, high_ref, tables_ref, head_ref, cond_ref, store_ref, rain_ref) = refs[:8]
        refs = refs[8:]
    else:
        p0 = SPANS[step - 1][0]
        old = slice(r0 - p0, r1 - p0)
        (sums_ref, old_head_ref, o0, o1, o2, o3, cond_ref, store_ref, rain_ref, head_ref) = refs[:10]
        old_basis = (o0, o1, o2, o3)
        refs = refs[10:]
    (v0, v1, v2, v3, inflow_ref, moments_ref) = refs[:6]
    (res_ref, cap_ref, diag_ref, face_ref, up_ref, dn_ref, ru_ref, rd_ref, xl_ref, xr_ref, water_ref, low_cond_ref, flux_ref) = refs[6:]
    basis = (v0, v1, v2, v3)
    here = slice(r0, r1)
    section, band = lax.axis_index("sec"), lax.axis_index("gx")

    if first:
        for s in range(3):
            rain_ref[s, 0:16, :] = low_ref[s, 8]
            rain_ref[s, 16:32, :] = mid_ref[s, 8]
            rain_ref[s, 32:48, :] = high_ref[s, 8]
    else:
        change = weights(sums_ref)

    def soil(s, carry):
        total = jnp.zeros((rows, WIDE), F32)
        for q in range(LZ):
            l = s * LZ + q
            if first:
                for part, ref in enumerate((low_ref, mid_ref, high_ref)):
                    at = slice(16 * part, 16 * part + 16)
                    kinds = ref[s, LZ + q].astype(jnp.int32)
                    head_ref[l, at, :] = ref[s, q]
                    cond_ref[l, at, :] = gather(tables_ref[0], kinds)
                    store_ref[l, at, :] = gather(tables_ref[1], kinds)
                h = head_ref[l]
            else:
                h = old_head_ref[l, old, :]
                for c, o in zip(change, old_basis):
                    h = h + c * o[l, old, :]
                head_ref[l] = h
            saturation, cond, capacity = setup_terms(h, cond_ref[l, here, :], store_ref[l, here, :])
            res_ref[l] = recip(cond)
            cap_ref[l] = capacity
            total = total + saturation
            if q == LZ - 1:
                low_cond_ref[s] = 0.5 * cond
        water_ref[s] = total
        return carry

    lax.fori_loop(0, SECTIONS, soil, 0)

    flux_ref[0] = rain_ref[step, here, :]
    belows = [None] * SECTIONS
    below = None
    for s in reversed(range(SECTIONS)):
        belows[s] = below
        below = water_ref[s] if below is None else below + water_ref[s]
    for s in range(SECTIONS):
        scale = 0.5 if belows[s] is None else 0.5 + 0.5 * belows[s] / (belows[s] + 4.0)
        flux_ref[s + 1] = water_ref[s] * 0.25 * scale * flux_ref[s] + low_cond_ref[s]
        inflow_ref[s] = flux_ref[s, own : own + OWN_ROWS, 0:OWN_COLS]

    lane = lax.broadcasted_iota(jnp.int32, (rows, WIDE), 1)
    col = section * OWN_COLS + lane - jnp.where(lane >= OWN_COLS + HALF, WIDE, 0)
    row = band * OWN_ROWS + (r0 - OWN_ROWS) + lax.broadcasted_iota(jnp.int32, (rows, WIDE), 0)
    col_gate = jnp.where((col >= 1) & (col < SECTIONS * OWN_COLS), 2.0, 0.0).astype(F32)
    row_gate = jnp.where((row >= 1) & (row < n_rows_all), 2.0, 0.0).astype(F32)
    kept = slice(own, own + OWN_ROWS)
    none = jnp.zeros((OWN_ROWS, OWN_COLS), F32)

    face_ref[0] = jnp.zeros((rows, WIDE), F32)

    def faces(s, acc):
        for q in range(LZ):
            l = s * LZ + q
            res = res_ref[l]
            up = face_ref[l]
            after = jnp.minimum(l + 1, NZ - 1)
            dn = jnp.where(l < NZ - 1, 2.0, 0.0).astype(F32) * recip(res + res_ref[after])
            face_ref[l + 1] = dn
            ru = row_gate * recip(res + pltpu.roll(res, 1, 0))
            rd = pltpu.roll(ru, rows - 1, 0)
            xl = col_gate * recip(res + pltpu.roll(res, 1, 1))
            xr = pltpu.roll(xl, WIDE - 1, 1)
            diag = cap_ref[l] + up + dn + ru + rd + xl + xr
            inv = recip(diag)
            h = head_ref[l]
            r = up - dn
            if q == 0:
                r = r + flux_ref[s]
            if q == LZ - 1:
                r = r - flux_ref[s + 1]
            r = r + up * (head_ref[jnp.maximum(l - 1, 0)] - h) + dn * (head_ref[after] - h)
            r = r + ru * (pltpu.roll(h, 1, 0) - h) + rd * (pltpu.roll(h, rows - 1, 0) - h)
            r = r + xl * (pltpu.roll(h, 1, 1) - h) + xr * (pltpu.roll(h, WIDE - 1, 1) - h)
            z = r * inv
            v0[l] = z
            diag_ref[l] = diag
            up_ref[l] = up * inv
            dn_ref[l] = dn * inv
            ru_ref[l] = ru * inv
            rd_ref[l] = rd * inv
            xl_ref[l] = xl * inv
            xr_ref[l] = xr * inv
            acc = acc + (r * z)[kept, 0:OWN_COLS]
        return acc

    moments = [lax.fori_loop(0, SECTIONS, faces, none)]

    for k in range(1, ITERS):
        src, dst = basis[k - 1], basis[k]

        def smooth(l, accs, src=src, dst=dst):
            v = src[l]
            new = up_ref[l] * src[jnp.maximum(l - 1, 0)] + dn_ref[l] * src[jnp.minimum(l + 1, NZ - 1)]
            new = new + ru_ref[l] * pltpu.roll(v, 1, 0) + rd_ref[l] * pltpu.roll(v, rows - 1, 0)
            new = new + xl_ref[l] * pltpu.roll(v, 1, 1) + xr_ref[l] * pltpu.roll(v, WIDE - 1, 1)
            dst[l] = new
            mine = new[kept, 0:OWN_COLS]
            scaled = mine * diag_ref[l, kept, 0:OWN_COLS]
            return accs[0] + v[kept, 0:OWN_COLS] * scaled, accs[1] + mine * scaled

        moments.extend(lax.fori_loop(0, NZ, smooth, (none, none)))

    def last(l, acc):
        block = slice(own - 8, own + OWN_ROWS)
        v = v3[l, block, :]
        mine = v[8:, 0:OWN_COLS]
        pairs = up_ref[l, kept, 0:OWN_COLS] * v3[jnp.maximum(l - 1, 0), kept, 0:OWN_COLS]
        pairs = pairs + ru_ref[l, kept, 0:OWN_COLS] * pltpu.roll(v, 1, 0)[8:, 0:OWN_COLS]
        pairs = pairs + xl_ref[l, kept, 0:OWN_COLS] * pltpu.roll(v, 1, 1)[8:, 0:OWN_COLS]
        return acc + 2.0 * mine * diag_ref[l, kept, 0:OWN_COLS] * pairs

    moments.append(lax.fori_loop(0, NZ, last, none))

    spot = lax.broadcasted_iota(jnp.int32, (8, 128), 1)
    line = jnp.zeros((8, 128), F32)
    for k, acc in enumerate(moments):
        value = jnp.sum(jnp.sum(acc, axis=0, keepdims=True), axis=1, keepdims=True)
        line = jnp.where(spot == k, value, line)
    for i in range(moments_ref.shape[0] // 8):
        moments_ref[8 * i : 8 * i + 8, :] = line


def last_kernel(sums_ref, head_ref, v0, v1, v2, v3, i0, i1, i2, out_ref):
    change = weights(sums_ref)
    own = OWN_ROWS - SPANS[2][0]
    kept = slice(own, own + OWN_ROWS)
    for l in range(NZ):
        h = head_ref[l, kept, 0:OWN_COLS]
        for c, o in zip(change, (v0, v1, v2, v3)):
            h = h + c * o[l, kept, 0:OWN_COLS]
        out_ref[l // LZ, l % LZ] = h
    for s in range(SECTIONS):
        for c, i in enumerate((i0, i1, i2)):
            out_ref[s, LZ + c] = i[s]


def shape(*dims):
    return jax.ShapeDtypeStruct(dims, F32)


def call(kernel, operands, outs, scratch=()):
    return pl.pallas_call(
        kernel,
        out_shape=outs,
        in_specs=[VMEM] * len(operands),
        out_specs=jax.tree.map(lambda _: VMEM, outs),
        scratch_shapes=[pltpu.VMEM(dims, F32) for dims in scratch],
        compiler_params=params(),
    )(*operands)


def add_up(moments):
    return lax.all_to_all(moments, ("sec", "gx"), 0, 0, tiled=True)


def body(pressure_start, soil_type, saturated_conductivity, storage_coefficient, rainfall):
    bands = lax.axis_size("gx")
    devices = SECTIONS * bands
    packed = call(pack_kernel, (pressure_start, soil_type, rainfall), shape(SECTIONS, 9, OWN_ROWS, WIDE))
    mid = lax.all_to_all(packed, "sec", 0, 0, tiled=True)
    low = lax.ppermute(mid, "gx", [(i, i + 1) for i in range(bands - 1)])
    high = lax.ppermute(mid, "gx", [(i + 1, i) for i in range(bands - 1)])
    tables = jnp.stack([saturated_conductivity, storage_coefficient])
    tables = jnp.broadcast_to(jnp.pad(tables, ((0, 0), (0, 128 - tables.shape[1])))[:, None, :], (2, 8, 128))
    inflows = []
    state = None
    for step, (r0, r1) in enumerate(SPANS):
        rows = r1 - r0
        field = (NZ, rows, WIDE)
        wide = (NZ, FRAME, WIDE)
        outs = [shape(*field)] * 5
        kernel = functools.partial(step_kernel, step, bands * OWN_ROWS)
        tail = [shape(SECTIONS, OWN_ROWS, OWN_COLS), shape(devices, 128)]
        scratch = [field, field, field, (NZ + 1, rows, WIDE)] + [field] * 6 + [(SECTIONS, rows, WIDE)] * 2 + [(SECTIONS + 1, rows, WIDE)]
        if step == 0:
            outs = [shape(*field), shape(*wide), shape(*wide), shape(3, FRAME, WIDE)] + [shape(*field)] * 4
            got = call(kernel, (low, mid, high, tables), outs + tail, scratch)
            head, cond, store, rain = got[:4]
            v = got[4:8]
        else:
            got = call(kernel, (sums, head, *v, cond, store, rain), outs + tail, scratch)
            head, v = got[0], got[1:5]
        inflows.append(got[-2])
        sums = add_up(got[-1])
    out = call(last_kernel, (sums, head, *v, *inflows), shape(SECTIONS, 7, OWN_ROWS, OWN_COLS))
    out = lax.all_to_all(out, "sec", 0, 0, tiled=True)
    out = jnp.transpose(out, (1, 2, 0, 3)).reshape(7, OWN_ROWS, SECTIONS * OWN_COLS)
    return out[:LZ], out[LZ:][None]


def solution(mesh):
    placed = (P("sec", "gx", None), P("sec", "gx", None), P(), P(), P(None, "gx", None))
    return jax.shard_map(
        body,
        mesh=mesh,
        in_specs=placed,
        out_specs=(P("sec", "gx", None), P("sec", None, "gx", None)),
        check_vma=False,
    )
```

time: 2020 us -> 171 us (0.08)
  blocking collectives: 1670 us -> 97 us
  starting transfers between devices: 204 us -> 7.96 us
  Pallas kernels: 0 us -> 51.9 us
  other arithmetic: 50.2 us -> 0.01 us
  waiting for transfers between devices: 41.8 us -> 9.93 us
  between operations: 30.5 us -> 0.69 us
    psum x21 -> x0, blocking collectives: 1590 us -> none  [the longest x9 685 us: body(): alpha = product / lax.psum(jnp.sum(direction * image), ('sec', 'gx'))]
    ppermute x60 -> x2, starting transfers between devices: 204 us -> 7.96 us  [the longest x1 4.52 us: body(): high = lax.ppermute(mid, 'gx', [(i + 1, i) for i in range(bands - 1)])]
    all_to_all x0 -> x5, blocking collectives: none -> 97 us  [the longest x3 68.5 us: add_up(): return lax.all_to_all(moments, ('sec', 'gx'), 0, 0, tiled=True)]
    all_gather x9 -> x0, blocking collectives: 86.9 us -> none  [prefix(): everything = jax.tree.map(lambda part: lax.all_gather(part, axis), shard)]
    pallas_call x0 -> x5, Pallas kernels: none -> 51.9 us  [call(): pl.pallas_call(kernel, out_shape=outs, in_specs=[VMEM] * len(operands), o...]
    ppermute x60 -> x2, waiting for transfers between devices: 41.8 us -> 9.93 us  [the longest x1 8.75 us: body(): high = lax.ppermute(mid, 'gx', [(i + 1, i) for i in range(bands - 1)])]
    reduce_sum x23 -> x0, other arithmetic: 22.5 us -> none  [the longest x12 16.1 us: body(): alpha = product / lax.psum(jnp.sum(direction * image), ('sec', 'gx'))]
  transfers between devices with their start and end apart: 60 -> 2, of which waited for: 39 -> 2; matrix products, arithmetic and copies ran while one was open for 0% -> 0% of each run, Pallas kernels for 0% -> 0%
where the time goes in v1:
time: 171 us; the launch traced here: 170 us
  blocking collectives  97 us (57%)
  Pallas kernels  51.9 us (30%)
  waiting for transfers between devices  9.93 us (6%)
  starting transfers between devices  7.96 us (5%)
  local copies, waits for them, and re-layouts  2.67 us (2%)
    all_to_all x3, blocking collectives, add_up(): return lax.all_to_all(moments, ('sec', 'gx'), 0, 0, tiled=True)  68.5 us
    pallas_call x5, Pallas kernels, call(): pl.pallas_call(kernel, out_shape=outs, in_specs=[VMEM] * len(operands), o...  51.9 us
    all_to_all x1, blocking collectives, body(): mid = lax.all_to_all(packed, 'sec', 0, 0, tiled=True)  16.8 us
    all_to_all x1, blocking collectives, body(): out = lax.all_to_all(out, 'sec', 0, 0, tiled=True)  11.7 us
    ppermute x1, waiting for transfers between devices, body(): high = lax.ppermute(mid, 'gx', [(i + 1, i) for i in range(bands - 1)])  8.75 us
    ppermute x1, starting transfers between devices, body(): high = lax.ppermute(mid, 'gx', [(i + 1, i) for i in range(bands - 1)])  4.52 us
    ppermute x1, starting transfers between devices, body(): low = lax.ppermute(mid, 'gx', [(i, i + 1) for i in range(bands - 1)])  3.44 us
  transfers between devices with their start and end apart: 2, of which 2 were waited for; matrix products, arithmetic and copies ran while one was open for 0% of the time, Pallas kernels for 0%

profile of v1, /device:TPU:1, one launch (start us, length us, event | category | flops | bytes accessed | tf_op | source)
XLA Modules:
  0.0 170.1 jit_solution(8441249326657801628)
XLA Ops:
  0.6 2.1 %shard_map.68 = f32[4,9,16,384]{3,2,1,0:T(8,128)} custom-call(f32[4,16,1024]{2,1,0:T(8,128)} %head_ref.1, s32[4,16,1024]{2,1,0:T(8,128)} %soil_ref.1, f32[3,16,1024]{2,1,0:T(8,128)} %rain_ref.1), custom_call_target="tpu_custom_call" | custom-call | tf_op jit(solution)/shard_map/pallas_call | solution.py:276
  2.7 0.0 copy-start.3
  2.7 16.8 %all_to_all.43.refs_1_ = f32[4,9,16,384]{3,2,1,0:T(8,128)S(1)} all-to-all(f32[4,9,16,384]{3,2,1,0:T(8,128)} %shard_map.68), channel_id=1, replica_groups=mesh['sec'=4,'gx'=64] {'sec'}, dimensions={0} | all-to-all | bytes 1769472 | tf_op jit(solution)/shard_map/all_to_all | solution.py:294
  19.5 4.5 %collective-permute-start.1 = (f32[4,9,16,384]{3,2,1,0:T(8,128)S(1)}, f32[4,9,16,384]{3,2,1,0:T(8,128)S(1)}, u32[]{:S(2)}, u32[]{:S(2)}) collective-permute-start(f32[4,9,16,384]{3,2,1,0:T(8,128)S(1)} %all_to_all.43.refs_1_), channel_id=1, source_target_pairs={{1,0},{2,1},{3,2},{4,3},{5,4},{6,5},{7,6},{8,7},{9,8},{10,9},{11,1... | collective-permute-start | bytes 2654216 | tf_op jit(solution)/shard_map/ppermute | solution.py:296
  24.1 3.4 %collective-permute-start = (f32[4,9,16,384]{3,2,1,0:T(8,128)S(1)}, f32[4,9,16,384]{3,2,1,0:T(8,128)S(1)}, u32[]{:S(2)}, u32[]{:S(2)}) collective-permute-start(f32[4,9,16,384]{3,2,1,0:T(8,128)S(1)} %all_to_all.43.refs_1_), channel_id=1, source_target_pairs={{0,1},{1,2},{2,3},{3,4},{4,5},{5,6},{6,7},{7,8},{8,9},{9,10},{10,1... | collective-permute-start | bytes 2654216 | tf_op jit(solution)/shard_map/ppermute | solution.py:295
  27.5 0.0 copy-done.3
  27.5 0.0 copy-done.4
  27.6 8.7 %collective-permute-done.1.refs_2_ = f32[4,9,16,384]{3,2,1,0:T(8,128)S(1)} collective-permute-done((f32[4,9,16,384]{3,2,1,0:T(8,128)S(1)}, f32[4,9,16,384]{3,2,1,0:T(8,128)S(1)}, u32[]{:S(2)}, u32[]{:S(2)}) %collective-permute-start.1) | collective-permute-done | bytes 884768 | tf_op jit(solution)/shard_map/ppermute | solution.py:296
  36.3 1.2 collective-permute-done.refs_0_
  37.5 0.6 broadcast_in_dim.4.refs_3_
  38.1 0.0 copy-done
  38.1 0.0 copy-done.1
  38.1 0.4 copy-done.2
  38.5 16.8 %shard_map.69 = (f32[16,48,384]{2,1,0:T(8,128)}, f32[16,48,384]{2,1,0:T(8,128)}, f32[16,48,384]{2,1,0:T(8,128)}, f32[3,48,384]{2,1,0:T(8,128)}, f32[16,48,384]{2...) custom-call(f32[4,9,16,384]{3,2,1,0:T(8,128)} %copy-done.2, ...), custom_call_target="tpu_custom_call" | custom-call | tf_op jit(solution)/shard_map/pallas_call | solution.py:276
  55.3 27.9 %all_to_all.44 = f32[256,1,128]{2,1,0:T(1,128)} all-to-all(f32[256,1,128]{2,1,0:T(1,128)} %bitcast.25), channel_id=1, replica_groups=mesh['sec'=4,'gx'=64] {'sec','gx'}, dimensions={0} | all-to-all | bytes 262144 | tf_op jit(solution)/shard_map/all_to_all | solution.py:287
  83.2 15.6 %shard_map.70 = (f32[16,40,384]{2,1,0:T(8,128)}, f32[16,40,384]{2,1,0:T(8,128)}, f32[16,40,384]{2,1,0:T(8,128)}, f32[16,40,384]{2,1,0:T(8,128)}, f32[16,40,384]{...) custom-call(f32[256,128]{1,0:T(8,128)} %bitcast.21, f32[16,48,384]{2,1,0:T(8,128)} %get-tuple-element.27.refs_1_, ...), custom_call_target="tpu_custom_call" | custom-call | tf_op jit(solution)/shard_map/pallas_call | solution.py:276
  98.8 20.1 %all_to_all.45 = f32[256,1,128]{2,1,0:T(1,128)} all-to-all(f32[256,1,128]{2,1,0:T(1,128)} %bitcast.26), channel_id=1, replica_groups=mesh['sec'=4,'gx'=64] {'sec','gx'}, dimensions={0} | all-to-all | bytes 262144 | tf_op jit(solution)/shard_map/all_to_all | solution.py:287
  118.9 14.2 %shard_map.71 = (f32[16,32,384]{2,1,0:T(8,128)}, f32[16,32,384]{2,1,0:T(8,128)}, f32[16,32,384]{2,1,0:T(8,128)}, f32[16,32,384]{2,1,0:T(8,128)}, f32[16,32,384]{...) custom-call(f32[256,128]{1,0:T(8,128)} %bitcast.20, f32[16,40,384]{2,1,0:T(8,128)} %get-tuple-element.36.refs_1_, ...), custom_call_target="tpu_custom_call" | custom-call | tf_op jit(solution)/shard_map/pallas_call | solution.py:276
  133.1 20.5 %all_to_all.46 = f32[256,1,128]{2,1,0:T(1,128)} all-to-all(f32[256,1,128]{2,1,0:T(1,128)} %bitcast.24), channel_id=1, replica_groups=mesh['sec'=4,'gx'=64] {'sec','gx'}, dimensions={0} | all-to-all | bytes 262144 | tf_op jit(solution)/shard_map/all_to_all | solution.py:287
  153.5 3.2 %shard_map.72 = f32[4,7,16,256]{3,2,1,0:T(8,128)} custom-call(f32[256,128]{1,0:T(8,128)} %bitcast.22, f32[16,32,384]{2,1,0:T(8,128)} %get-tuple-element.42.head_ref, f32[16,32,384]{2,1,0:T(8,128)} %get-tuple-element.43.v0, f32[16,32,384]{2,1,0:T(8,128)} %get-tuple-element.44.v1, f32[16,32,384]{2,1,0:T(8,128)} %get-tuple-element.45.v2, ...), custom_call_target="tpu_custom_call" | custom-call | tf_op jit(solution)/shard_map/pallas_call | solution.py:276
  156.8 11.7 %all_to_all.47 = f32[4,7,16,256]{3,2,1,0:T(8,128)S(1)} all-to-all(f32[4,7,16,256]{3,2,1,0:T(8,128)} %shard_map.72), channel_id=1, replica_groups=mesh['sec'=4,'gx'=64] {'sec'}, dimensions={0} | all-to-all | bytes 917504 | tf_op jit(solution)/shard_map/all_to_all | solution.py:320
  168.5 0.7 copy.14
  169.2 0.1 copy.13
  169.4 0.8 broadcast_in_dim.10
  (7 shorter events, 0.0 us)
Async XLA Ops:
  2.7 24.8 %copy-start.3 = (f32[12]{0:T(128)S(1)}, f32[12]{0:T(128)}, u32[]{:S(2)}) copy-start(f32[12]{0:T(128)} %param.8) | copy-start | bytes 148
  2.7 24.8 %copy-start.4 = (f32[12]{0:T(128)S(1)}, f32[12]{0:T(128)}, u32[]{:S(2)}) copy-start(f32[12]{0:T(128)} %param.7) | copy-start | bytes 148
  19.5 18.6 %copy-start = (f32[4,9,16,384]{3,2,1,0:T(8,128)}, f32[4,9,16,384]{3,2,1,0:T(8,128)S(1)}, u32[]{:S(2)}) copy-start(f32[4,9,16,384]{3,2,1,0:T(8,128)S(1)} %all_to_all.43.refs_1_) | copy-start | bytes 2654212
  19.5 16.8 %collective-permute-start.1 = (f32[4,9,16,384]{3,2,1,0:T(8,128)S(1)}, f32[4,9,16,384]{3,2,1,0:T(8,128)S(1)}, u32[]{:S(2)}, u32[]{:S(2)}) collective-permute-start(f32[4,9,16,384]{3,2,1,0:T(8,128)S(1)} %all_to_all.43.refs_1_), channel_id=1, source_target_pairs={{1,0},{2,1},{3,2},{4,3},{5,4},{6,5},{7,6},{8,7},{9,8},{10,9},{11,1... | collective-permute-start | bytes 2654216 | tf_op jit(solution)/shard_map/ppermute | solution.py:296
  24.1 13.4 %collective-permute-start = (f32[4,9,16,384]{3,2,1,0:T(8,128)S(1)}, f32[4,9,16,384]{3,2,1,0:T(8,128)S(1)}, u32[]{:S(2)}, u32[]{:S(2)}) collective-permute-start(f32[4,9,16,384]{3,2,1,0:T(8,128)S(1)} %all_to_all.43.refs_1_), channel_id=1, source_target_pairs={{0,1},{1,2},{2,3},{3,4},{4,5},{5,6},{6,7},{7,8},{8,9},{9,10},{10,1... | collective-permute-start | bytes 2654216 | tf_op jit(solution)/shard_map/ppermute | solution.py:295
  36.3 1.8 %copy-start.1 = (f32[4,9,16,384]{3,2,1,0:T(8,128)}, f32[4,9,16,384]{3,2,1,0:T(8,128)S(1)}, u32[]{:S(2)}) copy-start(f32[4,9,16,384]{3,2,1,0:T(8,128)S(1)} %collective-permute-done.1.refs_2_) | copy-start | bytes 2654212
  37.5 1.0 copy-start.2

commit v2 on v1

--- a/solution.py
+++ b/solution.py
@@ -22,7 +22,7 @@
 
 
 def params():
-    return pltpu.CompilerParams(vmem_limit_bytes=56 * 1024 * 1024)
+    return pltpu.CompilerParams(vmem_limit_bytes=24 * 1024 * 1024)
 
 
 def pack_kernel(head_ref, soil_ref, rain_ref, out_ref):
@@ -272,7 +272,12 @@
     return jax.ShapeDtypeStruct(dims, F32)
 
 
-def call(kernel, operands, outs, scratch=()):
+def near(*dims):
+    return pltpu.VMEM(dims, F32)
+
+
+def call(kernel, operands, outs, scratch=(), held=()):
+    operands = [pltpu.with_memory_space_constraint(x, pltpu.VMEM) if i in held else x for i, x in enumerate(operands)]
     return pl.pallas_call(
         kernel,
         out_shape=outs,
@@ -302,21 +307,21 @@
         rows = r1 - r0
         field = (NZ, rows, WIDE)
         wide = (NZ, FRAME, WIDE)
-        outs = [shape(*field)] * 5
+        outs = [near(*field)] * 5
         kernel = functools.partial(step_kernel, step, bands * OWN_ROWS)
-        tail = [shape(SECTIONS, OWN_ROWS, OWN_COLS), shape(devices, 128)]
+        tail = [near(SECTIONS, OWN_ROWS, OWN_COLS), shape(devices, 128)]
         scratch = [field, field, field, (NZ + 1, rows, WIDE)] + [field] * 6 + [(SECTIONS, rows, WIDE)] * 2 + [(SECTIONS + 1, rows, WIDE)]
         if step == 0:
-            outs = [shape(*field), shape(*wide), shape(*wide), shape(3, FRAME, WIDE)] + [shape(*field)] * 4
-            got = call(kernel, (low, mid, high, tables), outs + tail, scratch)
+            outs = [near(*field), near(*wide), near(*wide), near(3, FRAME, WIDE)] + [near(*field)] * 4
+            got = call(kernel, (low, mid, high, tables), outs + tail, scratch, (0, 1, 2))
             head, cond, store, rain = got[:4]
             v = got[4:8]
         else:
-            got = call(kernel, (sums, head, *v, cond, store, rain), outs + tail, scratch)
+            got = call(kernel, (sums, head, *v, cond, store, rain), outs + tail, scratch, range(1, 9))
             head, v = got[0], got[1:5]
         inflows.append(got[-2])
         sums = add_up(got[-1])
-    out = call(last_kernel, (sums, head, *v, *inflows), shape(SECTIONS, 7, OWN_ROWS, OWN_COLS))
+    out = call(last_kernel, (sums, head, *v, *inflows), shape(SECTIONS, 7, OWN_ROWS, OWN_COLS), (), range(1, 9))
     out = lax.all_to_all(out, "sec", 0, 0, tiled=True)
     out = jnp.transpose(out, (1, 2, 0, 3)).reshape(7, OWN_ROWS, SECTIONS * OWN_COLS)
     return out[:LZ], out[LZ:][None]

time: 171 us -> 146 us (0.85)
  Pallas kernels: 51.9 us -> 31.9 us
  blocking collectives: 97 us -> 91.8 us
  local copies, waits for them, and re-layouts: 2.67 us -> 4.5 us
    pallas_call x5, Pallas kernels: 51.9 us -> 31.9 us  [call(): pl.pallas_call(kernel, out_shape=outs, in_specs=[VMEM] * len(operands), o...]
    all_to_all x3, blocking collectives: 68.5 us -> 64.2 us  [add_up(): return lax.all_to_all(moments, ('sec', 'gx'), 0, 0, tiled=True)]
    unnamed x11, local copies, waits for them, and re-layouts: 0.39 us -> 2.85 us
where the time goes in v2:
time: 146 us
  blocking collectives  91.8 us (63%)
  Pallas kernels  31.9 us (22%)
  waiting for transfers between devices  9.93 us (7%)
  starting transfers between devices  7.2 us (5%)
  local copies, waits for them, and re-layouts  4.5 us (3%)
    all_to_all x3, blocking collectives, add_up(): return lax.all_to_all(moments, ('sec', 'gx'), 0, 0, tiled=True)  64.2 us
    pallas_call x5, Pallas kernels, call(): pl.pallas_call(kernel, out_shape=outs, in_specs=[VMEM] * len(operands), o...  31.9 us
    all_to_all x1, blocking collectives, body(): mid = lax.all_to_all(packed, 'sec', 0, 0, tiled=True)  17.2 us
    all_to_all x1, blocking collectives, body(): out = lax.all_to_all(out, 'sec', 0, 0, tiled=True)  10.3 us
    ppermute x1, waiting for transfers between devices, body(): high = lax.ppermute(mid, 'gx', [(i + 1, i) for i in range(bands - 1)])  8.75 us
    ppermute x1, starting transfers between devices, body(): high = lax.ppermute(mid, 'gx', [(i + 1, i) for i in range(bands - 1)])  3.76 us
    ppermute x1, starting transfers between devices, body(): low = lax.ppermute(mid, 'gx', [(i, i + 1) for i in range(bands - 1)])  3.44 us
  transfers between devices with their start and end apart: 2, of which 2 were waited for; matrix products, arithmetic and copies ran while one was open for 0% of the time, Pallas kernels for 0%

profile of v2, /device:TPU:1, one launch (start us, length us, event | category | flops | bytes accessed | tf_op | source)
XLA Modules:
  0.0 146.1 jit_solution(8540159433239216745)
XLA Ops:
  0.6 0.0 copy-start
  0.6 0.9 copy-done
  1.6 0.9 copy-done.1
  2.5 0.9 copy-done.2
  3.5 0.1 shard_map.68
  3.5 0.0 copy-start.3
  3.5 0.0 copy-start.4
  3.5 17.2 %all_to_all.43.refs_1_ = f32[4,9,16,384]{3,2,1,0:T(8,128)S(1)} all-to-all(f32[4,9,16,384]{3,2,1,0:T(8,128)S(1)} %shard_map.68), channel_id=1, replica_groups=mesh['sec'=4,'gx'=64] {'sec'}, dimensions={0} | all-to-all | bytes 1769472 | tf_op jit(solution)/shard_map/all_to_all | solution.py:299
  20.8 3.8 %collective-permute-start.1 = (f32[4,9,16,384]{3,2,1,0:T(8,128)S(1)}, f32[4,9,16,384]{3,2,1,0:T(8,128)S(1)}, u32[]{:S(2)}, u32[]{:S(2)}) collective-permute-start(f32[4,9,16,384]{3,2,1,0:T(8,128)S(1)} %all_to_all.43.refs_1_), channel_id=1, source_target_pairs={{1,0},{2,1},{3,2},{4,3},{5,4},{6,5},{7,6},{8,7},{9,8},{10,9},{11,1... | collective-permute-start | bytes 2654216 | tf_op jit(solution)/shard_map/ppermute | solution.py:301
  24.6 3.4 %collective-permute-start = (f32[4,9,16,384]{3,2,1,0:T(8,128)S(1)}, f32[4,9,16,384]{3,2,1,0:T(8,128)S(1)}, u32[]{:S(2)}, u32[]{:S(2)}) collective-permute-start(f32[4,9,16,384]{3,2,1,0:T(8,128)S(1)} %all_to_all.43.refs_1_), channel_id=1, source_target_pairs={{0,1},{1,2},{2,3},{3,4},{4,5},{5,6},{6,7},{7,8},{8,9},{9,10},{10,1... | collective-permute-start | bytes 2654216 | tf_op jit(solution)/shard_map/ppermute | solution.py:300
  28.0 0.0 copy-done.3
  28.0 8.7 %collective-permute-done.1.refs_2_ = f32[4,9,16,384]{3,2,1,0:T(8,128)S(1)} collective-permute-done((f32[4,9,16,384]{3,2,1,0:T(8,128)S(1)}, f32[4,9,16,384]{3,2,1,0:T(8,128)S(1)}, u32[]{:S(2)}, u32[]{:S(2)}) %collective-permute-start.1) | collective-permute-done | bytes 884768 | tf_op jit(solution)/shard_map/ppermute | solution.py:301
  36.8 1.2 collective-permute-done.refs_0_
  38.0 12.1 %shard_map.69 = (f32[16,48,384]{2,1,0:T(8,128)S(1)}, f32[16,48,384]{2,1,0:T(8,128)S(1)}, f32[16,48,384]{2,1,0:T(8,128)S(1)}, f32[3,48,384]{2,1,0:T(8,128)S(1)}, ...) custom-call(f32[4,9,16,384]{3,2,1,0:T(8,128)S(1)} %collective-permut, ...), custom_call_target="tpu_custom_call" | custom-call | tf_op jit(solution)/shard_map/pallas_call | solution.py:281
  50.1 27.0 %all_to_all.44 = f32[256,1,128]{2,1,0:T(1,128)S(1)} all-to-all(f32[256,1,128]{2,1,0:T(1,128)S(1)} %bitcast.22), channel_id=1, replica_groups=mesh['sec'=4,'gx'=64] {'sec','gx'}, dimensions={0} | all-to-all | bytes 262144 | tf_op jit(solution)/shard_map/all_to_all | solution.py:292
  77.1 10.2 %shard_map.70 = (f32[16,40,384]{2,1,0:T(8,128)S(1)}, f32[16,40,384]{2,1,0:T(8,128)S(1)}, f32[16,40,384]{2,1,0:T(8,128)S(1)}, f32[16,40,384]{2,1,0:T(8,128)S(1)},...) custom-call(f32[256,128]{1,0:T(8,128)S(1)} %bitcast.19, ...), custom_call_target="tpu_custom_call" | custom-call | tf_op jit(solution)/shard_map/pallas_call | solution.py:281
  87.2 18.6 %all_to_all.45 = f32[256,1,128]{2,1,0:T(1,128)S(1)} all-to-all(f32[256,1,128]{2,1,0:T(1,128)S(1)} %bitcast.23), channel_id=1, replica_groups=mesh['sec'=4,'gx'=64] {'sec','gx'}, dimensions={0} | all-to-all | bytes 262144 | tf_op jit(solution)/shard_map/all_to_all | solution.py:292
  105.8 9.3 %shard_map.71 = (f32[16,32,384]{2,1,0:T(8,128)S(1)}, f32[16,32,384]{2,1,0:T(8,128)S(1)}, f32[16,32,384]{2,1,0:T(8,128)S(1)}, f32[16,32,384]{2,1,0:T(8,128)S(1)},...) custom-call(f32[256,128]{1,0:T(8,128)S(1)} %bitcast.18, ...), custom_call_target="tpu_custom_call" | custom-call | tf_op jit(solution)/shard_map/pallas_call | solution.py:281
  115.1 18.6 %all_to_all.46 = f32[256,1,128]{2,1,0:T(1,128)S(1)} all-to-all(f32[256,1,128]{2,1,0:T(1,128)S(1)} %bitcast.21), channel_id=1, replica_groups=mesh['sec'=4,'gx'=64] {'sec','gx'}, dimensions={0} | all-to-all | bytes 262144 | tf_op jit(solution)/shard_map/all_to_all | solution.py:292
  133.7 0.3 shard_map.72
  134.1 10.3 %all_to_all.47 = f32[4,7,16,256]{3,2,1,0:T(8,128)S(1)} all-to-all(f32[4,7,16,256]{3,2,1,0:T(8,128)S(1)} %shard_map.72), channel_id=1, replica_groups=mesh['sec'=4,'gx'=64] {'sec'}, dimensions={0} | all-to-all | bytes 917504 | tf_op jit(solution)/shard_map/all_to_all | solution.py:325
  144.4 0.7 copy.14
  145.1 0.1 copy.13
  145.3 0.8 broadcast_in_dim.10
  (7 shorter events, 0.0 us)
Async XLA Ops:
  0.6 1.0 copy-start
  1.6 0.9 copy-start.1
  2.5 0.9 copy-start.2
  3.5 24.5 %copy-start.3 = (f32[12]{0:T(128)S(1)}, f32[12]{0:T(128)}, u32[]{:S(2)}) copy-start(f32[12]{0:T(128)} %param.8) | copy-start | bytes 148
  3.5 24.5 %copy-start.4 = (f32[12]{0:T(128)S(1)}, f32[12]{0:T(128)}, u32[]{:S(2)}) copy-start(f32[12]{0:T(128)} %param.7) | copy-start | bytes 148
  20.8 16.0 %collective-permute-start.1 = (f32[4,9,16,384]{3,2,1,0:T(8,128)S(1)}, f32[4,9,16,384]{3,2,1,0:T(8,128)S(1)}, u32[]{:S(2)}, u32[]{:S(2)}) collective-permute-start(f32[4,9,16,384]{3,2,1,0:T(8,128)S(1)} %all_to_all.43.refs_1_), channel_id=1, source_target_pairs={{1,0},{2,1},{3,2},{4,3},{5,4},{6,5},{7,6},{8,7},{9,8},{10,9},{11,1... | collective-permute-start | bytes 2654216 | tf_op jit(solution)/shard_map/ppermute | solution.py:301
  24.6 13.4 %collective-permute-start = (f32[4,9,16,384]{3,2,1,0:T(8,128)S(1)}, f32[4,9,16,384]{3,2,1,0:T(8,128)S(1)}, u32[]{:S(2)}, u32[]{:S(2)}) collective-permute-start(f32[4,9,16,384]{3,2,1,0:T(8,128)S(1)} %all_to_all.43.refs_1_), channel_id=1, source_target_pairs={{0,1},{1,2},{2,3},{3,4},{4,5},{5,6},{6,7},{7,8},{8,9},{9,10},{10,1... | collective-permute-start | bytes 2654216 | tf_op jit(solution)/shard_map/ppermute | solution.py:300

commit v3 on v2

--- a/solution.py
+++ b/solution.py
@@ -17,6 +17,7 @@
 HALF = 64
 FRAME = 48
 SPANS = ((0, 48), (0, 40), (8, 40))
+WORK = ((0, 48), (8, 40), (8, 40))
 F32 = jnp.float32
 VMEM = pl.BlockSpec(memory_space=pltpu.VMEM)
 
@@ -78,6 +79,12 @@
     return change
 
 
+def loop(n, f, init):
+    for i in range(n):
+        init = f(i, init)
+    return init
+
+
 def recip(x):
     return pl.reciprocal(x, approx=False)
 
@@ -109,18 +116,21 @@
     first = step == 0
     r0, r1 = SPANS[step]
     rows = r1 - r0
-    own = OWN_ROWS - r0
+    w0, w1 = WORK[step]
+    span = w1 - w0
+    work = slice(w0 - r0, w1 - r0)
+    own = OWN_ROWS - w0
     if first:
         (low_ref, mid_ref, high_ref, tables_ref, head_ref, cond_ref, store_ref, rain_ref) = refs[:8]
         refs = refs[8:]
     else:
-        p0 = SPANS[step - 1][0]
-        old = slice(r0 - p0, r1 - p0)
+        old = slice(r0 - SPANS[step - 1][0], r1 - SPANS[step - 1][0])
+        old_work = slice(r0 - WORK[step - 1][0], r1 - WORK[step - 1][0])
         (sums_ref, old_head_ref, o0, o1, o2, o3, cond_ref, store_ref, rain_ref, head_ref) = refs[:10]
         old_basis = (o0, o1, o2, o3)
         refs = refs[10:]
     (v0, v1, v2, v3, inflow_ref, moments_ref) = refs[:6]
-    (res_ref, cap_ref, diag_ref, face_ref, up_ref, dn_ref, ru_ref, rd_ref, xl_ref, xr_ref, water_ref, low_cond_ref, flux_ref) = refs[6:]
+    (res_ref, cap_ref, diag_ref, up_ref, dn_ref, ru_ref, rd_ref, xl_ref, xr_ref, water_ref, low_cond_ref, flux_ref) = refs[6:]
     basis = (v0, v1, v2, v3)
     here = slice(r0, r1)
     section, band = lax.axis_index("sec"), lax.axis_index("gx")
@@ -133,7 +143,7 @@
     else:
         change = weights(sums_ref)
 
-    def soil(s, carry):
+    for s in range(SECTIONS):
         total = jnp.zeros((rows, WIDE), F32)
         for q in range(LZ):
             l = s * LZ + q
@@ -148,7 +158,7 @@
             else:
                 h = old_head_ref[l, old, :]
                 for c, o in zip(change, old_basis):
-                    h = h + c * o[l, old, :]
+                    h = h + c * o[l, old_work, :]
                 head_ref[l] = h
             saturation, cond, capacity = setup_terms(h, cond_ref[l, here, :], store_ref[l, here, :])
             res_ref[l] = recip(cond)
@@ -157,9 +167,6 @@
             if q == LZ - 1:
                 low_cond_ref[s] = 0.5 * cond
         water_ref[s] = total
-        return carry
-
-    lax.fori_loop(0, SECTIONS, soil, 0)
 
     flux_ref[0] = rain_ref[step, here, :]
     belows = [None] * SECTIONS
@@ -170,80 +177,87 @@
     for s in range(SECTIONS):
         scale = 0.5 if belows[s] is None else 0.5 + 0.5 * belows[s] / (belows[s] + 4.0)
         flux_ref[s + 1] = water_ref[s] * 0.25 * scale * flux_ref[s] + low_cond_ref[s]
-        inflow_ref[s] = flux_ref[s, own : own + OWN_ROWS, 0:OWN_COLS]
-
-    lane = lax.broadcasted_iota(jnp.int32, (rows, WIDE), 1)
+        inflow_ref[s] = flux_ref[s, OWN_ROWS - r0 : 2 * OWN_ROWS - r0, 0:OWN_COLS]
+
+    lane = lax.broadcasted_iota(jnp.int32, (span, WIDE), 1)
     col = section * OWN_COLS + lane - jnp.where(lane >= OWN_COLS + HALF, WIDE, 0)
-    row = band * OWN_ROWS + (r0 - OWN_ROWS) + lax.broadcasted_iota(jnp.int32, (rows, WIDE), 0)
+    row = band * OWN_ROWS + (w0 - OWN_ROWS) + lax.broadcasted_iota(jnp.int32, (span, WIDE), 0)
     col_gate = jnp.where((col >= 1) & (col < SECTIONS * OWN_COLS), 2.0, 0.0).astype(F32)
     row_gate = jnp.where((row >= 1) & (row < n_rows_all), 2.0, 0.0).astype(F32)
     kept = slice(own, own + OWN_ROWS)
     none = jnp.zeros((OWN_ROWS, OWN_COLS), F32)
 
-    face_ref[0] = jnp.zeros((rows, WIDE), F32)
-
-    def faces(s, acc):
-        for q in range(LZ):
-            l = s * LZ + q
-            res = res_ref[l]
-            up = face_ref[l]
-            after = jnp.minimum(l + 1, NZ - 1)
-            dn = jnp.where(l < NZ - 1, 2.0, 0.0).astype(F32) * recip(res + res_ref[after])
-            face_ref[l + 1] = dn
-            ru = row_gate * recip(res + pltpu.roll(res, 1, 0))
-            rd = pltpu.roll(ru, rows - 1, 0)
-            xl = col_gate * recip(res + pltpu.roll(res, 1, 1))
-            xr = pltpu.roll(xl, WIDE - 1, 1)
-            diag = cap_ref[l] + up + dn + ru + rd + xl + xr
-            inv = recip(diag)
-            h = head_ref[l]
-            r = up - dn
-            if q == 0:
-                r = r + flux_ref[s]
-            if q == LZ - 1:
-                r = r - flux_ref[s + 1]
-            r = r + up * (head_ref[jnp.maximum(l - 1, 0)] - h) + dn * (head_ref[after] - h)
-            r = r + ru * (pltpu.roll(h, 1, 0) - h) + rd * (pltpu.roll(h, rows - 1, 0) - h)
-            r = r + xl * (pltpu.roll(h, 1, 1) - h) + xr * (pltpu.roll(h, WIDE - 1, 1) - h)
-            z = r * inv
-            v0[l] = z
-            diag_ref[l] = diag
+    def turned(x, by, axis):
+        return pltpu.roll(x, by % x.shape[axis], axis)
+
+    def faces(l, carry):
+        acc, up = carry
+        res = res_ref[l, work, :]
+        h = head_ref[l, work, :]
+        if l + 1 < NZ:
+            dn = 2.0 * recip(res + res_ref[l + 1, work, :])
+        else:
+            dn = jnp.zeros_like(res)
+        ru = row_gate * recip(res + turned(res_ref[l], 1, 0)[work])
+        rd = turned(ru, -1, 0)
+        xl = col_gate * recip(res + turned(res, 1, 1))
+        xr = turned(xl, -1, 1)
+        diag = cap_ref[l, work, :] + up + dn + ru + rd + xl + xr
+        inv = recip(diag)
+        r = up - dn
+        if l % LZ == 0:
+            r = r + flux_ref[l // LZ, work, :]
+        if l % LZ == LZ - 1:
+            r = r - flux_ref[l // LZ + 1, work, :]
+        if l > 0:
+            r = r + up * (head_ref[l - 1, work, :] - h)
+        if l + 1 < NZ:
+            r = r + dn * (head_ref[l + 1, work, :] - h)
+        r = r + ru * (turned(head_ref[l], 1, 0)[work] - h) + rd * (turned(head_ref[l], -1, 0)[work] - h)
+        r = r + xl * (turned(h, 1, 1) - h) + xr * (turned(h, -1, 1) - h)
+        z = r * inv
+        v0[l] = z
+        diag_ref[l] = diag[kept, 0:OWN_COLS]
+        if l > 0:
             up_ref[l] = up * inv
+        if l + 1 < NZ:
             dn_ref[l] = dn * inv
-            ru_ref[l] = ru * inv
-            rd_ref[l] = rd * inv
-            xl_ref[l] = xl * inv
-            xr_ref[l] = xr * inv
-            acc = acc + (r * z)[kept, 0:OWN_COLS]
-        return acc
-
-    moments = [lax.fori_loop(0, SECTIONS, faces, none)]
+        ru_ref[l] = ru * inv
+        rd_ref[l] = rd * inv
+        xl_ref[l] = xl * inv
+        xr_ref[l] = xr * inv
+        return acc + (r * z)[kept, 0:OWN_COLS], dn
+
+    moments = [loop(NZ, faces, (none, jnp.zeros((span, WIDE), F32)))[0]]
 
     for k in range(1, ITERS):
         src, dst = basis[k - 1], basis[k]
 
-        def smooth(l, accs, src=src, dst=dst):
+        def smooth(l, accs):
             v = src[l]
-            new = up_ref[l] * src[jnp.maximum(l - 1, 0)] + dn_ref[l] * src[jnp.minimum(l + 1, NZ - 1)]
-            new = new + ru_ref[l] * pltpu.roll(v, 1, 0) + rd_ref[l] * pltpu.roll(v, rows - 1, 0)
-            new = new + xl_ref[l] * pltpu.roll(v, 1, 1) + xr_ref[l] * pltpu.roll(v, WIDE - 1, 1)
+            new = ru_ref[l] * turned(v, 1, 0) + rd_ref[l] * turned(v, -1, 0)
+            new = new + xl_ref[l] * turned(v, 1, 1) + xr_ref[l] * turned(v, -1, 1)
+            if l > 0:
+                new = new + up_ref[l] * src[l - 1]
+            if l + 1 < NZ:
+                new = new + dn_ref[l] * src[l + 1]
             dst[l] = new
             mine = new[kept, 0:OWN_COLS]
-            scaled = mine * diag_ref[l, kept, 0:OWN_COLS]
+            scaled = mine * diag_ref[l]
             return accs[0] + v[kept, 0:OWN_COLS] * scaled, accs[1] + mine * scaled
 
-        moments.extend(lax.fori_loop(0, NZ, smooth, (none, none)))
+        moments.extend(loop(NZ, smooth, (none, none)))
 
     def last(l, acc):
-        block = slice(own - 8, own + OWN_ROWS)
-        v = v3[l, block, :]
+        v = v3[l, own - 8 : own + OWN_ROWS, :]
         mine = v[8:, 0:OWN_COLS]
-        pairs = up_ref[l, kept, 0:OWN_COLS] * v3[jnp.maximum(l - 1, 0), kept, 0:OWN_COLS]
-        pairs = pairs + ru_ref[l, kept, 0:OWN_COLS] * pltpu.roll(v, 1, 0)[8:, 0:OWN_COLS]
-        pairs = pairs + xl_ref[l, kept, 0:OWN_COLS] * pltpu.roll(v, 1, 1)[8:, 0:OWN_COLS]
-        return acc + 2.0 * mine * diag_ref[l, kept, 0:OWN_COLS] * pairs
-
-    moments.append(lax.fori_loop(0, NZ, last, none))
+        pairs = ru_ref[l, kept, 0:OWN_COLS] * turned(v, 1, 0)[8:, 0:OWN_COLS]
+        pairs = pairs + xl_ref[l, kept, 0:OWN_COLS] * turned(v, 1, 1)[8:, 0:OWN_COLS]
+        if l > 0:
+            pairs = pairs + up_ref[l, kept, 0:OWN_COLS] * v3[l - 1, kept, 0:OWN_COLS]
+        return acc + 2.0 * mine * diag_ref[l] * pairs
+
+    moments.append(loop(NZ, last, none))
 
     spot = lax.broadcasted_iota(jnp.int32, (8, 128), 1)
     line = jnp.zeros((8, 128), F32)
@@ -256,10 +270,10 @@
 
 def last_kernel(sums_ref, head_ref, v0, v1, v2, v3, i0, i1, i2, out_ref):
     change = weights(sums_ref)
-    own = OWN_ROWS - SPANS[2][0]
+    own = OWN_ROWS - WORK[2][0]
     kept = slice(own, own + OWN_ROWS)
     for l in range(NZ):
-        h = head_ref[l, kept, 0:OWN_COLS]
+        h = head_ref[l, OWN_ROWS - SPANS[2][0] : 2 * OWN_ROWS - SPANS[2][0], 0:OWN_COLS]
         for c, o in zip(change, (v0, v1, v2, v3)):
             h = h + c * o[l, kept, 0:OWN_COLS]
         out_ref[l // LZ, l % LZ] = h
@@ -306,13 +320,14 @@
     for step, (r0, r1) in enumerate(SPANS):
         rows = r1 - r0
         field = (NZ, rows, WIDE)
+        basis = (NZ, WORK[step][1] - WORK[step][0], WIDE)
         wide = (NZ, FRAME, WIDE)
-        outs = [near(*field)] * 5
+        outs = [near(*field)] + [near(*basis)] * 4
         kernel = functools.partial(step_kernel, step, bands * OWN_ROWS)
         tail = [near(SECTIONS, OWN_ROWS, OWN_COLS), shape(devices, 128)]
-        scratch = [field, field, field, (NZ + 1, rows, WIDE)] + [field] * 6 + [(SECTIONS, rows, WIDE)] * 2 + [(SECTIONS + 1, rows, WIDE)]
+        scratch = [field, field, (NZ, OWN_ROWS, OWN_COLS)] + [basis] * 6 + [(SECTIONS, rows, WIDE)] * 2 + [(SECTIONS + 1, rows, WIDE)]
         if step == 0:
-            outs = [near(*field), near(*wide), near(*wide), near(3, FRAME, WIDE)] + [near(*field)] * 4
+            outs = [near(*field), near(*wide), near(*wide), near(3, FRAME, WIDE)] + [near(*basis)] * 4
             got = call(kernel, (low, mid, high, tables), outs + tail, scratch, (0, 1, 2))
             head, cond, store, rain = got[:4]
             v = got[4:8]

time: 146 us -> 134 us (0.918)
  Pallas kernels: 31.9 us -> 19.3 us
    pallas_call x5, Pallas kernels: 31.9 us -> 19.3 us  [call(): pl.pallas_call(kernel, out_shape=outs, in_specs=[VMEM] * len(operands), o...]
where the time goes in v3:
time: 134 us
  blocking collectives  91.8 us (69%)
  Pallas kernels  19.3 us (14%)
  waiting for transfers between devices  9.93 us (7%)
  starting transfers between devices  7.2 us (5%)
  local copies, waits for them, and re-layouts  4.5 us (3%)
    all_to_all x3, blocking collectives, add_up(): return lax.all_to_all(moments, ('sec', 'gx'), 0, 0, tiled=True)  64.2 us
    pallas_call x5, Pallas kernels, call(): pl.pallas_call(kernel, out_shape=outs, in_specs=[VMEM] * len(operands), o...  19.3 us
    all_to_all x1, blocking collectives, body(): mid = lax.all_to_all(packed, 'sec', 0, 0, tiled=True)  17.2 us
    all_to_all x1, blocking collectives, body(): out = lax.all_to_all(out, 'sec', 0, 0, tiled=True)  10.3 us
    ppermute x1, waiting for transfers between devices, body(): high = lax.ppermute(mid, 'gx', [(i + 1, i) for i in range(bands - 1)])  8.75 us
    ppermute x1, starting transfers between devices, body(): high = lax.ppermute(mid, 'gx', [(i + 1, i) for i in range(bands - 1)])  3.76 us
    ppermute x1, starting transfers between devices, body(): low = lax.ppermute(mid, 'gx', [(i, i + 1) for i in range(bands - 1)])  3.44 us
    unnamed x11, local copies, waits for them, and re-layouts  2.85 us
  transfers between devices with their start and end apart: 2, of which 2 were waited for; matrix products, arithmetic and copies ran while one was open for 0% of the time, Pallas kernels for 0%

profile of v3, /device:TPU:1, one launch (start us, length us, event | category | flops | bytes accessed | tf_op | source)
XLA Modules:
  0.0 133.5 jit_solution(10670792419609885840)
XLA Ops:
  0.6 0.0 copy-start
  0.6 0.9 copy-done
  1.6 0.9 copy-done.1
  2.5 0.9 copy-done.2
  3.5 0.1 shard_map.68
  3.5 0.0 copy-start.3
  3.5 0.0 copy-start.4
  3.5 17.2 %all_to_all.43.refs_1_ = f32[4,9,16,384]{3,2,1,0:T(8,128)S(1)} all-to-all(f32[4,9,16,384]{3,2,1,0:T(8,128)S(1)} %shard_map.68), channel_id=1, replica_groups=mesh['sec'=4,'gx'=64] {'sec'}, dimensions={0} | all-to-all | bytes 1769472 | tf_op jit(solution)/shard_map/all_to_all | solution.py:313
  20.8 3.8 %collective-permute-start.1 = (f32[4,9,16,384]{3,2,1,0:T(8,128)S(1)}, f32[4,9,16,384]{3,2,1,0:T(8,128)S(1)}, u32[]{:S(2)}, u32[]{:S(2)}) collective-permute-start(f32[4,9,16,384]{3,2,1,0:T(8,128)S(1)} %all_to_all.43.refs_1_), channel_id=1, source_target_pairs={{1,0},{2,1},{3,2},{4,3},{5,4},{6,5},{7,6},{8,7},{9,8},{10,9},{11,1... | collective-permute-start | bytes 2654216 | tf_op jit(solution)/shard_map/ppermute | solution.py:315
  24.6 3.4 %collective-permute-start = (f32[4,9,16,384]{3,2,1,0:T(8,128)S(1)}, f32[4,9,16,384]{3,2,1,0:T(8,128)S(1)}, u32[]{:S(2)}, u32[]{:S(2)}) collective-permute-start(f32[4,9,16,384]{3,2,1,0:T(8,128)S(1)} %all_to_all.43.refs_1_), channel_id=1, source_target_pairs={{0,1},{1,2},{2,3},{3,4},{4,5},{5,6},{6,7},{7,8},{8,9},{9,10},{10,1... | collective-permute-start | bytes 2654216 | tf_op jit(solution)/shard_map/ppermute | solution.py:314
  28.0 0.0 copy-done.3
  28.0 8.7 %collective-permute-done.1.refs_2_ = f32[4,9,16,384]{3,2,1,0:T(8,128)S(1)} collective-permute-done((f32[4,9,16,384]{3,2,1,0:T(8,128)S(1)}, f32[4,9,16,384]{3,2,1,0:T(8,128)S(1)}, u32[]{:S(2)}, u32[]{:S(2)}) %collective-permute-start.1) | collective-permute-done | bytes 884768 | tf_op jit(solution)/shard_map/ppermute | solution.py:315
  36.8 1.2 collective-permute-done.refs_0_
  38.0 8.4 %shard_map.69 = (f32[16,48,384]{2,1,0:T(8,128)S(1)}, f32[16,48,384]{2,1,0:T(8,128)S(1)}, f32[16,48,384]{2,1,0:T(8,128)S(1)}, f32[3,48,384]{2,1,0:T(8,128)S(1)}, ...) custom-call(f32[4,9,16,384]{3,2,1,0:T(8,128)S(1)} %collective-permut, ...), custom_call_target="tpu_custom_call" | custom-call | tf_op jit(solution)/shard_map/pallas_call | solution.py:295
  46.4 27.0 %all_to_all.44 = f32[256,1,128]{2,1,0:T(1,128)S(1)} all-to-all(f32[256,1,128]{2,1,0:T(1,128)S(1)} %bitcast.22), channel_id=1, replica_groups=mesh['sec'=4,'gx'=64] {'sec','gx'}, dimensions={0} | all-to-all | bytes 262144 | tf_op jit(solution)/shard_map/all_to_all | solution.py:306
  73.4 5.3 %shard_map.70 = (f32[16,40,384]{2,1,0:T(8,128)S(1)}, f32[16,32,384]{2,1,0:T(8,128)S(1)}, f32[16,32,384]{2,1,0:T(8,128)S(1)}, f32[16,32,384]{2,1,0:T(8,128)S(1)},...) custom-call(f32[256,128]{1,0:T(8,128)S(1)} %bitcast.18, ...), custom_call_target="tpu_custom_call" | custom-call | tf_op jit(solution)/shard_map/pallas_call | solution.py:295
  78.7 18.6 %all_to_all.45 = f32[256,1,128]{2,1,0:T(1,128)S(1)} all-to-all(f32[256,1,128]{2,1,0:T(1,128)S(1)} %bitcast.23), channel_id=1, replica_groups=mesh['sec'=4,'gx'=64] {'sec','gx'}, dimensions={0} | all-to-all | bytes 262144 | tf_op jit(solution)/shard_map/all_to_all | solution.py:306
  97.3 5.3 %shard_map.71 = (f32[16,32,384]{2,1,0:T(8,128)S(1)}, f32[16,32,384]{2,1,0:T(8,128)S(1)}, f32[16,32,384]{2,1,0:T(8,128)S(1)}, f32[16,32,384]{2,1,0:T(8,128)S(1)},...) custom-call(f32[256,128]{1,0:T(8,128)S(1)} %bitcast.20, ...), custom_call_target="tpu_custom_call" | custom-call | tf_op jit(solution)/shard_map/pallas_call | solution.py:295
  102.6 18.6 %all_to_all.46 = f32[256,1,128]{2,1,0:T(1,128)S(1)} all-to-all(f32[256,1,128]{2,1,0:T(1,128)S(1)} %bitcast.21), channel_id=1, replica_groups=mesh['sec'=4,'gx'=64] {'sec','gx'}, dimensions={0} | all-to-all | bytes 262144 | tf_op jit(solution)/shard_map/all_to_all | solution.py:306
  121.2 0.3 shard_map.72
  121.5 10.3 %all_to_all.47 = f32[4,7,16,256]{3,2,1,0:T(8,128)S(1)} all-to-all(f32[4,7,16,256]{3,2,1,0:T(8,128)S(1)} %shard_map.72), channel_id=1, replica_groups=mesh['sec'=4,'gx'=64] {'sec'}, dimensions={0} | all-to-all | bytes 917504 | tf_op jit(solution)/shard_map/all_to_all | solution.py:340
  131.9 0.7 copy.14
  132.6 0.1 copy.13
  132.8 0.8 broadcast_in_dim.10
  (7 shorter events, 0.0 us)
Async XLA Ops:
  0.6 1.0 copy-start
  1.6 0.9 copy-start.1
  2.5 0.9 copy-start.2
  3.5 24.5 %copy-start.3 = (f32[12]{0:T(128)S(1)}, f32[12]{0:T(128)}, u32[]{:S(2)}) copy-start(f32[12]{0:T(128)} %param.8) | copy-start | bytes 148
  3.5 24.5 %copy-start.4 = (f32[12]{0:T(128)S(1)}, f32[12]{0:T(128)}, u32[]{:S(2)}) copy-start(f32[12]{0:T(128)} %param.7) | copy-start | bytes 148
  20.8 16.0 %collective-permute-start.1 = (f32[4,9,16,384]{3,2,1,0:T(8,128)S(1)}, f32[4,9,16,384]{3,2,1,0:T(8,128)S(1)}, u32[]{:S(2)}, u32[]{:S(2)}) collective-permute-start(f32[4,9,16,384]{3,2,1,0:T(8,128)S(1)} %all_to_all.43.refs_1_), channel_id=1, source_target_pairs={{1,0},{2,1},{3,2},{4,3},{5,4},{6,5},{7,6},{8,7},{9,8},{10,9},{11,1... | collective-permute-start | bytes 2654216 | tf_op jit(solution)/shard_map/ppermute | solution.py:315
  24.6 13.4 %collective-permute-start = (f32[4,9,16,384]{3,2,1,0:T(8,128)S(1)}, f32[4,9,16,384]{3,2,1,0:T(8,128)S(1)}, u32[]{:S(2)}, u32[]{:S(2)}) collective-permute-start(f32[4,9,16,384]{3,2,1,0:T(8,128)S(1)} %all_to_all.43.refs_1_), channel_id=1, source_target_pairs={{0,1},{1,2},{2,3},{3,4},{4,5},{5,6},{6,7},{7,8},{8,9},{9,10},{10,1... | collective-permute-start | bytes 2654216 | tf_op jit(solution)/shard_map/ppermute | solution.py:314

commit v4 on v3

--- a/solution.py
+++ b/solution.py
@@ -15,7 +15,10 @@
 OWN_COLS = 256
 WIDE = 384
 HALF = 64
+EDGE = 16
 FRAME = 48
+LOW, HIGH = 13, 12
+SLOTS = 40
 SPANS = ((0, 48), (0, 40), (8, 40))
 WORK = ((0, 48), (8, 40), (8, 40))
 F32 = jnp.float32
@@ -26,23 +29,66 @@
     return pltpu.CompilerParams(vmem_limit_bytes=24 * 1024 * 1024)
 
 
-def pack_kernel(head_ref, soil_ref, rain_ref, out_ref):
+def turned(x, by, axis):
+    return pltpu.roll(x, by % x.shape[axis], axis)
+
+
+def lanes(rows):
+    return lax.broadcasted_iota(jnp.int32, (rows, 128), 1)
+
+
+def tail_of(after, before):
+    return jnp.where(lanes(after.shape[0]) < EDGE, after, turned(before, 2 * EDGE, 1))
+
+
+def grouped(tails):
+    lane = lanes(tails[0].shape[0])
+    tile = tails[0]
+    for j in range(1, len(tails)):
+        tile = jnp.where(lane >= 2 * EDGE * j, turned(tails[j], 2 * EDGE * j, 1), tile)
+    return tile
+
+
+def spread(tile, j):
+    tail = turned(tile, -2 * EDGE * j, 1)
+    return jnp.where(lanes(tile.shape[0]) < HALF, tail, turned(tail, -2 * EDGE, 1))
+
+
+def split_kernel(head_hbm, soil_hbm, out_ref, head_ref, soil_ref, sems):
+    copies = [
+        pltpu.make_async_copy(head_hbm, head_ref, sems.at[0]),
+        pltpu.make_async_copy(soil_hbm, soil_ref, sems.at[1]),
+    ]
+    for copy in copies:
+        copy.start()
+    whole = SECTIONS * OWN_COLS
+    for part, ref in enumerate((head_ref, soil_ref)):
+        copies[part].wait()
+        for target in range(SECTIONS):
+            start = target * OWN_COLS
+            after, before = (start + OWN_COLS) % whole, (start - 128) % whole
+            tails = []
+            for q in range(LZ):
+                field = ref[q].astype(F32)
+                out_ref[target, part * LZ + q] = field[:, start : start + OWN_COLS]
+                tails.append(tail_of(field[:, after : after + 128], field[:, before : before + 128]))
+            out_ref[target, 2 * LZ, :, 128 * part : 128 * part + 128] = grouped(tails)
+
+
+def edges_kernel(mid_ref, rain_ref, low_ref, high_ref, rain_out_ref):
     section = lax.axis_index("sec")
-    low_half = lax.broadcasted_iota(jnp.int32, (OWN_ROWS, 128), 1) < HALF
-    rain_step = jnp.minimum(section, 2)
-    for target in range(SECTIONS):
-        start = target * OWN_COLS
-        after = (start + OWN_COLS) % (SECTIONS * OWN_COLS)
-        before = (start - 128) % (SECTIONS * OWN_COLS)
-
-        def put(slot, read):
-            out_ref[target, slot, :, 0:OWN_COLS] = read(start, OWN_COLS)
-            out_ref[target, slot, :, OWN_COLS:WIDE] = jnp.where(low_half, read(after, 128), read(before, 128))
-
-        for q in range(LZ):
-            put(q, lambda at, n: head_ref[q, :, at : at + n])
-            put(LZ + q, lambda at, n: soil_ref[q, :, at : at + n].astype(F32))
-        put(2 * LZ, lambda at, n: rain_ref[rain_step, :, at : at + n])
+    start = pl.multiple_of(section * OWN_COLS, OWN_COLS)
+    after = pl.multiple_of(lax.rem(section + 1, SECTIONS) * OWN_COLS, OWN_COLS)
+    before = pl.multiple_of(lax.rem(section + SECTIONS - 1, SECTIONS) * OWN_COLS + 128, 128)
+    tails = []
+    for c in range(3):
+        rain_out_ref[c] = rain_ref[c, :, pl.ds(start, OWN_COLS)]
+        tails.append(tail_of(rain_ref[c, :, pl.ds(after, 128)], rain_ref[c, :, pl.ds(before, 128)]))
+    rain_out_ref[3] = jnp.concatenate([grouped(tails), jnp.zeros((OWN_ROWS, 128), F32)], axis=1)
+    for slot in range(SLOTS):
+        field = mid_ref[slot // 9, slot % 9] if slot < 36 else rain_out_ref[slot - 36]
+        low_ref[LOW * slot : LOW * slot + LOW, :] = field[OWN_ROWS - LOW :]
+        high_ref[HIGH * slot : HIGH * slot + HIGH, :] = field[:HIGH]
 
 
 def weights(sums_ref):
@@ -121,8 +167,8 @@
     work = slice(w0 - r0, w1 - r0)
     own = OWN_ROWS - w0
     if first:
-        (low_ref, mid_ref, high_ref, tables_ref, head_ref, cond_ref, store_ref, rain_ref) = refs[:8]
-        refs = refs[8:]
+        (low_ref, mid_ref, high_ref, rain_own_ref, tables_ref, head_ref, cond_ref, store_ref, rain_ref) = refs[:9]
+        refs = refs[9:]
     else:
         old = slice(r0 - SPANS[step - 1][0], r1 - SPANS[step - 1][0])
         old_work = slice(r0 - WORK[step - 1][0], r1 - WORK[step - 1][0])
@@ -136,10 +182,29 @@
     section, band = lax.axis_index("sec"), lax.axis_index("gx")
 
     if first:
-        for s in range(3):
-            rain_ref[s, 0:16, :] = low_ref[s, 8]
-            rain_ref[s, 16:32, :] = mid_ref[s, 8]
-            rain_ref[s, 32:48, :] = high_ref[s, 8]
+
+        def unpack(to, slot, halo, tile, group):
+            to[0:8, :] = jnp.zeros((8, WIDE), F32)
+            to[FRAME - 8 : FRAME, :] = jnp.zeros((8, WIDE), F32)
+
+            def own(slot, cols):
+                return mid_ref[slot // 9, slot % 9, :, cols] if slot < 36 else rain_own_ref[slot - 36, :, cols]
+
+            tile = slice(128 * tile, 128 * tile + 128)
+            third = slice(OWN_COLS, WIDE)
+            full = slice(0, OWN_COLS)
+            at = slice(OWN_ROWS - LOW, OWN_ROWS)
+            to[at, full] = low_ref[LOW * slot : LOW * slot + LOW, :]
+            to[at, third] = spread(low_ref[LOW * halo : LOW * halo + LOW, tile], group)
+            at = slice(OWN_ROWS, 2 * OWN_ROWS)
+            to[at, full] = own(slot, full)
+            to[at, third] = spread(own(halo, tile), group)
+            at = slice(2 * OWN_ROWS, 2 * OWN_ROWS + HIGH)
+            to[at, full] = high_ref[HIGH * slot : HIGH * slot + HIGH, :]
+            to[at, third] = spread(high_ref[HIGH * halo : HIGH * halo + HIGH, tile], group)
+
+        for c in range(3):
+            unpack(rain_ref.at[c], 36 + c, 39, 0, c)
     else:
         change = weights(sums_ref)
 
@@ -148,12 +213,11 @@
         for q in range(LZ):
             l = s * LZ + q
             if first:
-                for part, ref in enumerate((low_ref, mid_ref, high_ref)):
-                    at = slice(16 * part, 16 * part + 16)
-                    kinds = ref[s, LZ + q].astype(jnp.int32)
-                    head_ref[l, at, :] = ref[s, q]
-                    cond_ref[l, at, :] = gather(tables_ref[0], kinds)
-                    store_ref[l, at, :] = gather(tables_ref[1], kinds)
+                unpack(head_ref.at[l], 9 * s + q, 9 * s + 8, 0, q)
+                unpack(cond_ref.at[l], 9 * s + LZ + q, 9 * s + 8, 1, q)
+                kinds = cond_ref[l].astype(jnp.int32)
+                cond_ref[l] = gather(tables_ref[0], kinds)
+                store_ref[l] = gather(tables_ref[1], kinds)
                 h = head_ref[l]
             else:
                 h = old_head_ref[l, old, :]
@@ -186,9 +250,6 @@
     row_gate = jnp.where((row >= 1) & (row < n_rows_all), 2.0, 0.0).astype(F32)
     kept = slice(own, own + OWN_ROWS)
     none = jnp.zeros((OWN_ROWS, OWN_COLS), F32)
-
-    def turned(x, by, axis):
-        return pltpu.roll(x, by % x.shape[axis], axis)
 
     def faces(l, carry):
         acc, up = carry
@@ -290,16 +351,31 @@
     return pltpu.VMEM(dims, F32)
 
 
-def call(kernel, operands, outs, scratch=(), held=()):
-    operands = [pltpu.with_memory_space_constraint(x, pltpu.VMEM) if i in held else x for i, x in enumerate(operands)]
+def held(*arrays, space=pltpu.VMEM):
+    return tuple(pltpu.with_memory_space_constraint(x, space) for x in arrays)
+
+
+def call(kernel, operands, outs, scratch=(), in_specs=None, out_specs=None):
     return pl.pallas_call(
         kernel,
         out_shape=outs,
-        in_specs=[VMEM] * len(operands),
-        out_specs=jax.tree.map(lambda _: VMEM, outs),
-        scratch_shapes=[pltpu.VMEM(dims, F32) for dims in scratch],
+        in_specs=in_specs or [VMEM] * len(operands),
+        out_specs=out_specs or jax.tree.map(lambda _: VMEM, outs),
+        scratch_shapes=[pltpu.VMEM(dims, F32) if isinstance(dims, tuple) else dims for dims in scratch],
         compiler_params=params(),
     )(*operands)
+
+
+def join_kernel(parts_ref, head_hbm, flows_hbm, sems):
+    copies = []
+    for t in range(SECTIONS):
+        cols = slice(t * OWN_COLS, (t + 1) * OWN_COLS)
+        copies.append(pltpu.make_async_copy(parts_ref.at[t, 0:LZ], head_hbm.at[:, :, cols], sems.at[0, t]))
+        copies.append(pltpu.make_async_copy(parts_ref.at[t, LZ : LZ + 3], flows_hbm.at[0, :, :, cols], sems.at[1, t]))
+    for copy in copies:
+        copy.start()
+    for copy in copies:
+        copy.wait()
 
 
 def add_up(moments):
@@ -309,10 +385,23 @@
 def body(pressure_start, soil_type, saturated_conductivity, storage_coefficient, rainfall):
     bands = lax.axis_size("gx")
     devices = SECTIONS * bands
-    packed = call(pack_kernel, (pressure_start, soil_type, rainfall), shape(SECTIONS, 9, OWN_ROWS, WIDE))
+    outside = pl.BlockSpec(memory_space=pl.ANY)
+    block = (LZ, OWN_ROWS, SECTIONS * OWN_COLS)
+    packed = call(
+        split_kernel,
+        held(pressure_start, soil_type, space=pltpu.HBM),
+        near(SECTIONS, 9, OWN_ROWS, OWN_COLS),
+        (block, pltpu.VMEM(block, jnp.int32), pltpu.SemaphoreType.DMA((2,))),
+        in_specs=[outside] * 2,
+    )
     mid = lax.all_to_all(packed, "sec", 0, 0, tiled=True)
-    low = lax.ppermute(mid, "gx", [(i, i + 1) for i in range(bands - 1)])
-    high = lax.ppermute(mid, "gx", [(i + 1, i) for i in range(bands - 1)])
+    to_low, to_high, rain_own = call(
+        edges_kernel,
+        held(mid, rainfall),
+        [near(LOW * SLOTS, OWN_COLS), near(HIGH * SLOTS, OWN_COLS), near(4, OWN_ROWS, OWN_COLS)],
+    )
+    low = lax.ppermute(to_low, "gx", [(i, i + 1) for i in range(bands - 1)])
+    high = lax.ppermute(to_high, "gx", [(i + 1, i) for i in range(bands - 1)])
     tables = jnp.stack([saturated_conductivity, storage_coefficient])
     tables = jnp.broadcast_to(jnp.pad(tables, ((0, 0), (0, 128 - tables.shape[1])))[:, None, :], (2, 8, 128))
     inflows = []
@@ -328,18 +417,23 @@
         scratch = [field, field, (NZ, OWN_ROWS, OWN_COLS)] + [basis] * 6 + [(SECTIONS, rows, WIDE)] * 2 + [(SECTIONS + 1, rows, WIDE)]
         if step == 0:
             outs = [near(*field), near(*wide), near(*wide), near(3, FRAME, WIDE)] + [near(*basis)] * 4
-            got = call(kernel, (low, mid, high, tables), outs + tail, scratch, (0, 1, 2))
+            got = call(kernel, (*held(low, mid, high, rain_own), tables), outs + tail, scratch)
             head, cond, store, rain = got[:4]
             v = got[4:8]
         else:
-            got = call(kernel, (sums, head, *v, cond, store, rain), outs + tail, scratch, range(1, 9))
+            got = call(kernel, (sums, *held(head, *v, cond, store, rain)), outs + tail, scratch)
             head, v = got[0], got[1:5]
         inflows.append(got[-2])
         sums = add_up(got[-1])
-    out = call(last_kernel, (sums, head, *v, *inflows), shape(SECTIONS, 7, OWN_ROWS, OWN_COLS), (), range(1, 9))
+    out = call(last_kernel, (sums, *held(head, *v, *inflows)), near(SECTIONS, 7, OWN_ROWS, OWN_COLS))
     out = lax.all_to_all(out, "sec", 0, 0, tiled=True)
-    out = jnp.transpose(out, (1, 2, 0, 3)).reshape(7, OWN_ROWS, SECTIONS * OWN_COLS)
-    return out[:LZ], out[LZ:][None]
+    return call(
+        join_kernel,
+        held(out),
+        [shape(*block), shape(1, 3, *block[1:])],
+        (pltpu.SemaphoreType.DMA((2, SECTIONS)),),
+        out_specs=[outside] * 2,
+    )
 
 
 def solution(mesh):

time: 134 us -> 130 us (0.970)
  Pallas kernels: 19.3 us -> 26.8 us
  blocking collectives: 91.8 us -> 86.1 us
  local copies, waits for them, and re-layouts: 4.5 us -> 0.02 us
  waiting for transfers between devices: 9.93 us -> 8.19 us
    pallas_call x5 -> x7, Pallas kernels: 19.3 us -> 26.8 us  [call(): pl.pallas_call(kernel, out_shape=outs, in_specs=in_specs or [VMEM] * len(...]
    all_to_all x1, blocking collectives: 17.2 us -> 13.8 us  [body(): mid = lax.all_to_all(packed, 'sec', 0, 0, tiled=True)]
    unnamed x11 -> x6, local copies, waits for them, and re-layouts: 2.85 us -> 0.02 us
    all_to_all x3, blocking collectives: 64.2 us -> 62 us  [add_up(): return lax.all_to_all(moments, ('sec', 'gx'), 0, 0, tiled=True)]
    ppermute x2, waiting for transfers between devices: 9.93 us -> 8.19 us  [the longest x1 8.18 us: body(): high = lax.ppermute(to_high, 'gx', [(i + 1, i) for i in range(bands - 1)])]
  transfers between devices with their start and end apart: 2 -> 2, of which waited for: 2 -> 1; matrix products, arithmetic and copies ran while one was open for 0% -> 0% of each run, Pallas kernels for 0% -> 0%
where the time goes in v4:
time: 130 us
  blocking collectives  86.1 us (66%)
  Pallas kernels  26.8 us (21%)
  waiting for transfers between devices  8.19 us (6%)
  starting transfers between devices  7.5 us (6%)
    all_to_all x3, blocking collectives, add_up(): return lax.all_to_all(moments, ('sec', 'gx'), 0, 0, tiled=True)  62 us
    pallas_call x7, Pallas kernels, call(): pl.pallas_call(kernel, out_shape=outs, in_specs=in_specs or [VMEM] * len(...  26.8 us
    all_to_all x1, blocking collectives, body(): mid = lax.all_to_all(packed, 'sec', 0, 0, tiled=True)  13.8 us
    all_to_all x1, blocking collectives, body(): out = lax.all_to_all(out, 'sec', 0, 0, tiled=True)  10.3 us
    ppermute x1, waiting for transfers between devices, body(): high = lax.ppermute(to_high, 'gx', [(i + 1, i) for i in range(bands - 1)])  8.18 us
    ppermute x1, starting transfers between devices, body(): low = lax.ppermute(to_low, 'gx', [(i, i + 1) for i in range(bands - 1)])  5.58 us
  transfers between devices with their start and end apart: 2, of which 1 were waited for; matrix products, arithmetic and copies ran while one was open for 0% of the time, Pallas kernels for 0%

profile of v4, /device:TPU:1, one launch (start us, length us, event | category | flops | bytes accessed | tf_op | source)
XLA Modules:
  0.0 129.6 jit_solution(4397624589410013624)
XLA Ops:
  0.6 0.0 copy-start
  0.6 1.4 %shard_map.68 = f32[4,9,16,256]{3,2,1,0:T(8,128)S(1)} custom-call(f32[4,16,1024]{2,1,0:T(8,128)} %head_hbm.1, s32[4,16,1024]{2,1,0:T(8,128)} %soil_hbm.1), custom_call_target="tpu_custom_call" | custom-call | tf_op jit(solution)/shard_map/pallas_call | solution.py:359
  2.0 0.0 copy-start.1
  2.0 0.0 copy-start.2
  2.0 13.8 %all_to_all.43.mid_ref.refs_1_ = f32[4,9,16,256]{3,2,1,0:T(8,128)S(1)} all-to-all(f32[4,9,16,256]{3,2,1,0:T(8,128)S(1)} %shard_map.68), channel_id=1, replica_groups=mesh['sec'=4,'gx'=64] {'sec'}, dimensions={0} | all-to-all | bytes 1179648 | tf_op jit(solution)/shard_map/all_to_all | solution.py:397
  15.8 0.0 copy-done
  15.8 0.2 shard_map.69
  16.0 5.6 %collective-permute-start = (f32[520,256]{1,0:T(8,128)S(1)}, f32[520,256]{1,0:T(8,128)S(1)}, u32[]{:S(2)}, u32[]{:S(2)}) collective-permute-start(f32[520,256]{1,0:T(8,128)S(1)} %get-tuple-element.29), channel_id=1, source_target_pairs={{0,1},{1,2},{2,3},{3,4},{4,5},{5,6},{6,7},{7,8},{8,9},{9,10},{10,1... | collective-permute-start | bytes 1597448 | tf_op jit(solution)/shard_map/ppermute | solution.py:403
  21.6 1.9 %collective-permute-start.1 = (f32[480,256]{1,0:T(8,128)S(1)}, f32[480,256]{1,0:T(8,128)S(1)}, u32[]{:S(2)}, u32[]{:S(2)}) collective-permute-start(f32[480,256]{1,0:T(8,128)S(1)} %get-tuple-element.30), channel_id=1, source_target_pairs={{1,0},{2,1},{3,2},{4,3},{5,4},{6,5},{7,6},{8,7},{9,8},{10,9},{11,1... | collective-permute-start | bytes 1474568 | tf_op jit(solution)/shard_map/ppermute | solution.py:404
  23.5 0.0 copy-done.1
  23.5 0.0 copy-done.2
  23.6 8.2 %collective-permute-done.1.refs_2_ = f32[480,256]{1,0:T(8,128)S(1)} collective-permute-done((f32[480,256]{1,0:T(8,128)S(1)}, f32[480,256]{1,0:T(8,128)S(1)}, u32[]{:S(2)}, u32[]{:S(2)}) %collective-permute-start.1) | collective-permute-done | bytes 491552 | tf_op jit(solution)/shard_map/ppermute | solution.py:404
  31.8 0.0 collective-permute-done.refs_0_
  31.8 13.6 %shard_map.70 = (f32[16,48,384]{2,1,0:T(8,128)S(1)}, f32[16,48,384]{2,1,0:T(8,128)S(1)}, f32[16,48,384]{2,1,0:T(8,128)S(1)}, f32[3,48,384]{2,1,0:T(8,128)S(1)}, ...) custom-call(f32[520,256]{1,0:T(8,128)S(1)} %collective-permute-done., ...), custom_call_target="tpu_custom_call" | custom-call | tf_op jit(solution)/shard_map/pallas_call | solution.py:359
  45.3 24.8 %all_to_all.44 = f32[256,1,128]{2,1,0:T(1,128)S(1)} all-to-all(f32[256,1,128]{2,1,0:T(1,128)S(1)} %bitcast.18), channel_id=1, replica_groups=mesh['sec'=4,'gx'=64] {'sec','gx'}, dimensions={0} | all-to-all | bytes 262144 | tf_op jit(solution)/shard_map/all_to_all | solution.py:382
  70.1 5.3 %shard_map.71 = (f32[16,40,384]{2,1,0:T(8,128)S(1)}, f32[16,32,384]{2,1,0:T(8,128)S(1)}, f32[16,32,384]{2,1,0:T(8,128)S(1)}, f32[16,32,384]{2,1,0:T(8,128)S(1)},...) custom-call(f32[256,128]{1,0:T(8,128)S(1)} %bitcast.14, ...), custom_call_target="tpu_custom_call" | custom-call | tf_op jit(solution)/shard_map/pallas_call | solution.py:359
  75.4 18.6 %all_to_all.45 = f32[256,1,128]{2,1,0:T(1,128)S(1)} all-to-all(f32[256,1,128]{2,1,0:T(1,128)S(1)} %bitcast.19), channel_id=1, replica_groups=mesh['sec'=4,'gx'=64] {'sec','gx'}, dimensions={0} | all-to-all | bytes 262144 | tf_op jit(solution)/shard_map/all_to_all | solution.py:382
  94.1 5.3 %shard_map.72 = (f32[16,32,384]{2,1,0:T(8,128)S(1)}, f32[16,32,384]{2,1,0:T(8,128)S(1)}, f32[16,32,384]{2,1,0:T(8,128)S(1)}, f32[16,32,384]{2,1,0:T(8,128)S(1)},...) custom-call(f32[256,128]{1,0:T(8,128)S(1)} %bitcast.16, ...), custom_call_target="tpu_custom_call" | custom-call | tf_op jit(solution)/shard_map/pallas_call | solution.py:359
  99.4 18.6 %all_to_all.46 = f32[256,1,128]{2,1,0:T(1,128)S(1)} all-to-all(f32[256,1,128]{2,1,0:T(1,128)S(1)} %bitcast.17), channel_id=1, replica_groups=mesh['sec'=4,'gx'=64] {'sec','gx'}, dimensions={0} | all-to-all | bytes 262144 | tf_op jit(solution)/shard_map/all_to_all | solution.py:382
  118.0 0.3 shard_map.73
  118.3 10.3 %all_to_all.47.parts_ref = f32[4,7,16,256]{3,2,1,0:T(8,128)S(1)} all-to-all(f32[4,7,16,256]{3,2,1,0:T(8,128)S(1)} %shard_map.73), channel_id=1, replica_groups=mesh['sec'=4,'gx'=64] {'sec'}, dimensions={0} | all-to-all | bytes 917504 | tf_op jit(solution)/shard_map/all_to_all | solution.py:429
  128.6 0.8 shard_map.74
  (2 shorter events, 0.0 us)
Async XLA Ops:
  0.6 15.2 %copy-start = (f32[3,16,1024]{2,1,0:T(8,128)S(1)}, f32[3,16,1024]{2,1,0:T(8,128)}, u32[]{:S(2)}) copy-start(f32[3,16,1024]{2,1,0:T(8,128)} %rain_ref.1) | copy-start | bytes 589828
  2.0 21.5 %copy-start.1 = (f32[12]{0:T(128)S(1)}, f32[12]{0:T(128)}, u32[]{:S(2)}) copy-start(f32[12]{0:T(128)} %param.8) | copy-start | bytes 148
  2.0 21.5 %copy-start.2 = (f32[12]{0:T(128)S(1)}, f32[12]{0:T(128)}, u32[]{:S(2)}) copy-start(f32[12]{0:T(128)} %param.7) | copy-start | bytes 148
  16.0 15.7 %collective-permute-start = (f32[520,256]{1,0:T(8,128)S(1)}, f32[520,256]{1,0:T(8,128)S(1)}, u32[]{:S(2)}, u32[]{:S(2)}) collective-permute-start(f32[520,256]{1,0:T(8,128)S(1)} %get-tuple-element.29), channel_id=1, source_target_pairs={{0,1},{1,2},{2,3},{3,4},{4,5},{5,6},{6,7},{7,8},{8,9},{9,10},{10,1... | collective-permute-start | bytes 1597448 | tf_op jit(solution)/shard_map/ppermute | solution.py:403
  21.6 10.1 %collective-permute-start.1 = (f32[480,256]{1,0:T(8,128)S(1)}, f32[480,256]{1,0:T(8,128)S(1)}, u32[]{:S(2)}, u32[]{:S(2)}) collective-permute-start(f32[480,256]{1,0:T(8,128)S(1)} %get-tuple-element.30), channel_id=1, source_target_pairs={{1,0},{2,1},{3,2},{4,3},{5,4},{6,5},{7,6},{8,7},{9,8},{10,9},{11,1... | collective-permute-start | bytes 1474568 | tf_op jit(solution)/shard_map/ppermute | solution.py:404

commit v5 on v4

--- a/solution.py
+++ b/solution.py
@@ -17,7 +17,6 @@
 HALF = 64
 EDGE = 16
 FRAME = 48
-LOW, HIGH = 13, 12
 SLOTS = 40
 SPANS = ((0, 48), (0, 40), (8, 40))
 WORK = ((0, 48), (8, 40), (8, 40))
@@ -49,9 +48,11 @@
     return tile
 
 
-def spread(tile, j):
-    tail = turned(tile, -2 * EDGE * j, 1)
-    return jnp.where(lanes(tile.shape[0]) < HALF, tail, turned(tail, -2 * EDGE, 1))
+def spread(tile, count):
+    for _ in range(count):
+        later = turned(tile, -2 * EDGE, 1)
+        yield jnp.where(lanes(tile.shape[0]) < HALF, tile, later)
+        tile = later
 
 
 def split_kernel(head_hbm, soil_hbm, out_ref, head_ref, soil_ref, sems):
@@ -75,20 +76,18 @@
             out_ref[target, 2 * LZ, :, 128 * part : 128 * part + 128] = grouped(tails)
 
 
-def edges_kernel(mid_ref, rain_ref, low_ref, high_ref, rain_out_ref):
+def edges_kernel(mid_ref, rain_ref, out_ref):
     section = lax.axis_index("sec")
     start = pl.multiple_of(section * OWN_COLS, OWN_COLS)
     after = pl.multiple_of(lax.rem(section + 1, SECTIONS) * OWN_COLS, OWN_COLS)
     before = pl.multiple_of(lax.rem(section + SECTIONS - 1, SECTIONS) * OWN_COLS + 128, 128)
     tails = []
     for c in range(3):
-        rain_out_ref[c] = rain_ref[c, :, pl.ds(start, OWN_COLS)]
+        out_ref[36 + c] = rain_ref[c, :, pl.ds(start, OWN_COLS)]
         tails.append(tail_of(rain_ref[c, :, pl.ds(after, 128)], rain_ref[c, :, pl.ds(before, 128)]))
-    rain_out_ref[3] = jnp.concatenate([grouped(tails), jnp.zeros((OWN_ROWS, 128), F32)], axis=1)
-    for slot in range(SLOTS):
-        field = mid_ref[slot // 9, slot % 9] if slot < 36 else rain_out_ref[slot - 36]
-        low_ref[LOW * slot : LOW * slot + LOW, :] = field[OWN_ROWS - LOW :]
-        high_ref[HIGH * slot : HIGH * slot + HIGH, :] = field[:HIGH]
+    out_ref[39] = jnp.concatenate([grouped(tails), jnp.zeros((OWN_ROWS, 128), F32)], axis=1)
+    for slot in range(36):
+        out_ref[slot] = mid_ref[slot // 9, slot % 9]
 
 
 def weights(sums_ref):
@@ -158,6 +157,43 @@
     return jnp.concatenate(parts, axis=1)
 
 
+def enter_kernel(from_ref, tables_ref, head_ref, cond_ref, store_ref, res_ref, cap_ref, rain_ref, water_ref, low_cond_ref):
+    packs = [(rain_ref, 0, 36, 39, 0, 3)]
+    for s in range(SECTIONS):
+        packs.append((head_ref, s * LZ, 9 * s, 9 * s + 8, 0, LZ))
+        packs.append((cond_ref, s * LZ, 9 * s + LZ, 9 * s + 8, 1, LZ))
+    for ref, first, slot, halo, tile, count in packs:
+        for q, third in enumerate(spread(from_ref[halo, :, 128 * tile : 128 * tile + 128], count)):
+            ref[first + q, :, 0:OWN_COLS] = from_ref[slot + q]
+            ref[first + q, :, OWN_COLS:WIDE] = third
+    for l in range(NZ):
+        store_ref[l] = gather(tables_ref[1], cond_ref[l].astype(jnp.int32))
+    for l in range(NZ):
+        cond_ref[l] = gather(tables_ref[0], cond_ref[l].astype(jnp.int32))
+    for s in range(SECTIONS):
+        total = jnp.zeros((OWN_ROWS, WIDE), F32)
+        for q in range(LZ):
+            l = s * LZ + q
+            saturation, cond, capacity = setup_terms(head_ref[l], cond_ref[l], store_ref[l])
+            res_ref[l] = recip(cond)
+            cap_ref[l] = capacity
+            total = total + saturation
+        water_ref[s] = total
+        low_cond_ref[s] = 0.5 * cond
+
+
+def framed(parts, start, stop):
+    def read(l):
+        pieces = []
+        for at, ref in enumerate(parts):
+            lo, hi = max(start - 16 * at, 0), min(stop - 16 * at, 16)
+            if lo < hi:
+                pieces.append(ref[l, lo:hi, :])
+        return jnp.concatenate(pieces, axis=0)
+
+    return read
+
+
 def step_kernel(step, n_rows_all, *refs):
     first = step == 0
     r0, r1 = SPANS[step]
@@ -166,81 +202,67 @@
     span = w1 - w0
     work = slice(w0 - r0, w1 - r0)
     own = OWN_ROWS - w0
+    refs = list(refs)
+
+    def take(n):
+        taken, refs[:n] = refs[:n], []
+        return taken
+
+    def take_framed(n):
+        low, mid, high = take(n), take(n), take(n)
+        return [framed(parts, r0, r1) for parts in zip(low, mid, high)]
+
     if first:
-        (low_ref, mid_ref, high_ref, rain_own_ref, tables_ref, head_ref, cond_ref, store_ref, rain_ref) = refs[:9]
-        refs = refs[9:]
+        head, res, cap, rain, water, low_cond = take_framed(6)
     else:
-        old = slice(r0 - SPANS[step - 1][0], r1 - SPANS[step - 1][0])
+        (sums_ref,) = take(1)
+        old_basis = take(ITERS)
         old_work = slice(r0 - WORK[step - 1][0], r1 - WORK[step - 1][0])
-        (sums_ref, old_head_ref, o0, o1, o2, o3, cond_ref, store_ref, rain_ref, head_ref) = refs[:10]
-        old_basis = (o0, o1, o2, o3)
-        refs = refs[10:]
-    (v0, v1, v2, v3, inflow_ref, moments_ref) = refs[:6]
-    (res_ref, cap_ref, diag_ref, up_ref, dn_ref, ru_ref, rd_ref, xl_ref, xr_ref, water_ref, low_cond_ref, flux_ref) = refs[6:]
+        if step == 1:
+            old_head, cond_of, store_of, rain = take_framed(4)
+        else:
+            (old_head_ref,) = take(1)
+            old = slice(r0 - SPANS[step - 1][0], r1 - SPANS[step - 1][0])
+            old_head = lambda l: old_head_ref[l, old, :]
+            cond_of, store_of, rain = take_framed(3)
+        (head_ref,) = take(1)
+    v0, v1, v2, v3, inflow_ref, moments_ref = take(6)
+    diag_ref, up_ref, dn_ref, ru_ref, rd_ref, xl_ref, xr_ref, flux_ref = take(8)
+    if not first:
+        res_ref, cap_ref, water_ref, low_cond_ref = take(4)
+        head, res, cap, water, low_cond = [
+            (lambda l, ref=ref: ref[l]) for ref in (head_ref, res_ref, cap_ref, water_ref, low_cond_ref)
+        ]
     basis = (v0, v1, v2, v3)
-    here = slice(r0, r1)
-    section, band = lax.axis_index("sec"), lax.axis_index("gx")
-
-    if first:
-
-        def unpack(to, slot, halo, tile, group):
-            to[0:8, :] = jnp.zeros((8, WIDE), F32)
-            to[FRAME - 8 : FRAME, :] = jnp.zeros((8, WIDE), F32)
-
-            def own(slot, cols):
-                return mid_ref[slot // 9, slot % 9, :, cols] if slot < 36 else rain_own_ref[slot - 36, :, cols]
-
-            tile = slice(128 * tile, 128 * tile + 128)
-            third = slice(OWN_COLS, WIDE)
-            full = slice(0, OWN_COLS)
-            at = slice(OWN_ROWS - LOW, OWN_ROWS)
-            to[at, full] = low_ref[LOW * slot : LOW * slot + LOW, :]
-            to[at, third] = spread(low_ref[LOW * halo : LOW * halo + LOW, tile], group)
-            at = slice(OWN_ROWS, 2 * OWN_ROWS)
-            to[at, full] = own(slot, full)
-            to[at, third] = spread(own(halo, tile), group)
-            at = slice(2 * OWN_ROWS, 2 * OWN_ROWS + HIGH)
-            to[at, full] = high_ref[HIGH * slot : HIGH * slot + HIGH, :]
-            to[at, third] = spread(high_ref[HIGH * halo : HIGH * halo + HIGH, tile], group)
-
-        for c in range(3):
-            unpack(rain_ref.at[c], 36 + c, 39, 0, c)
-    else:
+    section = lax.axis_index("sec")
+    band = lax.axis_index("pair") * 2 + lax.axis_index("core")
+
+    if not first:
         change = weights(sums_ref)
-
-    for s in range(SECTIONS):
-        total = jnp.zeros((rows, WIDE), F32)
-        for q in range(LZ):
-            l = s * LZ + q
-            if first:
-                unpack(head_ref.at[l], 9 * s + q, 9 * s + 8, 0, q)
-                unpack(cond_ref.at[l], 9 * s + LZ + q, 9 * s + 8, 1, q)
-                kinds = cond_ref[l].astype(jnp.int32)
-                cond_ref[l] = gather(tables_ref[0], kinds)
-                store_ref[l] = gather(tables_ref[1], kinds)
-                h = head_ref[l]
-            else:
-                h = old_head_ref[l, old, :]
+        for s in range(SECTIONS):
+            total = jnp.zeros((rows, WIDE), F32)
+            for q in range(LZ):
+                l = s * LZ + q
+                h = old_head(l)
                 for c, o in zip(change, old_basis):
                     h = h + c * o[l, old_work, :]
                 head_ref[l] = h
-            saturation, cond, capacity = setup_terms(h, cond_ref[l, here, :], store_ref[l, here, :])
-            res_ref[l] = recip(cond)
-            cap_ref[l] = capacity
-            total = total + saturation
-            if q == LZ - 1:
-                low_cond_ref[s] = 0.5 * cond
-        water_ref[s] = total
-
-    flux_ref[0] = rain_ref[step, here, :]
+                saturation, cond, capacity = setup_terms(h, cond_of(l), store_of(l))
+                res_ref[l] = recip(cond)
+                cap_ref[l] = capacity
+                total = total + saturation
+            water_ref[s] = total
+            low_cond_ref[s] = 0.5 * cond
+
+    flux_ref[0] = rain(step)
     belows = [None] * SECTIONS
     below = None
     for s in reversed(range(SECTIONS)):
         belows[s] = below
-        below = water_ref[s] if below is None else below + water_ref[s]
+        below = water(s) if below is None else below + water(s)
     for s in range(SECTIONS):
         scale = 0.5 if belows[s] is None else 0.5 + 0.5 * belows[s] / (belows[s] + 4.0)
-        flux_ref[s + 1] = water_ref[s] * 0.25 * scale * flux_ref[s] + low_cond_ref[s]
+        flux_ref[s + 1] = water(s) * 0.25 * scale * flux_ref[s] + low_cond(s)
         inflow_ref[s] = flux_ref[s, OWN_ROWS - r0 : 2 * OWN_ROWS - r0, 0:OWN_COLS]
 
     lane = lax.broadcasted_iota(jnp.int32, (span, WIDE), 1)
@@ -253,17 +275,17 @@
 
     def faces(l, carry):
         acc, up = carry
-        res = res_ref[l, work, :]
-        h = head_ref[l, work, :]
+        around, tops = res(l), head(l)
+        mine, h = around[work], tops[work]
         if l + 1 < NZ:
-            dn = 2.0 * recip(res + res_ref[l + 1, work, :])
+            dn = 2.0 * recip(mine + res(l + 1)[work])
         else:
-            dn = jnp.zeros_like(res)
-        ru = row_gate * recip(res + turned(res_ref[l], 1, 0)[work])
+            dn = jnp.zeros_like(mine)
+        ru = row_gate * recip(mine + turned(around, 1, 0)[work])
         rd = turned(ru, -1, 0)
-        xl = col_gate * recip(res + turned(res, 1, 1))
+        xl = col_gate * recip(mine + turned(mine, 1, 1))
         xr = turned(xl, -1, 1)
-        diag = cap_ref[l, work, :] + up + dn + ru + rd + xl + xr
+        diag = cap(l)[work] + up + dn + ru + rd + xl + xr
         inv = recip(diag)
         r = up - dn
         if l % LZ == 0:
@@ -271,10 +293,10 @@
         if l % LZ == LZ - 1:
             r = r - flux_ref[l // LZ + 1, work, :]
         if l > 0:
-            r = r + up * (head_ref[l - 1, work, :] - h)
+            r = r + up * (head(l - 1)[work] - h)
         if l + 1 < NZ:
-            r = r + dn * (head_ref[l + 1, work, :] - h)
-        r = r + ru * (turned(head_ref[l], 1, 0)[work] - h) + rd * (turned(head_ref[l], -1, 0)[work] - h)
+            r = r + dn * (head(l + 1)[work] - h)
+        r = r + ru * (turned(tops, 1, 0)[work] - h) + rd * (turned(tops, -1, 0)[work] - h)
         r = r + xl * (turned(h, 1, 1) - h) + xr * (turned(h, -1, 1) - h)
         z = r * inv
         v0[l] = z
@@ -325,8 +347,7 @@
     for k, acc in enumerate(moments):
         value = jnp.sum(jnp.sum(acc, axis=0, keepdims=True), axis=1, keepdims=True)
         line = jnp.where(spot == k, value, line)
-    for i in range(moments_ref.shape[0] // 8):
-        moments_ref[8 * i : 8 * i + 8, :] = line
+    moments_ref[...] = line
 
 
 def last_kernel(sums_ref, head_ref, v0, v1, v2, v3, i0, i1, i2, out_ref):
@@ -355,9 +376,10 @@
     return tuple(pltpu.with_memory_space_constraint(x, space) for x in arrays)
 
 
-def call(kernel, operands, outs, scratch=(), in_specs=None, out_specs=None):
+def call(kernel, operands, outs, scratch=(), in_specs=None, out_specs=None, **more):
     return pl.pallas_call(
         kernel,
+        **more,
         out_shape=outs,
         in_specs=in_specs or [VMEM] * len(operands),
         out_specs=out_specs or jax.tree.map(lambda _: VMEM, outs),
@@ -379,12 +401,15 @@
 
 
 def add_up(moments):
-    return lax.all_to_all(moments, ("sec", "gx"), 0, 0, tiled=True)
+    chips = SECTIONS * lax.axis_size("pair")
+    both = moments + lax.ppermute(moments, "core", [(0, 1), (1, 0)])
+    rows = lax.all_to_all(jnp.broadcast_to(both[:1, None], (chips, 1, 128)), ("sec", "pair"), 0, 0, tiled=True)
+    return rows.reshape(chips, 128)
 
 
 def body(pressure_start, soil_type, saturated_conductivity, storage_coefficient, rainfall):
-    bands = lax.axis_size("gx")
-    devices = SECTIONS * bands
+    gx = ("pair", "core")
+    bands = 2 * lax.axis_size("pair")
     outside = pl.BlockSpec(memory_space=pl.ANY)
     block = (LZ, OWN_ROWS, SECTIONS * OWN_COLS)
     packed = call(
@@ -395,33 +420,42 @@
         in_specs=[outside] * 2,
     )
     mid = lax.all_to_all(packed, "sec", 0, 0, tiled=True)
-    to_low, to_high, rain_own = call(
-        edges_kernel,
-        held(mid, rainfall),
-        [near(LOW * SLOTS, OWN_COLS), near(HIGH * SLOTS, OWN_COLS), near(4, OWN_ROWS, OWN_COLS)],
-    )
-    low = lax.ppermute(to_low, "gx", [(i, i + 1) for i in range(bands - 1)])
-    high = lax.ppermute(to_high, "gx", [(i + 1, i) for i in range(bands - 1)])
+    to_send = call(edges_kernel, held(mid, rainfall), near(SLOTS, OWN_ROWS, OWN_COLS))
+    low = lax.ppermute(to_send, gx, [(i, i + 1) for i in range(bands - 1)])
+    high = lax.ppermute(to_send, gx, [(i + 1, i) for i in range(bands - 1)])
     tables = jnp.stack([saturated_conductivity, storage_coefficient])
     tables = jnp.broadcast_to(jnp.pad(tables, ((0, 0), (0, 128 - tables.shape[1])))[:, None, :], (2, 8, 128))
+
+    def entered(rows_sent):
+        return call(
+            enter_kernel,
+            (*held(rows_sent), tables),
+            [near(n, OWN_ROWS, WIDE) for n in (NZ,) * 5 + (3,) + (SECTIONS,) * 2],
+            cost_estimate=pl.CostEstimate(flops=10_000_000, bytes_accessed=4_000_000, transcendentals=300_000),
+        )
+
+    parts = [entered(low), entered(to_send), entered(high)]
+
+    def pick(*which):
+        return [part[k] for part in parts for k in which]
+
     inflows = []
     state = None
     for step, (r0, r1) in enumerate(SPANS):
         rows = r1 - r0
         field = (NZ, rows, WIDE)
         basis = (NZ, WORK[step][1] - WORK[step][0], WIDE)
-        wide = (NZ, FRAME, WIDE)
         outs = [near(*field)] + [near(*basis)] * 4
         kernel = functools.partial(step_kernel, step, bands * OWN_ROWS)
-        tail = [near(SECTIONS, OWN_ROWS, OWN_COLS), shape(devices, 128)]
-        scratch = [field, field, (NZ, OWN_ROWS, OWN_COLS)] + [basis] * 6 + [(SECTIONS, rows, WIDE)] * 2 + [(SECTIONS + 1, rows, WIDE)]
+        tail = [near(SECTIONS, OWN_ROWS, OWN_COLS), near(8, 128)]
+        scratch = [(NZ, OWN_ROWS, OWN_COLS)] + [basis] * 6 + [(SECTIONS + 1, rows, WIDE)]
         if step == 0:
-            outs = [near(*field), near(*wide), near(*wide), near(3, FRAME, WIDE)] + [near(*basis)] * 4
-            got = call(kernel, (*held(low, mid, high, rain_own), tables), outs + tail, scratch)
-            head, cond, store, rain = got[:4]
-            v = got[4:8]
+            got = call(kernel, held(*pick(0, 3, 4, 5, 6, 7)), [near(*basis)] * 4 + tail, scratch)
+            v = got[:4]
         else:
-            got = call(kernel, (sums, *held(head, *v, cond, store, rain)), outs + tail, scratch)
+            state = pick(0, 1, 2, 5) if step == 1 else [head, *pick(1, 2, 5)]
+            soil = [field] * 2 + [(SECTIONS, rows, WIDE)] * 2
+            got = call(kernel, (sums, *held(*v, *state)), outs + tail, scratch + soil)
             head, v = got[0], got[1:5]
         inflows.append(got[-2])
         sums = add_up(got[-1])
@@ -437,11 +471,13 @@
 
 
 def solution(mesh):
-    placed = (P("sec", "gx", None), P("sec", "gx", None), P(), P(), P(None, "gx", None))
+    sections, bands = mesh.devices.shape
+    gx = ("pair", "core")
+    placed = (P("sec", gx, None), P("sec", gx, None), P(), P(), P(None, gx, None))
     return jax.shard_map(
         body,
-        mesh=mesh,
+        mesh=jax.sharding.Mesh(mesh.devices.reshape(sections, bands // 2, 2), ("sec", *gx)),
         in_specs=placed,
-        out_specs=(P("sec", "gx", None), P("sec", None, "gx", None)),
+        out_specs=(P("sec", gx, None), P("sec", None, gx, None)),
         check_vma=False,
     )

time: 130 us -> 125 us (0.962)
  blocking collectives: 86.1 us -> 78.9 us
  Pallas kernels: 26.8 us -> 21.8 us
  starting transfers between devices: 7.5 us -> 10.8 us
  waiting for transfers between devices: 8.19 us -> 11.3 us
    all_to_all x3, blocking collectives: 62 us -> 55.9 us  [add_up(): lax.all_to_all(jnp.broadcast_to(both[:1, None], (chips, 1, 128)), ('sec',...]
    pallas_call x7 -> x10, Pallas kernels: 26.8 us -> 21.8 us  [call(): pl.pallas_call(kernel, **more, out_shape=outs, in_specs=in_specs or [VMEM...]
    ppermute x2 -> x5, starting transfers between devices: 7.5 us -> 10.8 us  [the longest x1 5.58 us: body(): low = lax.ppermute(to_send, gx, [(i, i + 1) for i in range(bands - 1)])]
    ppermute x2 -> x5, waiting for transfers between devices: 8.19 us -> 11.3 us  [the longest x1 4.83 us: body(): low = lax.ppermute(to_send, gx, [(i, i + 1) for i in range(bands - 1)])]
  transfers between devices with their start and end apart: 2 -> 5, of which waited for: 1 -> 5; matrix products, arithmetic and copies ran while one was open for 0% -> 0% of each run, Pallas kernels for 0% -> 1%
where the time goes in v5:
time: 125 us; the launch traced here: 124 us
  blocking collectives  78.9 us (63%)
  Pallas kernels  21.8 us (17%)
  waiting for transfers between devices  11.3 us (9%)
  starting transfers between devices  10.8 us (9%)
    all_to_all x3, blocking collectives, add_up(): lax.all_to_all(jnp.broadcast_to(both[:1, None], (chips, 1, 128)), ('sec',...  55.9 us
    pallas_call x10, Pallas kernels, call(): pl.pallas_call(kernel, **more, out_shape=outs, in_specs=in_specs or [VMEM...  21.8 us
    all_to_all x1, blocking collectives, body(): mid = lax.all_to_all(packed, 'sec', 0, 0, tiled=True)  13.8 us
    all_to_all x1, blocking collectives, body(): out = lax.all_to_all(out, 'sec', 0, 0, tiled=True)  9.26 us
    ppermute x1, starting transfers between devices, body(): low = lax.ppermute(to_send, gx, [(i, i + 1) for i in range(bands - 1)])  5.58 us
    ppermute x1, waiting for transfers between devices, body(): low = lax.ppermute(to_send, gx, [(i, i + 1) for i in range(bands - 1)])  4.83 us
    ppermute x1, waiting for transfers between devices, body(): high = lax.ppermute(to_send, gx, [(i + 1, i) for i in range(bands - 1)])  3.69 us
    ppermute x3, starting transfers between devices, add_up(): both = moments + lax.ppermute(moments, 'core', [(0, 1), (1, 0)])  3.26 us
  transfers between devices with their start and end apart: 5, of which 5 were waited for; matrix products, arithmetic and copies ran while one was open for 0% of the time, Pallas kernels for 1%

profile of v5, /device:TPU:1, one launch (start us, length us, event | category | flops | bytes accessed | tf_op | source)
XLA Modules:
  0.0 123.9 jit_solution(31700025912307863)
XLA Ops:
  0.6 1.4 %shard_map.68 = f32[4,9,16,256]{3,2,1,0:T(8,128)S(1)} custom-call(f32[4,16,1024]{2,1,0:T(8,128)} %head_hbm.1, s32[4,16,1024]{2,1,0:T(8,128)} %soil_hbm.1), custom_call_target="tpu_custom_call" | custom-call | tf_op jit(solution)/shard_map/pallas_call | solution.py:380
  2.0 13.8 %all_to_all.25.mid_ref = f32[4,9,16,256]{3,2,1,0:T(8,128)S(1)} all-to-all(f32[4,9,16,256]{3,2,1,0:T(8,128)S(1)} %shard_map.68), channel_id=1, replica_groups=mesh['sec'=4,'pair'=32,'core'=2] {'sec'}, dimensions={0} | all-to-all | bytes 1179648 | tf_op jit(solution)/shard_map/all_to_all | solution.py:422
  15.8 0.2 shard_map.69.from_ref
  16.0 5.6 %collective-permute-start = (f32[40,16,256]{2,1,0:T(8,128)S(1)}, f32[40,16,256]{2,1,0:T(8,128)S(1)}, u32[]{:S(2)}, u32[]{:S(2)}) collective-permute-start(f32[40,16,256]{2,1,0:T(8,128)S(1)} %shard_map.69.from_ref), channel_id=1, source_target_pairs={{0,1},{1,2},{2,3},{3,4},{4,5},{5,6},{6,7},{7,8},{8,9},{9,10},{10,1... | collective-permute-start | bytes 1966088 | tf_op jit(solution)/shard_map/ppermute | solution.py:424
  21.6 1.9 %collective-permute-start.1 = (f32[40,16,256]{2,1,0:T(8,128)S(1)}, f32[40,16,256]{2,1,0:T(8,128)S(1)}, u32[]{:S(2)}, u32[]{:S(2)}) collective-permute-start(f32[40,16,256]{2,1,0:T(8,128)S(1)} %shard_map.69.from_ref), channel_id=1, source_target_pairs={{1,0},{2,1},{3,2},{4,3},{5,4},{6,5},{7,6},{8,7},{9,8},{10,9},{11,1... | collective-permute-start | bytes 1966088 | tf_op jit(solution)/shard_map/ppermute | solution.py:425
  23.6 0.7 shard_map.71
  24.3 4.8 %collective-permute-done.from_ref = f32[40,16,256]{2,1,0:T(8,128)S(1)} collective-permute-done((f32[40,16,256]{2,1,0:T(8,128)S(1)}, f32[40,16,256]{2,1,0:T(8,128)S(1)}, u32[]{:S(2)}, u32[]{:S(2)}) %collective-permute-start) | collective-permute-done | bytes 655392 | tf_op jit(solution)/shard_map/ppermute | solution.py:424
  29.1 0.7 shard_map.70
  29.8 3.7 %collective-permute-done.1.from_ref = f32[40,16,256]{2,1,0:T(8,128)S(1)} collective-permute-done((f32[40,16,256]{2,1,0:T(8,128)S(1)}, f32[40,16,256]{2,1,0:T(8,128)S(1)}, u32[]{:S(2)}, u32[]{:S(2)}) %collective-permute-start.1) | collective-permute-done | bytes 655392 | tf_op jit(solution)/shard_map/ppermute | solution.py:425
  33.5 0.7 shard_map.72
  34.2 6.7 %shard_map.73 = (f32[16,48,384]{2,1,0:T(8,128)S(1)}, f32[16,48,384]{2,1,0:T(8,128)S(1)}, f32[16,48,384]{2,1,0:T(8,128)S(1)}, f32[16,48,384]{2,1,0:T(8,128)S(1)},...) custom-call(f32[16,16,384]{2,1,0:T(8,128)S(1)} %get-tuple-element.46.refs_0_.refs_5_, ...), custom_call_target="tpu_custom_call" | custom-call | tf_op jit(solution)/shard_map/pallas_call | solution.py:380
  40.9 1.2 collective-permute-done.2
  42.1 23.7 %all_to_all.26 = f32[128,1,128]{2,1,0:T(1,128)S(1)} all-to-all(f32[128,1,128]{2,1,0:T(1,128)S(1)} %broadcast_in_dim.32), channel_id=1, replica_groups=mesh['sec'=4,'pair'=32,'core'=2] {'sec','pair'}, dimensions={0} | all-to-all | bytes 131072 | tf_op jit(solution)/shard_map/all_to_all | solution.py:406
  65.8 5.3 %shard_map.74 = (f32[16,40,384]{2,1,0:T(8,128)S(1)}, f32[16,32,384]{2,1,0:T(8,128)S(1)}, f32[16,32,384]{2,1,0:T(8,128)S(1)}, f32[16,32,384]{2,1,0:T(8,128)S(1)},...) custom-call(f32[128,128]{1,0:T(8,128)S(1)} %bitcast.12, ...), custom_call_target="tpu_custom_call" | custom-call | tf_op jit(solution)/shard_map/pallas_call | solution.py:380
  71.1 1.6 %collective-permute-start.3 = (f32[8,128]{1,0:T(8,128)S(1)}, f32[8,128]{1,0:T(8,128)S(1)}, u32[]{:S(2)}, u32[]{:S(2)}) collective-permute-start(f32[8,128]{1,0:T(8,128)S(1)} %get-tuple-element.75), channel_id=1, source_target_pairs={{0,1},{1,0},{2,3},{3,2},{4,5},{5,4},{6,7},{7,6},{8,9},{9,8},{10,11... | collective-permute-start | bytes 12296 | tf_op jit(solution)/shard_map/ppermute | solution.py:405
  72.7 0.8 collective-permute-done.3
  73.6 16.1 %all_to_all.27 = f32[128,1,128]{2,1,0:T(1,128)S(1)} all-to-all(f32[128,1,128]{2,1,0:T(1,128)S(1)} %broadcast_in_dim.34), channel_id=1, replica_groups=mesh['sec'=4,'pair'=32,'core'=2] {'sec','pair'}, dimensions={0} | all-to-all | bytes 131072 | tf_op jit(solution)/shard_map/all_to_all | solution.py:406
  89.7 5.1 %shard_map.75 = (f32[16,32,384]{2,1,0:T(8,128)S(1)}, f32[16,32,384]{2,1,0:T(8,128)S(1)}, f32[16,32,384]{2,1,0:T(8,128)S(1)}, f32[16,32,384]{2,1,0:T(8,128)S(1)},...) custom-call(f32[128,128]{1,0:T(8,128)S(1)} %bitcast.11, ...), custom_call_target="tpu_custom_call" | custom-call | tf_op jit(solution)/shard_map/pallas_call | solution.py:380
  94.8 1.6 %collective-permute-start.4 = (f32[8,128]{1,0:T(8,128)S(1)}, f32[8,128]{1,0:T(8,128)S(1)}, u32[]{:S(2)}, u32[]{:S(2)}) collective-permute-start(f32[8,128]{1,0:T(8,128)S(1)} %get-tuple-element.81), channel_id=1, source_target_pairs={{0,1},{1,0},{2,3},{3,2},{4,5},{5,4},{6,7},{7,6},{8,9},{9,8},{10,11... | collective-permute-start | bytes 12296 | tf_op jit(solution)/shard_map/ppermute | solution.py:405
  96.4 0.8 collective-permute-done.4
  97.3 16.1 %all_to_all.28 = f32[128,1,128]{2,1,0:T(1,128)S(1)} all-to-all(f32[128,1,128]{2,1,0:T(1,128)S(1)} %broadcast_in_dim.36), channel_id=1, replica_groups=mesh['sec'=4,'pair'=32,'core'=2] {'sec','pair'}, dimensions={0} | all-to-all | bytes 131072 | tf_op jit(solution)/shard_map/all_to_all | solution.py:406
  113.3 0.3 shard_map.76
  113.7 9.3 %all_to_all.29.parts_ref = f32[4,7,16,256]{3,2,1,0:T(8,128)S(1)} all-to-all(f32[4,7,16,256]{3,2,1,0:T(8,128)S(1)} %shard_map.76), channel_id=1, replica_groups=mesh['sec'=4,'pair'=32,'core'=2] {'sec'}, dimensions={0} | all-to-all | bytes 917504 | tf_op jit(solution)/shard_map/all_to_all | solution.py:463
  122.9 0.8 shard_map.77
  (18 shorter events, 0.2 us)
Async XLA Ops:
  0.6 15.2 %copy-start = (f32[3,16,1024]{2,1,0:T(8,128)S(1)}, f32[3,16,1024]{2,1,0:T(8,128)}, u32[]{:S(2)}) copy-start(f32[3,16,1024]{2,1,0:T(8,128)} %rain_ref.1) | copy-start | bytes 589828
  2.0 21.5 %copy-start.1 = (f32[12]{0:T(128)S(1)}, f32[12]{0:T(128)}, u32[]{:S(2)}) copy-start(f32[12]{0:T(128)} %param.8) | copy-start | bytes 148
  2.0 21.5 %copy-start.2 = (f32[12]{0:T(128)S(1)}, f32[12]{0:T(128)}, u32[]{:S(2)}) copy-start(f32[12]{0:T(128)} %param.7) | copy-start | bytes 148
  16.0 13.1 %collective-permute-start = (f32[40,16,256]{2,1,0:T(8,128)S(1)}, f32[40,16,256]{2,1,0:T(8,128)S(1)}, u32[]{:S(2)}, u32[]{:S(2)}) collective-permute-start(f32[40,16,256]{2,1,0:T(8,128)S(1)} %shard_map.69.from_ref), channel_id=1, source_target_pairs={{0,1},{1,2},{2,3},{3,4},{4,5},{5,6},{6,7},{7,8},{8,9},{9,10},{10,1... | collective-permute-start | bytes 1966088 | tf_op jit(solution)/shard_map/ppermute | solution.py:424
  21.6 11.9 %collective-permute-start.1 = (f32[40,16,256]{2,1,0:T(8,128)S(1)}, f32[40,16,256]{2,1,0:T(8,128)S(1)}, u32[]{:S(2)}, u32[]{:S(2)}) collective-permute-start(f32[40,16,256]{2,1,0:T(8,128)S(1)} %shard_map.69.from_ref), channel_id=1, source_target_pairs={{1,0},{2,1},{3,2},{4,3},{5,4},{6,5},{7,6},{8,7},{9,8},{10,9},{11,1... | collective-permute-start | bytes 1966088 | tf_op jit(solution)/shard_map/ppermute | solution.py:425
  40.9 1.2 collective-permute-start.2
  71.1 2.5 %collective-permute-start.3 = (f32[8,128]{1,0:T(8,128)S(1)}, f32[8,128]{1,0:T(8,128)S(1)}, u32[]{:S(2)}, u32[]{:S(2)}) collective-permute-start(f32[8,128]{1,0:T(8,128)S(1)} %get-tuple-element.75), channel_id=1, source_target_pairs={{0,1},{1,0},{2,3},{3,2},{4,5},{5,4},{6,7},{7,6},{8,9},{9,8},{10,11... | collective-permute-start | bytes 12296 | tf_op jit(solution)/shard_map/ppermute | solution.py:405
  94.8 2.4 %collective-permute-start.4 = (f32[8,128]{1,0:T(8,128)S(1)}, f32[8,128]{1,0:T(8,128)S(1)}, u32[]{:S(2)}, u32[]{:S(2)}) collective-permute-start(f32[8,128]{1,0:T(8,128)S(1)} %get-tuple-element.81), channel_id=1, source_target_pairs={{0,1},{1,0},{2,3},{3,2},{4,5},{5,4},{6,7},{7,6},{8,9},{9,8},{10,11... | collective-permute-start | bytes 12296 | tf_op jit(solution)/shard_map/ppermute | solution.py:405

commit v6 on v5

--- a/solution.py
+++ b/solution.py
@@ -180,6 +180,14 @@
             total = total + saturation
         water_ref[s] = total
         low_cond_ref[s] = 0.5 * cond
+
+
+def sides_kernel(chip_ref, beyond_ref, low_ref, high_ref):
+    first = lax.axis_index("core") == 0
+    for slot in range(SLOTS):
+        chip, beyond = chip_ref[slot], beyond_ref[slot]
+        low_ref[slot] = jnp.where(first, beyond, chip)
+        high_ref[slot] = jnp.where(first, chip, beyond)
 
 
 def framed(parts, start, stop):
@@ -421,8 +429,10 @@
     )
     mid = lax.all_to_all(packed, "sec", 0, 0, tiled=True)
     to_send = call(edges_kernel, held(mid, rainfall), near(SLOTS, OWN_ROWS, OWN_COLS))
-    low = lax.ppermute(to_send, gx, [(i, i + 1) for i in range(bands - 1)])
-    high = lax.ppermute(to_send, gx, [(i + 1, i) for i in range(bands - 1)])
+    pairs = [(i, i + 1) for i in range(1, bands - 1, 2)]
+    beyond = lax.ppermute(to_send, gx, pairs + [(j, i) for i, j in pairs])
+    chip = lax.ppermute(to_send, "core", [(0, 1), (1, 0)])
+    low, high = call(sides_kernel, held(chip, beyond), [near(SLOTS, OWN_ROWS, OWN_COLS)] * 2)
     tables = jnp.stack([saturated_conductivity, storage_coefficient])
     tables = jnp.broadcast_to(jnp.pad(tables, ((0, 0), (0, 128 - tables.shape[1])))[:, None, :], (2, 8, 128))
 

time: 125 us -> 123 us (0.984)
  starting transfers between devices: 10.8 us -> 9.11 us
  blocking collectives: 78.9 us -> 80.2 us
    ppermute x2, starting transfers between devices: 7.5 us -> 5.67 us  [the longest x1 5.58 us: body(): beyond = lax.ppermute(to_send, gx, pairs + [(j, i) for i, j in pairs])]
    pallas_call x10 -> x11, Pallas kernels: 21.8 us -> 21.9 us  [call(): pl.pallas_call(kernel, **more, out_shape=outs, in_specs=in_specs or [VMEM...]
  transfers between devices with their start and end apart: 5 -> 5, of which waited for: 5 -> 4; matrix products, arithmetic and copies ran while one was open for 0% -> 0% of each run, Pallas kernels for 1% -> 1%
where the time goes in v6:
time: 123 us; the launch traced here: 122 us
  blocking collectives  80.2 us (65%)
  Pallas kernels  21.9 us (18%)
  waiting for transfers between devices  10.2 us (8%)
  starting transfers between devices  9.11 us (7%)
    all_to_all x3, blocking collectives, add_up(): lax.all_to_all(jnp.broadcast_to(both[:1, None], (chips, 1, 128)), ('sec',...  57.1 us
    pallas_call x11, Pallas kernels, call(): pl.pallas_call(kernel, **more, out_shape=outs, in_specs=in_specs or [VMEM...  21.9 us
    all_to_all x1, blocking collectives, body(): mid = lax.all_to_all(packed, 'sec', 0, 0, tiled=True)  13.8 us
    all_to_all x1, blocking collectives, body(): out = lax.all_to_all(out, 'sec', 0, 0, tiled=True)  9.26 us
    ppermute x1, waiting for transfers between devices, body(): beyond = lax.ppermute(to_send, gx, pairs + [(j, i) for i, j in pairs])  7.4 us
    ppermute x1, starting transfers between devices, body(): beyond = lax.ppermute(to_send, gx, pairs + [(j, i) for i, j in pairs])  5.58 us
    ppermute x3, starting transfers between devices, add_up(): both = moments + lax.ppermute(moments, 'core', [(0, 1), (1, 0)])  3.44 us
    ppermute x3, waiting for transfers between devices, add_up(): both = moments + lax.ppermute(moments, 'core', [(0, 1), (1, 0)])  2.8 us
  transfers between devices with their start and end apart: 5, of which 4 were waited for; matrix products, arithmetic and copies ran while one was open for 0% of the time, Pallas kernels for 1%

profile of v6, /device:TPU:1, one launch (start us, length us, event | category | flops | bytes accessed | tf_op | source)
XLA Modules:
  0.0 122.5 jit_solution(17744697445395116628)
XLA Ops:
  0.6 1.4 %shard_map.68 = f32[4,9,16,256]{3,2,1,0:T(8,128)S(1)} custom-call(f32[4,16,1024]{2,1,0:T(8,128)} %head_hbm.1, s32[4,16,1024]{2,1,0:T(8,128)} %soil_hbm.1), custom_call_target="tpu_custom_call" | custom-call | tf_op jit(solution)/shard_map/pallas_call | solution.py:388
  2.0 13.8 %all_to_all.25.mid_ref = f32[4,9,16,256]{3,2,1,0:T(8,128)S(1)} all-to-all(f32[4,9,16,256]{3,2,1,0:T(8,128)S(1)} %shard_map.68), channel_id=1, replica_groups=mesh['sec'=4,'pair'=32,'core'=2] {'sec'}, dimensions={0} | all-to-all | bytes 1179648 | tf_op jit(solution)/shard_map/all_to_all | solution.py:430
  15.8 0.2 shard_map.69.from_ref
  16.0 5.6 %collective-permute-start.1 = (f32[40,16,256]{2,1,0:T(8,128)S(1)}, f32[40,16,256]{2,1,0:T(8,128)S(1)}, u32[]{:S(2)}, u32[]{:S(2)}) collective-permute-start(f32[40,16,256]{2,1,0:T(8,128)S(1)} %shard_map.69.from_ref), channel_id=1, source_target_pairs={{1,2},{3,4},{5,6},{7,8},{9,10},{11,12},{13,14},{15,16},{17,18},{19... | collective-permute-start | bytes 1966088 | tf_op jit(solution)/shard_map/ppermute | solution.py:433
  21.6 0.1 collective-permute-start
  21.7 0.7 shard_map.72
  22.4 7.4 %collective-permute-done.1.beyond_ref = f32[40,16,256]{2,1,0:T(8,128)S(1)} collective-permute-done((f32[40,16,256]{2,1,0:T(8,128)S(1)}, f32[40,16,256]{2,1,0:T(8,128)S(1)}, u32[]{:S(2)}, u32[]{:S(2)}) %collective-permute-start.1) | collective-permute-done | bytes 655392 | tf_op jit(solution)/shard_map/ppermute | solution.py:433
  29.9 0.1 shard_map.70
  30.0 0.7 shard_map.71
  30.7 0.7 shard_map.73
  31.4 6.7 %shard_map.74 = (f32[16,48,384]{2,1,0:T(8,128)S(1)}, f32[16,48,384]{2,1,0:T(8,128)S(1)}, f32[16,48,384]{2,1,0:T(8,128)S(1)}, f32[16,48,384]{2,1,0:T(8,128)S(1)},...) custom-call(f32[16,16,384]{2,1,0:T(8,128)S(1)} %get-tuple-element.49.refs_0_.refs_5_, ...), custom_call_target="tpu_custom_call" | custom-call | tf_op jit(solution)/shard_map/pallas_call | solution.py:388
  38.1 1.2 collective-permute-done.2
  39.3 24.9 %all_to_all.26 = f32[128,1,128]{2,1,0:T(1,128)S(1)} all-to-all(f32[128,1,128]{2,1,0:T(1,128)S(1)} %broadcast_in_dim.32), channel_id=1, replica_groups=mesh['sec'=4,'pair'=32,'core'=2] {'sec','pair'}, dimensions={0} | all-to-all | bytes 131072 | tf_op jit(solution)/shard_map/all_to_all | solution.py:414
  64.2 5.3 %shard_map.75 = (f32[16,40,384]{2,1,0:T(8,128)S(1)}, f32[16,32,384]{2,1,0:T(8,128)S(1)}, f32[16,32,384]{2,1,0:T(8,128)S(1)}, f32[16,32,384]{2,1,0:T(8,128)S(1)},...) custom-call(f32[128,128]{1,0:T(8,128)S(1)} %bitcast.12, ...), custom_call_target="tpu_custom_call" | custom-call | tf_op jit(solution)/shard_map/pallas_call | solution.py:388
  69.5 1.8 %collective-permute-start.3 = (f32[8,128]{1,0:T(8,128)S(1)}, f32[8,128]{1,0:T(8,128)S(1)}, u32[]{:S(2)}, u32[]{:S(2)}) collective-permute-start(f32[8,128]{1,0:T(8,128)S(1)} %get-tuple-element.79), channel_id=1, source_target_pairs={{0,1},{1,0},{2,3},{3,2},{4,5},{5,4},{6,7},{7,6},{8,9},{9,8},{10,11... | collective-permute-start | bytes 12296 | tf_op jit(solution)/shard_map/ppermute | solution.py:413
  71.3 0.8 collective-permute-done.3
  72.1 16.1 %all_to_all.27 = f32[128,1,128]{2,1,0:T(1,128)S(1)} all-to-all(f32[128,1,128]{2,1,0:T(1,128)S(1)} %broadcast_in_dim.34), channel_id=1, replica_groups=mesh['sec'=4,'pair'=32,'core'=2] {'sec','pair'}, dimensions={0} | all-to-all | bytes 131072 | tf_op jit(solution)/shard_map/all_to_all | solution.py:414
  88.2 5.1 %shard_map.76 = (f32[16,32,384]{2,1,0:T(8,128)S(1)}, f32[16,32,384]{2,1,0:T(8,128)S(1)}, f32[16,32,384]{2,1,0:T(8,128)S(1)}, f32[16,32,384]{2,1,0:T(8,128)S(1)},...) custom-call(f32[128,128]{1,0:T(8,128)S(1)} %bitcast.11, ...), custom_call_target="tpu_custom_call" | custom-call | tf_op jit(solution)/shard_map/pallas_call | solution.py:388
  93.4 1.6 %collective-permute-start.4 = (f32[8,128]{1,0:T(8,128)S(1)}, f32[8,128]{1,0:T(8,128)S(1)}, u32[]{:S(2)}, u32[]{:S(2)}) collective-permute-start(f32[8,128]{1,0:T(8,128)S(1)} %get-tuple-element.85), channel_id=1, source_target_pairs={{0,1},{1,0},{2,3},{3,2},{4,5},{5,4},{6,7},{7,6},{8,9},{9,8},{10,11... | collective-permute-start | bytes 12296 | tf_op jit(solution)/shard_map/ppermute | solution.py:413
  95.0 0.8 collective-permute-done.4
  95.8 16.1 %all_to_all.28 = f32[128,1,128]{2,1,0:T(1,128)S(1)} all-to-all(f32[128,1,128]{2,1,0:T(1,128)S(1)} %broadcast_in_dim.36), channel_id=1, replica_groups=mesh['sec'=4,'pair'=32,'core'=2] {'sec','pair'}, dimensions={0} | all-to-all | bytes 131072 | tf_op jit(solution)/shard_map/all_to_all | solution.py:414
  111.9 0.3 shard_map.77
  112.2 9.3 %all_to_all.29.parts_ref = f32[4,7,16,256]{3,2,1,0:T(8,128)S(1)} all-to-all(f32[4,7,16,256]{3,2,1,0:T(8,128)S(1)} %shard_map.77), channel_id=1, replica_groups=mesh['sec'=4,'pair'=32,'core'=2] {'sec'}, dimensions={0} | all-to-all | bytes 917504 | tf_op jit(solution)/shard_map/all_to_all | solution.py:473
  121.5 0.8 shard_map.78
  (19 shorter events, 0.2 us)
Async XLA Ops:
  0.6 15.2 %copy-start = (f32[3,16,1024]{2,1,0:T(8,128)S(1)}, f32[3,16,1024]{2,1,0:T(8,128)}, u32[]{:S(2)}) copy-start(f32[3,16,1024]{2,1,0:T(8,128)} %rain_ref.1) | copy-start | bytes 589828
  2.0 19.7 %copy-start.1 = (f32[12]{0:T(128)S(1)}, f32[12]{0:T(128)}, u32[]{:S(2)}) copy-start(f32[12]{0:T(128)} %param.8) | copy-start | bytes 148
  2.0 19.7 %copy-start.2 = (f32[12]{0:T(128)S(1)}, f32[12]{0:T(128)}, u32[]{:S(2)}) copy-start(f32[12]{0:T(128)} %param.7) | copy-start | bytes 148
  16.0 13.8 %collective-permute-start.1 = (f32[40,16,256]{2,1,0:T(8,128)S(1)}, f32[40,16,256]{2,1,0:T(8,128)S(1)}, u32[]{:S(2)}, u32[]{:S(2)}) collective-permute-start(f32[40,16,256]{2,1,0:T(8,128)S(1)} %shard_map.69.from_ref), channel_id=1, source_target_pairs={{1,2},{3,4},{5,6},{7,8},{9,10},{11,12},{13,14},{15,16},{17,18},{19... | collective-permute-start | bytes 1966088 | tf_op jit(solution)/shard_map/ppermute | solution.py:433
  21.6 8.3 %collective-permute-start = (f32[40,16,256]{2,1,0:T(8,128)S(1)}, f32[40,16,256]{2,1,0:T(8,128)S(1)}, u32[]{:S(2)}, u32[]{:S(2)}) collective-permute-start(f32[40,16,256]{2,1,0:T(8,128)S(1)} %shard_map.69.from_ref), channel_id=1, source_target_pairs={{0,1},{1,0},{2,3},{3,2},{4,5},{5,4},{6,7},{7,6},{8,9},{9,8},{10,11... | collective-permute-start | bytes 1966088 | tf_op jit(solution)/shard_map/ppermute | solution.py:434
  38.0 1.2 collective-permute-start.2
  69.5 2.6 %collective-permute-start.3 = (f32[8,128]{1,0:T(8,128)S(1)}, f32[8,128]{1,0:T(8,128)S(1)}, u32[]{:S(2)}, u32[]{:S(2)}) collective-permute-start(f32[8,128]{1,0:T(8,128)S(1)} %get-tuple-element.79), channel_id=1, source_target_pairs={{0,1},{1,0},{2,3},{3,2},{4,5},{5,4},{6,7},{7,6},{8,9},{9,8},{10,11... | collective-permute-start | bytes 12296 | tf_op jit(solution)/shard_map/ppermute | solution.py:413
  93.4 2.4 %collective-permute-start.4 = (f32[8,128]{1,0:T(8,128)S(1)}, f32[8,128]{1,0:T(8,128)S(1)}, u32[]{:S(2)}, u32[]{:S(2)}) collective-permute-start(f32[8,128]{1,0:T(8,128)S(1)} %get-tuple-element.85), channel_id=1, source_target_pairs={{0,1},{1,0},{2,3},{3,2},{4,5},{5,4},{6,7},{7,6},{8,9},{9,8},{10,11... | collective-permute-start | bytes 12296 | tf_op jit(solution)/shard_map/ppermute | solution.py:413

commit v7 on v6

--- a/solution.py
+++ b/solution.py
@@ -18,6 +18,7 @@
 EDGE = 16
 FRAME = 48
 SLOTS = 40
+REACH = 13
 SPANS = ((0, 48), (0, 40), (8, 40))
 WORK = ((0, 48), (8, 40), (8, 40))
 F32 = jnp.float32
@@ -76,7 +77,7 @@
             out_ref[target, 2 * LZ, :, 128 * part : 128 * part + 128] = grouped(tails)
 
 
-def edges_kernel(mid_ref, rain_ref, out_ref):
+def edges_kernel(mid_ref, rain_ref, out_ref, beyond_ref):
     section = lax.axis_index("sec")
     start = pl.multiple_of(section * OWN_COLS, OWN_COLS)
     after = pl.multiple_of(lax.rem(section + 1, SECTIONS) * OWN_COLS, OWN_COLS)
@@ -88,6 +89,10 @@
     out_ref[39] = jnp.concatenate([grouped(tails), jnp.zeros((OWN_ROWS, 128), F32)], axis=1)
     for slot in range(36):
         out_ref[slot] = mid_ref[slot // 9, slot % 9]
+    first = lax.axis_index("core") == 0
+    for slot in range(SLOTS):
+        field = out_ref[slot]
+        beyond_ref[REACH * slot : REACH * slot + REACH, :] = jnp.where(first, field[:REACH], field[OWN_ROWS - REACH :])
 
 
 def weights(sums_ref):
@@ -185,7 +190,9 @@
 def sides_kernel(chip_ref, beyond_ref, low_ref, high_ref):
     first = lax.axis_index("core") == 0
     for slot in range(SLOTS):
-        chip, beyond = chip_ref[slot], beyond_ref[slot]
+        chip, beyond = chip_ref[slot], beyond_ref[REACH * slot : REACH * slot + REACH, :]
+        gap = jnp.zeros((OWN_ROWS - REACH, OWN_COLS), F32)
+        beyond = jnp.where(first, jnp.concatenate([gap, beyond], axis=0), jnp.concatenate([beyond, gap], axis=0))
         low_ref[slot] = jnp.where(first, beyond, chip)
         high_ref[slot] = jnp.where(first, chip, beyond)
 
@@ -428,9 +435,11 @@
         in_specs=[outside] * 2,
     )
     mid = lax.all_to_all(packed, "sec", 0, 0, tiled=True)
-    to_send = call(edges_kernel, held(mid, rainfall), near(SLOTS, OWN_ROWS, OWN_COLS))
+    to_send, to_beyond = call(
+        edges_kernel, held(mid, rainfall), [near(SLOTS, OWN_ROWS, OWN_COLS), near(REACH * SLOTS, OWN_COLS)]
+    )
     pairs = [(i, i + 1) for i in range(1, bands - 1, 2)]
-    beyond = lax.ppermute(to_send, gx, pairs + [(j, i) for i, j in pairs])
+    beyond = lax.ppermute(to_beyond, gx, pairs + [(j, i) for i, j in pairs])
     chip = lax.ppermute(to_send, "core", [(0, 1), (1, 0)])
     low, high = call(sides_kernel, held(chip, beyond), [near(SLOTS, OWN_ROWS, OWN_COLS)] * 2)
     tables = jnp.stack([saturated_conductivity, storage_coefficient])

time: 123 us -> 122 us (level)
    ppermute x1, starting transfers between devices: 0.09 us -> 2.24 us  [body(): chip = lax.ppermute(to_send, 'core', [(0, 1), (1, 0)])]
    ppermute x1, starting transfers between devices: 5.58 us -> 3.44 us  [body(): beyond = lax.ppermute(to_beyond, gx, pairs + [(j, i) for i, j in pairs])]
where the time goes in v7:
time: 122 us; the launch traced here: 121 us
  blocking collectives  80 us (66%)
  Pallas kernels  22 us (18%)
  waiting for transfers between devices  9.17 us (8%)
  starting transfers between devices  9.12 us (7%)
    all_to_all x3, blocking collectives, add_up(): lax.all_to_all(jnp.broadcast_to(both[:1, None], (chips, 1, 128)), ('sec',...  56.9 us
    pallas_call x11, Pallas kernels, call(): pl.pallas_call(kernel, **more, out_shape=outs, in_specs=in_specs or [VMEM...  22 us
    all_to_all x1, blocking collectives, body(): mid = lax.all_to_all(packed, 'sec', 0, 0, tiled=True)  13.8 us
    all_to_all x1, blocking collectives, body(): out = lax.all_to_all(out, 'sec', 0, 0, tiled=True)  9.26 us
    ppermute x1, waiting for transfers between devices, body(): beyond = lax.ppermute(to_beyond, gx, pairs + [(j, i) for i, j in pairs])  6.37 us
    ppermute x1, starting transfers between devices, body(): beyond = lax.ppermute(to_beyond, gx, pairs + [(j, i) for i, j in pairs])  3.44 us
    ppermute x3, starting transfers between devices, add_up(): both = moments + lax.ppermute(moments, 'core', [(0, 1), (1, 0)])  3.44 us
    ppermute x3, waiting for transfers between devices, add_up(): both = moments + lax.ppermute(moments, 'core', [(0, 1), (1, 0)])  2.8 us
  transfers between devices with their start and end apart: 5, of which 4 were waited for; matrix products, arithmetic and copies ran while one was open for 0% of the time, Pallas kernels for 1%

profile of v7, /device:TPU:1, one launch (start us, length us, event | category | flops | bytes accessed | tf_op | source)
XLA Modules:
  0.0 121.3 jit_solution(5778631851842345951)
XLA Ops:
  0.6 1.4 %shard_map.68 = f32[4,9,16,256]{3,2,1,0:T(8,128)S(1)} custom-call(f32[4,16,1024]{2,1,0:T(8,128)} %head_hbm.1, s32[4,16,1024]{2,1,0:T(8,128)} %soil_hbm.1), custom_call_target="tpu_custom_call" | custom-call | tf_op jit(solution)/shard_map/pallas_call | solution.py:395
  2.0 13.8 %all_to_all.25.mid_ref = f32[4,9,16,256]{3,2,1,0:T(8,128)S(1)} all-to-all(f32[4,9,16,256]{3,2,1,0:T(8,128)S(1)} %shard_map.68), channel_id=1, replica_groups=mesh['sec'=4,'pair'=32,'core'=2] {'sec'}, dimensions={0} | all-to-all | bytes 1179648 | tf_op jit(solution)/shard_map/all_to_all | solution.py:437
  15.8 0.2 shard_map.69
  16.0 2.2 %collective-permute-start = (f32[40,16,256]{2,1,0:T(8,128)S(1)}, f32[40,16,256]{2,1,0:T(8,128)S(1)}, u32[]{:S(2)}, u32[]{:S(2)}) collective-permute-start(f32[40,16,256]{2,1,0:T(8,128)S(1)} %get-tuple-element.50.from_ref), channel_id=1, source_target_pairs={{0,1},{1,0},{2,3},{3,2},{4,5},{5,4},{6,7},{7,6},{8,9},{9,8},{10,11... | collective-permute-start | bytes 1966088 | tf_op jit(solution)/shard_map/ppermute | solution.py:443
  18.2 3.4 %collective-permute-start.1 = (f32[520,256]{1,0:T(8,128)S(1)}, f32[520,256]{1,0:T(8,128)S(1)}, u32[]{:S(2)}, u32[]{:S(2)}) collective-permute-start(f32[520,256]{1,0:T(8,128)S(1)} %get-tuple-element.51), channel_id=1, source_target_pairs={{1,2},{3,4},{5,6},{7,8},{9,10},{11,12},{13,14},{15,16},{17,18},{19... | collective-permute-start | bytes 1597448 | tf_op jit(solution)/shard_map/ppermute | solution.py:442
  21.7 0.7 shard_map.72
  22.5 6.4 %collective-permute-done.1.beyond_ref = f32[520,256]{1,0:T(8,128)S(1)} collective-permute-done((f32[520,256]{1,0:T(8,128)S(1)}, f32[520,256]{1,0:T(8,128)S(1)}, u32[]{:S(2)}, u32[]{:S(2)}) %collective-permute-start.1) | collective-permute-done | bytes 532512 | tf_op jit(solution)/shard_map/ppermute | solution.py:442
  28.8 0.1 shard_map.70
  29.0 0.7 shard_map.71
  29.7 0.7 shard_map.73
  30.4 6.7 %shard_map.74 = (f32[16,48,384]{2,1,0:T(8,128)S(1)}, f32[16,48,384]{2,1,0:T(8,128)S(1)}, f32[16,48,384]{2,1,0:T(8,128)S(1)}, f32[16,48,384]{2,1,0:T(8,128)S(1)},...) custom-call(f32[16,16,384]{2,1,0:T(8,128)S(1)} %get-tuple-element.53.refs_0_.refs_5_, ...), custom_call_target="tpu_custom_call" | custom-call | tf_op jit(solution)/shard_map/pallas_call | solution.py:395
  37.1 1.2 collective-permute-done.2
  38.3 24.7 %all_to_all.26 = f32[128,1,128]{2,1,0:T(1,128)S(1)} all-to-all(f32[128,1,128]{2,1,0:T(1,128)S(1)} %broadcast_in_dim.32), channel_id=1, replica_groups=mesh['sec'=4,'pair'=32,'core'=2] {'sec','pair'}, dimensions={0} | all-to-all | bytes 131072 | tf_op jit(solution)/shard_map/all_to_all | solution.py:421
  63.1 5.3 %shard_map.75 = (f32[16,40,384]{2,1,0:T(8,128)S(1)}, f32[16,32,384]{2,1,0:T(8,128)S(1)}, f32[16,32,384]{2,1,0:T(8,128)S(1)}, f32[16,32,384]{2,1,0:T(8,128)S(1)},...) custom-call(f32[128,128]{1,0:T(8,128)S(1)} %bitcast.12, ...), custom_call_target="tpu_custom_call" | custom-call | tf_op jit(solution)/shard_map/pallas_call | solution.py:395
  68.3 1.8 %collective-permute-start.3 = (f32[8,128]{1,0:T(8,128)S(1)}, f32[8,128]{1,0:T(8,128)S(1)}, u32[]{:S(2)}, u32[]{:S(2)}) collective-permute-start(f32[8,128]{1,0:T(8,128)S(1)} %get-tuple-element.83), channel_id=1, source_target_pairs={{0,1},{1,0},{2,3},{3,2},{4,5},{5,4},{6,7},{7,6},{8,9},{9,8},{10,11... | collective-permute-start | bytes 12296 | tf_op jit(solution)/shard_map/ppermute | solution.py:420
  70.1 0.8 collective-permute-done.3
  71.0 16.1 %all_to_all.27 = f32[128,1,128]{2,1,0:T(1,128)S(1)} all-to-all(f32[128,1,128]{2,1,0:T(1,128)S(1)} %broadcast_in_dim.34), channel_id=1, replica_groups=mesh['sec'=4,'pair'=32,'core'=2] {'sec','pair'}, dimensions={0} | all-to-all | bytes 131072 | tf_op jit(solution)/shard_map/all_to_all | solution.py:421
  87.1 5.1 %shard_map.76 = (f32[16,32,384]{2,1,0:T(8,128)S(1)}, f32[16,32,384]{2,1,0:T(8,128)S(1)}, f32[16,32,384]{2,1,0:T(8,128)S(1)}, f32[16,32,384]{2,1,0:T(8,128)S(1)},...) custom-call(f32[128,128]{1,0:T(8,128)S(1)} %bitcast.11, ...), custom_call_target="tpu_custom_call" | custom-call | tf_op jit(solution)/shard_map/pallas_call | solution.py:395
  92.2 1.6 %collective-permute-start.4 = (f32[8,128]{1,0:T(8,128)S(1)}, f32[8,128]{1,0:T(8,128)S(1)}, u32[]{:S(2)}, u32[]{:S(2)}) collective-permute-start(f32[8,128]{1,0:T(8,128)S(1)} %get-tuple-element.89), channel_id=1, source_target_pairs={{0,1},{1,0},{2,3},{3,2},{4,5},{5,4},{6,7},{7,6},{8,9},{9,8},{10,11... | collective-permute-start | bytes 12296 | tf_op jit(solution)/shard_map/ppermute | solution.py:420
  93.8 0.8 collective-permute-done.4
  94.7 16.1 %all_to_all.28 = f32[128,1,128]{2,1,0:T(1,128)S(1)} all-to-all(f32[128,1,128]{2,1,0:T(1,128)S(1)} %broadcast_in_dim.36), channel_id=1, replica_groups=mesh['sec'=4,'pair'=32,'core'=2] {'sec','pair'}, dimensions={0} | all-to-all | bytes 131072 | tf_op jit(solution)/shard_map/all_to_all | solution.py:421
  110.8 0.3 shard_map.77
  111.1 9.3 %all_to_all.29.parts_ref = f32[4,7,16,256]{3,2,1,0:T(8,128)S(1)} all-to-all(f32[4,7,16,256]{3,2,1,0:T(8,128)S(1)} %shard_map.77), channel_id=1, replica_groups=mesh['sec'=4,'pair'=32,'core'=2] {'sec'}, dimensions={0} | all-to-all | bytes 917504 | tf_op jit(solution)/shard_map/all_to_all | solution.py:482
  120.3 0.8 shard_map.78
  (19 shorter events, 0.2 us)
Async XLA Ops:
  0.6 15.2 %copy-start = (f32[3,16,1024]{2,1,0:T(8,128)S(1)}, f32[3,16,1024]{2,1,0:T(8,128)}, u32[]{:S(2)}) copy-start(f32[3,16,1024]{2,1,0:T(8,128)} %rain_ref.1) | copy-start | bytes 589828
  2.0 19.7 %copy-start.1 = (f32[12]{0:T(128)S(1)}, f32[12]{0:T(128)}, u32[]{:S(2)}) copy-start(f32[12]{0:T(128)} %param.8) | copy-start | bytes 148
  2.0 19.7 %copy-start.2 = (f32[12]{0:T(128)S(1)}, f32[12]{0:T(128)}, u32[]{:S(2)}) copy-start(f32[12]{0:T(128)} %param.7) | copy-start | bytes 148
  16.0 12.8 %collective-permute-start = (f32[40,16,256]{2,1,0:T(8,128)S(1)}, f32[40,16,256]{2,1,0:T(8,128)S(1)}, u32[]{:S(2)}, u32[]{:S(2)}) collective-permute-start(f32[40,16,256]{2,1,0:T(8,128)S(1)} %get-tuple-element.50.from_ref), channel_id=1, source_target_pairs={{0,1},{1,0},{2,3},{3,2},{4,5},{5,4},{6,7},{7,6},{8,9},{9,8},{10,11... | collective-permute-start | bytes 1966088 | tf_op jit(solution)/shard_map/ppermute | solution.py:443
  18.2 10.6 %collective-permute-start.1 = (f32[520,256]{1,0:T(8,128)S(1)}, f32[520,256]{1,0:T(8,128)S(1)}, u32[]{:S(2)}, u32[]{:S(2)}) collective-permute-start(f32[520,256]{1,0:T(8,128)S(1)} %get-tuple-element.51), channel_id=1, source_target_pairs={{1,2},{3,4},{5,6},{7,8},{9,10},{11,12},{13,14},{15,16},{17,18},{19... | collective-permute-start | bytes 1597448 | tf_op jit(solution)/shard_map/ppermute | solution.py:442
  37.1 1.2 collective-permute-start.2
  68.3 2.6 %collective-permute-start.3 = (f32[8,128]{1,0:T(8,128)S(1)}, f32[8,128]{1,0:T(8,128)S(1)}, u32[]{:S(2)}, u32[]{:S(2)}) collective-permute-start(f32[8,128]{1,0:T(8,128)S(1)} %get-tuple-element.83), channel_id=1, source_target_pairs={{0,1},{1,0},{2,3},{3,2},{4,5},{5,4},{6,7},{7,6},{8,9},{9,8},{10,11... | collective-permute-start | bytes 12296 | tf_op jit(solution)/shard_map/ppermute | solution.py:420
  92.2 2.4 %collective-permute-start.4 = (f32[8,128]{1,0:T(8,128)S(1)}, f32[8,128]{1,0:T(8,128)S(1)}, u32[]{:S(2)}, u32[]{:S(2)}) collective-permute-start(f32[8,128]{1,0:T(8,128)S(1)} %get-tuple-element.89), channel_id=1, source_target_pairs={{0,1},{1,0},{2,3},{3,2},{4,5},{5,4},{6,7},{7,6},{8,9},{9,8},{10,11... | collective-permute-start | bytes 12296 | tf_op jit(solution)/shard_map/ppermute | solution.py:420

commit v8 on v7

--- a/solution.py
+++ b/solution.py
@@ -77,22 +77,29 @@
             out_ref[target, 2 * LZ, :, 128 * part : 128 * part + 128] = grouped(tails)
 
 
-def edges_kernel(mid_ref, rain_ref, out_ref, beyond_ref):
+def edges_kernel(mid_ref, rain_ref, beyond_ref, chip_ref, rain_out_ref):
     section = lax.axis_index("sec")
     start = pl.multiple_of(section * OWN_COLS, OWN_COLS)
     after = pl.multiple_of(lax.rem(section + 1, SECTIONS) * OWN_COLS, OWN_COLS)
     before = pl.multiple_of(lax.rem(section + SECTIONS - 1, SECTIONS) * OWN_COLS + 128, 128)
     tails = []
     for c in range(3):
-        out_ref[36 + c] = rain_ref[c, :, pl.ds(start, OWN_COLS)]
+        rain_out_ref[c] = rain_ref[c, :, pl.ds(start, OWN_COLS)]
         tails.append(tail_of(rain_ref[c, :, pl.ds(after, 128)], rain_ref[c, :, pl.ds(before, 128)]))
-    out_ref[39] = jnp.concatenate([grouped(tails), jnp.zeros((OWN_ROWS, 128), F32)], axis=1)
-    for slot in range(36):
-        out_ref[slot] = mid_ref[slot // 9, slot % 9]
+    rain_out_ref[3] = jnp.concatenate([grouped(tails), jnp.zeros((OWN_ROWS, 128), F32)], axis=1)
     first = lax.axis_index("core") == 0
+    beyond_ref[REACH * SLOTS :, :] = jnp.zeros((8, OWN_COLS), F32)
     for slot in range(SLOTS):
-        field = out_ref[slot]
-        beyond_ref[REACH * slot : REACH * slot + REACH, :] = jnp.where(first, field[:REACH], field[OWN_ROWS - REACH :])
+        field = mid_ref[slot // 9, slot % 9] if slot < 36 else rain_out_ref[slot - 36]
+        at = slice(REACH * slot, REACH * slot + REACH)
+        top, bottom = field[:REACH], field[OWN_ROWS - REACH :]
+        beyond_ref[at, :] = jnp.where(first, top, bottom)
+        chip_ref[at, :] = jnp.where(first, bottom, top)
+
+
+def whole_kernel(mid_ref, rain_ref, out_ref):
+    for slot in range(SLOTS):
+        out_ref[slot] = mid_ref[slot // 9, slot % 9] if slot < 36 else rain_ref[slot - 36]
 
 
 def weights(sums_ref):
@@ -190,11 +197,11 @@
 def sides_kernel(chip_ref, beyond_ref, low_ref, high_ref):
     first = lax.axis_index("core") == 0
     for slot in range(SLOTS):
-        chip, beyond = chip_ref[slot], beyond_ref[REACH * slot : REACH * slot + REACH, :]
+        at = slice(REACH * slot, REACH * slot + REACH)
+        chip, beyond = chip_ref[at, :], beyond_ref[at, :]
         gap = jnp.zeros((OWN_ROWS - REACH, OWN_COLS), F32)
-        beyond = jnp.where(first, jnp.concatenate([gap, beyond], axis=0), jnp.concatenate([beyond, gap], axis=0))
-        low_ref[slot] = jnp.where(first, beyond, chip)
-        high_ref[slot] = jnp.where(first, chip, beyond)
+        low_ref[slot] = jnp.concatenate([gap, jnp.where(first, beyond, chip)], axis=0)
+        high_ref[slot] = jnp.concatenate([jnp.where(first, chip, beyond), gap], axis=0)
 
 
 def framed(parts, start, stop):
@@ -331,15 +338,18 @@
     for k in range(1, ITERS):
         src, dst = basis[k - 1], basis[k]
 
+        made = slice(0, SPANS[1][1]) if first and k == ITERS - 1 else slice(0, span)
+
         def smooth(l, accs):
             v = src[l]
-            new = ru_ref[l] * turned(v, 1, 0) + rd_ref[l] * turned(v, -1, 0)
-            new = new + xl_ref[l] * turned(v, 1, 1) + xr_ref[l] * turned(v, -1, 1)
+            new = ru_ref[l, made] * turned(v, 1, 0)[made] + rd_ref[l, made] * turned(v, -1, 0)[made]
+            near_v = v[made]
+            new = new + xl_ref[l, made] * turned(near_v, 1, 1) + xr_ref[l, made] * turned(near_v, -1, 1)
             if l > 0:
-                new = new + up_ref[l] * src[l - 1]
+                new = new + up_ref[l, made] * src[l - 1, made]
             if l + 1 < NZ:
-                new = new + dn_ref[l] * src[l + 1]
-            dst[l] = new
+                new = new + dn_ref[l, made] * src[l + 1, made]
+            dst[l, made] = new
             mine = new[kept, 0:OWN_COLS]
             scaled = mine * diag_ref[l]
             return accs[0] + v[kept, 0:OWN_COLS] * scaled, accs[1] + mine * scaled
@@ -435,12 +445,15 @@
         in_specs=[outside] * 2,
     )
     mid = lax.all_to_all(packed, "sec", 0, 0, tiled=True)
-    to_send, to_beyond = call(
-        edges_kernel, held(mid, rainfall), [near(SLOTS, OWN_ROWS, OWN_COLS), near(REACH * SLOTS, OWN_COLS)]
+    to_beyond, to_chip, rain_own = call(
+        edges_kernel,
+        held(mid, rainfall),
+        [near(REACH * SLOTS + 8, OWN_COLS), near(REACH * SLOTS, OWN_COLS), near(4, OWN_ROWS, OWN_COLS)],
     )
+    to_send = call(whole_kernel, held(mid, rain_own), near(SLOTS, OWN_ROWS, OWN_COLS))
     pairs = [(i, i + 1) for i in range(1, bands - 1, 2)]
     beyond = lax.ppermute(to_beyond, gx, pairs + [(j, i) for i, j in pairs])
-    chip = lax.ppermute(to_send, "core", [(0, 1), (1, 0)])
+    chip = lax.ppermute(to_chip, "core", [(0, 1), (1, 0)])
     low, high = call(sides_kernel, held(chip, beyond), [near(SLOTS, OWN_ROWS, OWN_COLS)] * 2)
     tables = jnp.stack([saturated_conductivity, storage_coefficient])
     tables = jnp.broadcast_to(jnp.pad(tables, ((0, 0), (0, 128 - tables.shape[1])))[:, None, :], (2, 8, 128))

time: 122 us -> 122 us (level)
    ppermute x1, starting transfers between devices: 2.24 us -> 0.09 us  [body(): chip = lax.ppermute(to_chip, 'core', [(0, 1), (1, 0)])]
    ppermute x1, starting transfers between devices: 3.44 us -> 5.59 us  [body(): beyond = lax.ppermute(to_beyond, gx, pairs + [(j, i) for i, j in pairs])]
    ppermute x1, waiting for transfers between devices: 6.37 us -> 5.02 us  [body(): beyond = lax.ppermute(to_beyond, gx, pairs + [(j, i) for i, j in pairs])]
    pallas_call x11 -> x12, Pallas kernels: 22 us -> 21.9 us  [call(): pl.pallas_call(kernel, **more, out_shape=outs, in_specs=in_specs or [VMEM...]
  transfers between devices with their start and end apart: 5 -> 5, of which waited for: 4 -> 5; matrix products, arithmetic and copies ran while one was open for 0% -> 0% of each run, Pallas kernels for 1% -> 1%
where the time goes in v8:
time: 122 us; the launch traced here: 121 us
  blocking collectives  80.2 us (66%)
  Pallas kernels  21.9 us (18%)
  starting transfers between devices  9.12 us (7%)
  waiting for transfers between devices  8.92 us (7%)
    all_to_all x3, blocking collectives, add_up(): lax.all_to_all(jnp.broadcast_to(both[:1, None], (chips, 1, 128)), ('sec',...  57.1 us
    pallas_call x12, Pallas kernels, call(): pl.pallas_call(kernel, **more, out_shape=outs, in_specs=in_specs or [VMEM...  21.9 us
    all_to_all x1, blocking collectives, body(): mid = lax.all_to_all(packed, 'sec', 0, 0, tiled=True)  13.8 us
    all_to_all x1, blocking collectives, body(): out = lax.all_to_all(out, 'sec', 0, 0, tiled=True)  9.26 us
    ppermute x1, starting transfers between devices, body(): beyond = lax.ppermute(to_beyond, gx, pairs + [(j, i) for i, j in pairs])  5.59 us
    ppermute x1, waiting for transfers between devices, body(): beyond = lax.ppermute(to_beyond, gx, pairs + [(j, i) for i, j in pairs])  5.02 us
    ppermute x3, starting transfers between devices, add_up(): both = moments + lax.ppermute(moments, 'core', [(0, 1), (1, 0)])  3.44 us
    ppermute x3, waiting for transfers between devices, add_up(): both = moments + lax.ppermute(moments, 'core', [(0, 1), (1, 0)])  2.8 us
  transfers between devices with their start and end apart: 5, of which 5 were waited for; matrix products, arithmetic and copies ran while one was open for 0% of the time, Pallas kernels for 1%

profile of v8, /device:TPU:1, one launch (start us, length us, event | category | flops | bytes accessed | tf_op | source)
XLA Modules:
  0.0 121.2 jit_solution(13597336845038210736)
XLA Ops:
  0.6 1.4 %shard_map.68 = f32[4,9,16,256]{3,2,1,0:T(8,128)S(1)} custom-call(f32[4,16,1024]{2,1,0:T(8,128)} %head_hbm.1, s32[4,16,1024]{2,1,0:T(8,128)} %soil_hbm.1), custom_call_target="tpu_custom_call" | custom-call | tf_op jit(solution)/shard_map/pallas_call | solution.py:405
  2.0 13.8 %all_to_all.25.mid_ref = f32[4,9,16,256]{3,2,1,0:T(8,128)S(1)} all-to-all(f32[4,9,16,256]{3,2,1,0:T(8,128)S(1)} %shard_map.68), channel_id=1, replica_groups=mesh['sec'=4,'pair'=32,'core'=2] {'sec'}, dimensions={0} | all-to-all | bytes 1179648 | tf_op jit(solution)/shard_map/all_to_all | solution.py:447
  15.8 0.2 shard_map.69
  16.1 5.6 %collective-permute-start.1 = (f32[528,256]{1,0:T(8,128)S(1)}, f32[528,256]{1,0:T(8,128)S(1)}, u32[]{:S(2)}, u32[]{:S(2)}) collective-permute-start(f32[528,256]{1,0:T(8,128)S(1)} %get-tuple-element.52), channel_id=1, source_target_pairs={{1,2},{3,4},{5,6},{7,8},{9,10},{11,12},{13,14},{15,16},{17,18},{19... | collective-permute-start | bytes 1622024 | tf_op jit(solution)/shard_map/ppermute | solution.py:455
  21.9 0.7 shard_map.73
  22.6 1.1 collective-permute-done.chip_ref
  23.7 5.0 %collective-permute-done.1.beyond_ref = f32[528,256]{1,0:T(8,128)S(1)} collective-permute-done((f32[528,256]{1,0:T(8,128)S(1)}, f32[528,256]{1,0:T(8,128)S(1)}, u32[]{:S(2)}, u32[]{:S(2)}) %collective-permute-start.1) | collective-permute-done | bytes 540704 | tf_op jit(solution)/shard_map/ppermute | solution.py:455
  28.7 0.2 shard_map.70
  28.9 0.7 shard_map.71
  29.6 0.7 shard_map.74
  30.3 6.4 %shard_map.75 = (f32[16,48,384]{2,1,0:T(8,128)S(1)}, f32[16,48,384]{2,1,0:T(8,128)S(1)}, f32[16,48,384]{2,1,0:T(8,128)S(1)}, f32[16,48,384]{2,1,0:T(8,128)S(1)},...) custom-call(f32[16,16,384]{2,1,0:T(8,128)S(1)} %get-tuple-element.54.refs_0_.refs_5_, ...), custom_call_target="tpu_custom_call" | custom-call | tf_op jit(solution)/shard_map/pallas_call | solution.py:405
  36.8 1.2 collective-permute-done.2
  38.0 24.9 %all_to_all.26 = f32[128,1,128]{2,1,0:T(1,128)S(1)} all-to-all(f32[128,1,128]{2,1,0:T(1,128)S(1)} %broadcast_in_dim.32), channel_id=1, replica_groups=mesh['sec'=4,'pair'=32,'core'=2] {'sec','pair'}, dimensions={0} | all-to-all | bytes 131072 | tf_op jit(solution)/shard_map/all_to_all | solution.py:431
  62.9 5.3 %shard_map.76 = (f32[16,40,384]{2,1,0:T(8,128)S(1)}, f32[16,32,384]{2,1,0:T(8,128)S(1)}, f32[16,32,384]{2,1,0:T(8,128)S(1)}, f32[16,32,384]{2,1,0:T(8,128)S(1)},...) custom-call(f32[128,128]{1,0:T(8,128)S(1)} %bitcast.12, ...), custom_call_target="tpu_custom_call" | custom-call | tf_op jit(solution)/shard_map/pallas_call | solution.py:405
  68.2 1.8 %collective-permute-start.3 = (f32[8,128]{1,0:T(8,128)S(1)}, f32[8,128]{1,0:T(8,128)S(1)}, u32[]{:S(2)}, u32[]{:S(2)}) collective-permute-start(f32[8,128]{1,0:T(8,128)S(1)} %get-tuple-element.85), channel_id=1, source_target_pairs={{0,1},{1,0},{2,3},{3,2},{4,5},{5,4},{6,7},{7,6},{8,9},{9,8},{10,11... | collective-permute-start | bytes 12296 | tf_op jit(solution)/shard_map/ppermute | solution.py:430
  70.0 0.8 collective-permute-done.3
  70.8 16.1 %all_to_all.27 = f32[128,1,128]{2,1,0:T(1,128)S(1)} all-to-all(f32[128,1,128]{2,1,0:T(1,128)S(1)} %broadcast_in_dim.34), channel_id=1, replica_groups=mesh['sec'=4,'pair'=32,'core'=2] {'sec','pair'}, dimensions={0} | all-to-all | bytes 131072 | tf_op jit(solution)/shard_map/all_to_all | solution.py:431
  86.9 5.1 %shard_map.77 = (f32[16,32,384]{2,1,0:T(8,128)S(1)}, f32[16,32,384]{2,1,0:T(8,128)S(1)}, f32[16,32,384]{2,1,0:T(8,128)S(1)}, f32[16,32,384]{2,1,0:T(8,128)S(1)},...) custom-call(f32[128,128]{1,0:T(8,128)S(1)} %bitcast.11, ...), custom_call_target="tpu_custom_call" | custom-call | tf_op jit(solution)/shard_map/pallas_call | solution.py:405
  92.1 1.6 %collective-permute-start.4 = (f32[8,128]{1,0:T(8,128)S(1)}, f32[8,128]{1,0:T(8,128)S(1)}, u32[]{:S(2)}, u32[]{:S(2)}) collective-permute-start(f32[8,128]{1,0:T(8,128)S(1)} %get-tuple-element.91), channel_id=1, source_target_pairs={{0,1},{1,0},{2,3},{3,2},{4,5},{5,4},{6,7},{7,6},{8,9},{9,8},{10,11... | collective-permute-start | bytes 12296 | tf_op jit(solution)/shard_map/ppermute | solution.py:430
  93.7 0.8 collective-permute-done.4
  94.5 16.1 %all_to_all.28 = f32[128,1,128]{2,1,0:T(1,128)S(1)} all-to-all(f32[128,1,128]{2,1,0:T(1,128)S(1)} %broadcast_in_dim.36), channel_id=1, replica_groups=mesh['sec'=4,'pair'=32,'core'=2] {'sec','pair'}, dimensions={0} | all-to-all | bytes 131072 | tf_op jit(solution)/shard_map/all_to_all | solution.py:431
  110.6 0.3 shard_map.78
  110.9 9.3 %all_to_all.29.parts_ref = f32[4,7,16,256]{3,2,1,0:T(8,128)S(1)} all-to-all(f32[4,7,16,256]{3,2,1,0:T(8,128)S(1)} %shard_map.78), channel_id=1, replica_groups=mesh['sec'=4,'pair'=32,'core'=2] {'sec'}, dimensions={0} | all-to-all | bytes 917504 | tf_op jit(solution)/shard_map/all_to_all | solution.py:495
  120.2 0.8 shard_map.79
  (20 shorter events, 0.3 us)
Async XLA Ops:
  0.6 15.2 %copy-start = (f32[3,16,1024]{2,1,0:T(8,128)S(1)}, f32[3,16,1024]{2,1,0:T(8,128)}, u32[]{:S(2)}) copy-start(f32[3,16,1024]{2,1,0:T(8,128)} %rain_ref.1) | copy-start | bytes 589828
  2.0 19.8 %copy-start.1 = (f32[12]{0:T(128)S(1)}, f32[12]{0:T(128)}, u32[]{:S(2)}) copy-start(f32[12]{0:T(128)} %param.8) | copy-start | bytes 148
  2.0 19.8 %copy-start.2 = (f32[12]{0:T(128)S(1)}, f32[12]{0:T(128)}, u32[]{:S(2)}) copy-start(f32[12]{0:T(128)} %param.7) | copy-start | bytes 148
  16.1 12.6 %collective-permute-start.1 = (f32[528,256]{1,0:T(8,128)S(1)}, f32[528,256]{1,0:T(8,128)S(1)}, u32[]{:S(2)}, u32[]{:S(2)}) collective-permute-start(f32[528,256]{1,0:T(8,128)S(1)} %get-tuple-element.52), channel_id=1, source_target_pairs={{1,2},{3,4},{5,6},{7,8},{9,10},{11,12},{13,14},{15,16},{17,18},{19... | collective-permute-start | bytes 1622024 | tf_op jit(solution)/shard_map/ppermute | solution.py:455
  21.7 2.0 %collective-permute-start = (f32[520,256]{1,0:T(8,128)S(1)}, f32[520,256]{1,0:T(8,128)S(1)}, u32[]{:S(2)}, u32[]{:S(2)}) collective-permute-start(f32[520,256]{1,0:T(8,128)S(1)} %get-tuple-element.51), channel_id=1, source_target_pairs={{0,1},{1,0},{2,3},{3,2},{4,5},{5,4},{6,7},{7,6},{8,9},{9,8},{10,11... | collective-permute-start | bytes 1597448 | tf_op jit(solution)/shard_map/ppermute | solution.py:456
  36.7 1.2 collective-permute-start.2
  68.2 2.6 %collective-permute-start.3 = (f32[8,128]{1,0:T(8,128)S(1)}, f32[8,128]{1,0:T(8,128)S(1)}, u32[]{:S(2)}, u32[]{:S(2)}) collective-permute-start(f32[8,128]{1,0:T(8,128)S(1)} %get-tuple-element.85), channel_id=1, source_target_pairs={{0,1},{1,0},{2,3},{3,2},{4,5},{5,4},{6,7},{7,6},{8,9},{9,8},{10,11... | collective-permute-start | bytes 12296 | tf_op jit(solution)/shard_map/ppermute | solution.py:430
  92.1 2.4 %collective-permute-start.4 = (f32[8,128]{1,0:T(8,128)S(1)}, f32[8,128]{1,0:T(8,128)S(1)}, u32[]{:S(2)}, u32[]{:S(2)}) collective-permute-start(f32[8,128]{1,0:T(8,128)S(1)} %get-tuple-element.91), channel_id=1, source_target_pairs={{0,1},{1,0},{2,3},{3,2},{4,5},{5,4},{6,7},{7,6},{8,9},{9,8},{10,11... | collective-permute-start | bytes 12296 | tf_op jit(solution)/shard_map/ppermute | solution.py:430

commit v9 on v8

--- a/solution.py
+++ b/solution.py
@@ -375,18 +375,21 @@
     moments_ref[...] = line
 
 
-def last_kernel(sums_ref, head_ref, v0, v1, v2, v3, i0, i1, i2, out_ref):
+def last_kernel(sums_ref, head_ref, v0, v1, v2, v3, i0, i1, i2, *out_refs):
     change = weights(sums_ref)
     own = OWN_ROWS - WORK[2][0]
     kept = slice(own, own + OWN_ROWS)
-    for l in range(NZ):
-        h = head_ref[l, OWN_ROWS - SPANS[2][0] : 2 * OWN_ROWS - SPANS[2][0], 0:OWN_COLS]
-        for c, o in zip(change, (v0, v1, v2, v3)):
-            h = h + c * o[l, kept, 0:OWN_COLS]
-        out_ref[l // LZ, l % LZ] = h
-    for s in range(SECTIONS):
+    section = lax.axis_index("sec")
+    for on, out_ref in enumerate(out_refs):
+        target = lax.rem(section + on, SECTIONS)
+        for q in range(LZ):
+            l = target * LZ + q
+            h = head_ref[l, OWN_ROWS - SPANS[2][0] : 2 * OWN_ROWS - SPANS[2][0], 0:OWN_COLS]
+            for c, o in zip(change, (v0, v1, v2, v3)):
+                h = h + c * o[l, kept, 0:OWN_COLS]
+            out_ref[q] = h
         for c, i in enumerate((i0, i1, i2)):
-            out_ref[s, LZ + c] = i[s]
+            out_ref[LZ + c] = i[target]
 
 
 def shape(*dims):
@@ -413,12 +416,14 @@
     )(*operands)
 
 
-def join_kernel(parts_ref, head_hbm, flows_hbm, sems):
+def join_kernel(p0, p1, p2, p3, head_hbm, flows_hbm, sems):
+    section = lax.axis_index("sec")
     copies = []
-    for t in range(SECTIONS):
-        cols = slice(t * OWN_COLS, (t + 1) * OWN_COLS)
-        copies.append(pltpu.make_async_copy(parts_ref.at[t, 0:LZ], head_hbm.at[:, :, cols], sems.at[0, t]))
-        copies.append(pltpu.make_async_copy(parts_ref.at[t, LZ : LZ + 3], flows_hbm.at[0, :, :, cols], sems.at[1, t]))
+    for on, part in enumerate((p0, p1, p2, p3)):
+        source = lax.rem(section + SECTIONS - on, SECTIONS)
+        cols = pl.ds(pl.multiple_of(source * OWN_COLS, OWN_COLS), OWN_COLS)
+        copies.append(pltpu.make_async_copy(part.at[0:LZ], head_hbm.at[:, :, cols], sems.at[0, on]))
+        copies.append(pltpu.make_async_copy(part.at[LZ : LZ + 3], flows_hbm.at[0, :, :, cols], sems.at[1, on]))
     for copy in copies:
         copy.start()
     for copy in copies:
@@ -491,11 +496,13 @@
             head, v = got[0], got[1:5]
         inflows.append(got[-2])
         sums = add_up(got[-1])
-    out = call(last_kernel, (sums, *held(head, *v, *inflows)), near(SECTIONS, 7, OWN_ROWS, OWN_COLS))
-    out = lax.all_to_all(out, "sec", 0, 0, tiled=True)
+    out = call(last_kernel, (sums, *held(head, *v, *inflows)), [near(7, OWN_ROWS, OWN_COLS)] * SECTIONS)
+    out = list(out)
+    for on in (2, 1, 3):
+        out[on] = lax.ppermute(out[on], "sec", [(i, (i + on) % SECTIONS) for i in range(SECTIONS)])
     return call(
         join_kernel,
-        held(out),
+        held(*out),
         [shape(*block), shape(1, 3, *block[1:])],
         (pltpu.SemaphoreType.DMA((2, SECTIONS)),),
         out_specs=[outside] * 2,

time: 122 us -> 120 us (0.984)
  blocking collectives: 80.2 us -> 70.9 us
  waiting for transfers between devices: 8.92 us -> 12.8 us
  starting transfers between devices: 9.12 us -> 12.4 us
    all_to_all x1 -> x0, blocking collectives: 9.26 us -> none  [body(): out = lax.all_to_all(out, 'sec', 0, 0, tiled=True)]
    ppermute x0 -> x3, waiting for transfers between devices: none -> 3.87 us  [body(): lax.ppermute(out[on], 'sec', [(i, (i + on) % SECTIONS) for i in range(SEC...]
    ppermute x0 -> x3, starting transfers between devices: none -> 3.25 us  [body(): lax.ppermute(out[on], 'sec', [(i, (i + on) % SECTIONS) for i in range(SEC...]
  transfers between devices with their start and end apart: 5 -> 8, of which waited for: 5 -> 7; matrix products, arithmetic and copies ran while one was open for 0% -> 0% of each run, Pallas kernels for 1% -> 1%
where the time goes in v9:
time: 120 us; the launch traced here: 119 us
  blocking collectives  70.9 us (59%)
  Pallas kernels  21.9 us (18%)
  waiting for transfers between devices  12.8 us (11%)
  starting transfers between devices  12.4 us (10%)
    all_to_all x3, blocking collectives, add_up(): lax.all_to_all(jnp.broadcast_to(both[:1, None], (chips, 1, 128)), ('sec',...  57.1 us
    pallas_call x12, Pallas kernels, call(): pl.pallas_call(kernel, **more, out_shape=outs, in_specs=in_specs or [VMEM...  21.9 us
    all_to_all x1, blocking collectives, body(): mid = lax.all_to_all(packed, 'sec', 0, 0, tiled=True)  13.8 us
    ppermute x1, starting transfers between devices, body(): beyond = lax.ppermute(to_beyond, gx, pairs + [(j, i) for i, j in pairs])  5.59 us
    ppermute x1, waiting for transfers between devices, body(): beyond = lax.ppermute(to_beyond, gx, pairs + [(j, i) for i, j in pairs])  5.02 us
    ppermute x3, waiting for transfers between devices, body(): lax.ppermute(out[on], 'sec', [(i, (i + on) % SECTIONS) for i in range(SEC...  3.87 us
    ppermute x3, starting transfers between devices, add_up(): both = moments + lax.ppermute(moments, 'core', [(0, 1), (1, 0)])  3.44 us
    ppermute x3, starting transfers between devices, body(): lax.ppermute(out[on], 'sec', [(i, (i + on) % SECTIONS) for i in range(SEC...  3.25 us
  transfers between devices with their start and end apart: 8, of which 7 were waited for; matrix products, arithmetic and copies ran while one was open for 0% of the time, Pallas kernels for 1%

profile of v9, /device:TPU:1, one launch (start us, length us, event | category | flops | bytes accessed | tf_op | source)
XLA Modules:
  0.0 119.0 jit_solution(10975193697371129675)
XLA Ops:
  0.6 1.4 %shard_map.68 = f32[4,9,16,256]{3,2,1,0:T(8,128)S(1)} custom-call(f32[4,16,1024]{2,1,0:T(8,128)} %head_hbm.1, s32[4,16,1024]{2,1,0:T(8,128)} %soil_hbm.1), custom_call_target="tpu_custom_call" | custom-call | tf_op jit(solution)/shard_map/pallas_call | solution.py:408
  2.0 13.8 %all_to_all.20.mid_ref = f32[4,9,16,256]{3,2,1,0:T(8,128)S(1)} all-to-all(f32[4,9,16,256]{3,2,1,0:T(8,128)S(1)} %shard_map.68), channel_id=1, replica_groups=mesh['sec'=4,'pair'=32,'core'=2] {'sec'}, dimensions={0} | all-to-all | bytes 1179648 | tf_op jit(solution)/shard_map/all_to_all | solution.py:452
  16.1 5.6 %collective-permute-start.1 = (f32[528,256]{1,0:T(8,128)S(1)}, f32[528,256]{1,0:T(8,128)S(1)}, u32[]{:S(2)}, u32[]{:S(2)}) collective-permute-start(f32[528,256]{1,0:T(8,128)S(1)} %get-tuple-element.56), channel_id=1, source_target_pairs={{1,2},{3,4},{5,6},{7,8},{9,10},{11,12},{13,14},{15,16},{17,18},{19... | collective-permute-start | bytes 1622024 | tf_op jit(solution)/shard_map/ppermute | solution.py:460
  21.9 0.7 shard_map.73
  22.6 1.1 collective-permute-done.chip_ref
  23.7 5.0 %collective-permute-done.1.beyond_ref = f32[528,256]{1,0:T(8,128)S(1)} collective-permute-done((f32[528,256]{1,0:T(8,128)S(1)}, f32[528,256]{1,0:T(8,128)S(1)}, u32[]{:S(2)}, u32[]{:S(2)}) %collective-permute-start.1) | collective-permute-done | bytes 540704 | tf_op jit(solution)/shard_map/ppermute | solution.py:460
  28.9 0.7 shard_map.71
  29.6 0.7 shard_map.74
  30.3 6.4 %shard_map.75 = (f32[16,48,384]{2,1,0:T(8,128)S(1)}, f32[16,48,384]{2,1,0:T(8,128)S(1)}, f32[16,48,384]{2,1,0:T(8,128)S(1)}, f32[16,48,384]{2,1,0:T(8,128)S(1)},...) custom-call(f32[16,16,384]{2,1,0:T(8,128)S(1)} %get-tuple-element.58.refs_0_.refs_5_, ...), custom_call_target="tpu_custom_call" | custom-call | tf_op jit(solution)/shard_map/pallas_call | solution.py:408
  36.8 1.2 collective-permute-done.2
  38.0 24.9 %all_to_all.21 = f32[128,1,128]{2,1,0:T(1,128)S(1)} all-to-all(f32[128,1,128]{2,1,0:T(1,128)S(1)} %broadcast_in_dim.32), channel_id=1, replica_groups=mesh['sec'=4,'pair'=32,'core'=2] {'sec','pair'}, dimensions={0} | all-to-all | bytes 131072 | tf_op jit(solution)/shard_map/all_to_all | solution.py:436
  62.9 5.3 %shard_map.76 = (f32[16,40,384]{2,1,0:T(8,128)S(1)}, f32[16,32,384]{2,1,0:T(8,128)S(1)}, f32[16,32,384]{2,1,0:T(8,128)S(1)}, f32[16,32,384]{2,1,0:T(8,128)S(1)},...) custom-call(f32[128,128]{1,0:T(8,128)S(1)} %bitcast.12, ...), custom_call_target="tpu_custom_call" | custom-call | tf_op jit(solution)/shard_map/pallas_call | solution.py:408
  68.2 1.8 %collective-permute-start.3 = (f32[8,128]{1,0:T(8,128)S(1)}, f32[8,128]{1,0:T(8,128)S(1)}, u32[]{:S(2)}, u32[]{:S(2)}) collective-permute-start(f32[8,128]{1,0:T(8,128)S(1)} %get-tuple-element.89), channel_id=1, source_target_pairs={{0,1},{1,0},{2,3},{3,2},{4,5},{5,4},{6,7},{7,6},{8,9},{9,8},{10,11... | collective-permute-start | bytes 12296 | tf_op jit(solution)/shard_map/ppermute | solution.py:435
  70.0 0.8 collective-permute-done.3
  70.8 16.1 %all_to_all.22 = f32[128,1,128]{2,1,0:T(1,128)S(1)} all-to-all(f32[128,1,128]{2,1,0:T(1,128)S(1)} %broadcast_in_dim.34), channel_id=1, replica_groups=mesh['sec'=4,'pair'=32,'core'=2] {'sec','pair'}, dimensions={0} | all-to-all | bytes 131072 | tf_op jit(solution)/shard_map/all_to_all | solution.py:436
  86.9 5.1 %shard_map.77 = (f32[16,32,384]{2,1,0:T(8,128)S(1)}, f32[16,32,384]{2,1,0:T(8,128)S(1)}, f32[16,32,384]{2,1,0:T(8,128)S(1)}, f32[16,32,384]{2,1,0:T(8,128)S(1)},...) custom-call(f32[128,128]{1,0:T(8,128)S(1)} %bitcast.11, ...), custom_call_target="tpu_custom_call" | custom-call | tf_op jit(solution)/shard_map/pallas_call | solution.py:408
  92.1 1.6 %collective-permute-start.4 = (f32[8,128]{1,0:T(8,128)S(1)}, f32[8,128]{1,0:T(8,128)S(1)}, u32[]{:S(2)}, u32[]{:S(2)}) collective-permute-start(f32[8,128]{1,0:T(8,128)S(1)} %get-tuple-element.95), channel_id=1, source_target_pairs={{0,1},{1,0},{2,3},{3,2},{4,5},{5,4},{6,7},{7,6},{8,9},{9,8},{10,11... | collective-permute-start | bytes 12296 | tf_op jit(solution)/shard_map/ppermute | solution.py:435
  93.7 0.8 collective-permute-done.4
  94.5 16.1 %all_to_all.23 = f32[128,1,128]{2,1,0:T(1,128)S(1)} all-to-all(f32[128,1,128]{2,1,0:T(1,128)S(1)} %broadcast_in_dim.36), channel_id=1, replica_groups=mesh['sec'=4,'pair'=32,'core'=2] {'sec','pair'}, dimensions={0} | all-to-all | bytes 131072 | tf_op jit(solution)/shard_map/all_to_all | solution.py:436
  111.1 1.4 %collective-permute-start.6 = (f32[7,16,256]{2,1,0:T(8,128)S(1)}, f32[7,16,256]{2,1,0:T(8,128)S(1)}, u32[]{:S(2)}, u32[]{:S(2)}) collective-permute-start(f32[7,16,256]{2,1,0:T(8,128)S(1)} %get-tuple-element.106), channel_id=1, source_target_pairs={{0,128},{64,192},{128,0},{192,64},{1,129},{65,193},{129,1},{193,65... | collective-permute-start | bytes 344072 | tf_op jit(solution)/shard_map/ppermute | solution.py:502
  112.6 1.6 %collective-permute-start.7 = (f32[7,16,256]{2,1,0:T(8,128)S(1)}, f32[7,16,256]{2,1,0:T(8,128)S(1)}, u32[]{:S(2)}, u32[]{:S(2)}) collective-permute-start(f32[7,16,256]{2,1,0:T(8,128)S(1)} %get-tuple-element.107), channel_id=1, source_target_pairs={{0,192},{64,0},{128,64},{192,128},{1,193},{65,1},{129,65},{193,129... | collective-permute-start | bytes 344072 | tf_op jit(solution)/shard_map/ppermute | solution.py:502
  114.2 3.4 %collective-permute-done.5.p1 = f32[7,16,256]{2,1,0:T(8,128)S(1)} collective-permute-done((f32[7,16,256]{2,1,0:T(8,128)S(1)}, f32[7,16,256]{2,1,0:T(8,128)S(1)}, u32[]{:S(2)}, u32[]{:S(2)}) %collective-permute-start.5) | collective-permute-done | bytes 114720 | tf_op jit(solution)/shard_map/ppermute | solution.py:502
  117.6 0.5 collective-permute-done.7.p3
  118.0 0.8 shard_map.79
  (25 shorter events, 1.2 us)
Async XLA Ops:
  0.6 15.2 %copy-start = (f32[3,16,1024]{2,1,0:T(8,128)S(1)}, f32[3,16,1024]{2,1,0:T(8,128)}, u32[]{:S(2)}) copy-start(f32[3,16,1024]{2,1,0:T(8,128)} %rain_ref.1) | copy-start | bytes 589828
  2.0 19.8 %copy-start.1 = (f32[12]{0:T(128)S(1)}, f32[12]{0:T(128)}, u32[]{:S(2)}) copy-start(f32[12]{0:T(128)} %param.8) | copy-start | bytes 148
  2.0 19.8 %copy-start.2 = (f32[12]{0:T(128)S(1)}, f32[12]{0:T(128)}, u32[]{:S(2)}) copy-start(f32[12]{0:T(128)} %param.7) | copy-start | bytes 148
  16.1 12.6 %collective-permute-start.1 = (f32[528,256]{1,0:T(8,128)S(1)}, f32[528,256]{1,0:T(8,128)S(1)}, u32[]{:S(2)}, u32[]{:S(2)}) collective-permute-start(f32[528,256]{1,0:T(8,128)S(1)} %get-tuple-element.56), channel_id=1, source_target_pairs={{1,2},{3,4},{5,6},{7,8},{9,10},{11,12},{13,14},{15,16},{17,18},{19... | collective-permute-start | bytes 1622024 | tf_op jit(solution)/shard_map/ppermute | solution.py:460
  21.7 2.0 %collective-permute-start = (f32[520,256]{1,0:T(8,128)S(1)}, f32[520,256]{1,0:T(8,128)S(1)}, u32[]{:S(2)}, u32[]{:S(2)}) collective-permute-start(f32[520,256]{1,0:T(8,128)S(1)} %get-tuple-element.55), channel_id=1, source_target_pairs={{0,1},{1,0},{2,3},{3,2},{4,5},{5,4},{6,7},{7,6},{8,9},{9,8},{10,11... | collective-permute-start | bytes 1597448 | tf_op jit(solution)/shard_map/ppermute | solution.py:461
  36.7 1.2 %collective-permute-start.2 = (f32[8,128]{1,0:T(8,128)S(1)}, f32[8,128]{1,0:T(8,128)S(1)}, u32[]{:S(2)}, u32[]{:S(2)}) collective-permute-start(f32[8,128]{1,0:T(8,128)S(1)} %get-tuple-element.78), channel_id=1, source_target_pairs={{0,1},{1,0},{2,3},{3,2},{4,5},{5,4},{6,7},{7,6},{8,9},{9,8},{10,11... | collective-permute-start | bytes 12296 | tf_op jit(solution)/shard_map/ppermute | solution.py:435
  68.2 2.6 %collective-permute-start.3 = (f32[8,128]{1,0:T(8,128)S(1)}, f32[8,128]{1,0:T(8,128)S(1)}, u32[]{:S(2)}, u32[]{:S(2)}) collective-permute-start(f32[8,128]{1,0:T(8,128)S(1)} %get-tuple-element.89), channel_id=1, source_target_pairs={{0,1},{1,0},{2,3},{3,2},{4,5},{5,4},{6,7},{7,6},{8,9},{9,8},{10,11... | collective-permute-start | bytes 12296 | tf_op jit(solution)/shard_map/ppermute | solution.py:435
  92.1 2.4 %collective-permute-start.4 = (f32[8,128]{1,0:T(8,128)S(1)}, f32[8,128]{1,0:T(8,128)S(1)}, u32[]{:S(2)}, u32[]{:S(2)}) collective-permute-start(f32[8,128]{1,0:T(8,128)S(1)} %get-tuple-element.95), channel_id=1, source_target_pairs={{0,1},{1,0},{2,3},{3,2},{4,5},{5,4},{6,7},{7,6},{8,9},{9,8},{10,11... | collective-permute-start | bytes 12296 | tf_op jit(solution)/shard_map/ppermute | solution.py:435
  110.9 6.6 %collective-permute-start.5 = (f32[7,16,256]{2,1,0:T(8,128)S(1)}, f32[7,16,256]{2,1,0:T(8,128)S(1)}, u32[]{:S(2)}, u32[]{:S(2)}) collective-permute-start(f32[7,16,256]{2,1,0:T(8,128)S(1)} %get-tuple-element.105), channel_id=1, source_target_pairs={{0,64},{64,128},{128,192},{192,0},{1,65},{65,129},{129,193},{193,1... | collective-permute-start | bytes 344072 | tf_op jit(solution)/shard_map/ppermute | solution.py:502
  111.1 6.4 %collective-permute-start.6 = (f32[7,16,256]{2,1,0:T(8,128)S(1)}, f32[7,16,256]{2,1,0:T(8,128)S(1)}, u32[]{:S(2)}, u32[]{:S(2)}) collective-permute-start(f32[7,16,256]{2,1,0:T(8,128)S(1)} %get-tuple-element.106), channel_id=1, source_target_pairs={{0,128},{64,192},{128,0},{192,64},{1,129},{65,193},{129,1},{193,65... | collective-permute-start | bytes 344072 | tf_op jit(solution)/shard_map/ppermute | solution.py:502
  112.6 5.5 %collective-permute-start.7 = (f32[7,16,256]{2,1,0:T(8,128)S(1)}, f32[7,16,256]{2,1,0:T(8,128)S(1)}, u32[]{:S(2)}, u32[]{:S(2)}) collective-permute-start(f32[7,16,256]{2,1,0:T(8,128)S(1)} %get-tuple-element.107), channel_id=1, source_target_pairs={{0,192},{64,0},{128,64},{192,128},{1,193},{65,1},{129,65},{193,129... | collective-permute-start | bytes 344072 | tf_op jit(solution)/shard_map/ppermute | solution.py:502
